TPU v7x, 512 devices: a whole 4x4x16 slice. The times are simulated.
512 devices in a mesh: member: 16 (over y, x), band: 16 (over z), rep: 2 (over core).
Axes of the slice: x: 4, y: 4, z: 16, core: 2. Of those that a mesh axis runs over, the one named last changes fastest.
Arguments:
- features: bfloat16 [2, 16, 512, 128, 128], P('rep', 'member', None, 'band'), may hold values from -6 to 6
- kernel: bfloat16 [3, 3, 512, 90], replicated, may hold values from -0.09375 to 0.09375
- noise_seed: int32 [2, 16], P('rep', 'member'), may hold values from 0 to 31
- noise_table: float32 [32, 90], replicated, may hold values from -4 to 4
- truth: bfloat16 [2, 90, 128, 128], P('rep', None, 'band'), may hold values from -6 to 6
- area_weight: float32 [128], P('band'), may hold values from 0.1 to 1
Outputs:
- feature_grad: bfloat16 [2, 16, 512, 128, 128], P('rep', 'member', None, 'band')
- kernel_grad: float32 [3, 3, 512, 90], replicated
All inputs are finite; a program needn't handle non-finite values.
Results may differ from a plain program's by a relative error of at most 0.014.
Values may be sent and summed in bfloat16 or wider, within the bound.
No kernel may reach another device: no remote copies, remote signals or barrier semaphores. Data moves between devices by JAX's collectives and lax.ppermute only.
A program may use at most 64 MiB of HBM per device.

v0:
```python
import math

import jax
import jax.numpy as jnp
from jax import lax
from jax.sharding import PartitionSpec as P

smoothing = 0.1
alpha_level = 0.95


def extended(block, sides, width):
    for axis, dim in sides:
        count = lax.axis_size(axis)
        forward = [(i, i + 1) for i in range(count - 1)]
        backward = [(target, source) for source, target in forward]
        low = lax.ppermute(
            lax.slice_in_dim(block, block.shape[dim] - width, None, axis=dim), axis, forward
        )
        high = lax.ppermute(lax.slice_in_dim(block, 0, width, axis=dim), axis, backward)
        block = jnp.concatenate([low, block, high], axis=dim)
    return block


def slope(values):
    return values / jnp.sqrt(values * values + smoothing * smoothing)


def local(features, kernel, noise_seed, noise_table, truth, area_weight):
    feature_map = features[0, 0]
    hidden, rows, cols = feature_map.shape
    chans = kernel.shape[3]
    rimmed = extended(feature_map, (("band", 1),), 1)
    padded = jnp.pad(rimmed, ((0, 0), (0, 0), (1, 1)))
    classes = noise_table.shape[0]
    picker = (jnp.arange(classes, dtype=jnp.int32) == noise_seed[0, 0]).astype(jnp.float32)
    offset = jnp.dot(picker, noise_table, precision=lax.Precision.HIGHEST)
    predicted = jnp.zeros((chans, rows, cols), jnp.float32) + offset[:, None, None]
    for tap_row in range(3):
        for tap_col in range(3):
            predicted = predicted + jnp.einsum(
                "hc,hrl->crl",
                kernel[tap_row, tap_col],
                padded[:, tap_row : tap_row + rows, tap_col : tap_col + cols],
                preferred_element_type=jnp.float32,
            )
    members = lax.axis_size("member")
    eps_value = (1.0 - alpha_level) / members
    coef = (1.0 - eps_value) / (members - 1)
    own_term = slope(predicted - truth[0].astype(jnp.float32))
    everyone = lax.all_gather(predicted[None], "member", axis=0, tiled=True)
    pairs = jnp.sum(slope(predicted[None] - everyone), axis=0)
    delta = (area_weight[None, :, None] * (own_term - coef * pairs)).astype(jnp.bfloat16)
    delta_rimmed = extended(delta, (("band", 1),), 1)
    delta_pad = jnp.pad(delta_rimmed, ((0, 0), (0, 0), (1, 1)))
    grad_map = jnp.zeros((hidden, rows, cols), jnp.float32)
    tap_terms = []
    for tap_row in range(3):
        row_terms = []
        for tap_col in range(3):
            grad_map = grad_map + jnp.einsum(
                "hc,crl->hrl",
                kernel[tap_row, tap_col],
                delta_pad[:, 2 - tap_row : 2 - tap_row + rows, 2 - tap_col : 2 - tap_col + cols],
                preferred_element_type=jnp.float32,
            )
            row_terms.append(
                jnp.einsum(
                    "hrl,crl->hc",
                    padded[:, tap_row : tap_row + rows, tap_col : tap_col + cols],
                    delta,
                    preferred_element_type=jnp.float32,
                )
            )
        tap_terms.append(jnp.stack(row_terms))
    local_kernel = jnp.stack(tap_terms)
    count = lax.axis_size("rep") * members * lax.axis_size("band") * rows * cols
    scale = 1.0 / math.sqrt(count)
    total = lax.psum(local_kernel, ("member", "band", "rep"))
    kernel_grad = total * scale
    feature_grad = grad_map.astype(jnp.bfloat16)[None, None]
    return (feature_grad, kernel_grad)


def solution(mesh):
    return jax.shard_map(
        local,
        mesh=mesh,
        in_specs=(
            P("rep", "member", None, "band", None),
            P(),
            P("rep", "member"),
            P(),
            P("rep", None, "band", None),
            P("band"),
        ),
        out_specs=(P("rep", "member", None, "band", None), P()),
        check_vma=False,
    )
```

profile of v0, /device:TPU:1, one launch (start us, length us, event | category | flops | bytes accessed | tf_op | source)
XLA Modules:
  0.0 606.8 jit_solution(408701182893254380)
XLA Ops:
  7.2 1.4 copy.33
  8.7 4.4 collective-permute-start
  13.1 1.3 collective-permute-start.1
  14.4 1.2 fusion.74
  16.5 2.5 collective-permute-done.1
  19.0 1.8 fusion.5
  21.1 0.6 fusion.27
  21.7 0.6 convolution_bitcast_fusion.1
  22.9 0.6 fusion.7
  24.1 1.0 copy.18
  25.1 80.5 %all-gather.3.cloned.1.call-done = f32[1440,8,128]{2,1,0:T(8,128)} async-done(((f32[90,8,128]{2,1,0:T(8,128)}), f32[1440,8,128]{2,1,0:T(8,128)}) %all-gather.3.cloned.1.call-update) | async-done | bytes 5898256 | tf_op jit(solution)/shard_map/all_gather | solution.py:51
  105.6 3.9 multiply_reduce_fusion
  109.8 0.6 fusion.111
  110.8 0.6 convolution_bitcast_fusion.6
  112.3 0.6 convolution_bitcast_fusion.9
  113.3 0.6 convolution_bitcast_fusion.4
  113.9 1.4 fusion.72
  115.3 1.3 collective-permute-start.3
  116.6 4.2 collective-permute-start.2
  121.8 1.4 pad_maximum_fusion
  126.9 1.9 fusion.15
  128.8 1.5 copy.21
  130.3 466.7 %all-reduce.4.cloned.1.call-done = f32[3,3,512,90]{2,3,1,0:T(8,128)} async-done(((f32[3,3,512,90]{2,3,1,0:T(8,128)}), f32[3,3,512,90]{2,3,1,0:T(8,128)}) %all-reduce.4.cloned.1.call-update) | async-done | bytes 1658896 | tf_op jit(solution)/shard_map/psum | solution.py:79
  597.0 3.0 broadcast_multiply_fusion
  (49 shorter events, 8.5 us)
Async XLA Ops:
  7.2 9.2 %copy-start = (f32[32,90]{1,0:T(8,128)S(1)}, f32[32,90]{1,0:T(8,128)}, u32[]{:S(2)}) copy-start(f32[32,90]{1,0:T(8,128)} %param.9) | copy-start | bytes 34564
  7.2 7.2 %copy-start.3 = (bf16[1,1,512,8,128]{4,3,2,1,0:T(8,128)(2,1)S(1)}, bf16[1,1,512,8,128]{4,3,2,1,0:T(8,128)(2,1)}, u32[]{:S(2)}) copy-start(bf16[1,1,512,8,128]{4,3,2,1,0:T(8,128)(2,1)} %param.6) | copy-start | bytes 3145732
  7.2 98.4 %all-gather.3.cloned.1.call-start = ((), (), s32[]{:S(2)}) async-start(), calls=%async_computation.1 | async-start | bytes 6266880 | tf_op jit(solution)/shard_map/all_gather | solution.py:51
  8.7 14.8 %copy-start.1 = (bf16[1,1,512,8,128]{4,2,3,1,0:T(8,128)(2,1)}, bf16[1,1,512,8,128]{4,2,3,1,0:T(8,128)(2,1)S(1)}, u32[]{:S(2)}) copy-start(bf16[1,1,512,8,128]{4,2,3,1,0:T(8,128)(2,1)S(1)} %copy.33) | copy-start | bytes 3145732
  8.7 7.8 %collective-permute-start = (bf16[512,1,128]{2,0,1:T(8,128)(2,1)S(1)}, bf16[512,1,128]{2,0,1:T(8,128)(2,1)S(1)}, u32[]{:S(2)}, u32[]{:S(2)}) collective-permute-start(bf16[512,1,128]{2,0,1:T(8,128)(2,1)S(1)} %get-tuple-element.8), channel_id=1, source_target_pairs={{0,2},{2,4},{4,6},{6,8},{8,10},{10,12},{12,14},{14,16},{16,18},{18... | collective-permute-start | bytes 393224 | tf_op jit(solution)/shard_map/ppermute | solution.py:17
  13.1 5.9 collective-permute-start.1
  15.6 5.2 copy-start.5
  25.1 571.9 %all-reduce.4.cloned.1.call-start = ((), (), s32[]{:S(2)}) async-start(), calls=%async_computation | async-start | bytes 3538944 | tf_op jit(solution)/shard_map/psum | solution.py:79
  105.6 3.9 copy-start.7
  105.6 3.9 copy-start.8
  109.6 1.8 copy-start.4
  113.3 7.4 %copy-start.2 = (bf16[1,1,512,8,128]{4,2,3,1,0:T(8,128)(2,1)S(1)}, bf16[1,1,512,8,128]{4,2,3,1,0:T(8,128)(2,1)}, u32[]{:S(2)}) copy-start(bf16[1,1,512,8,128]{4,2,3,1,0:T(8,128)(2,1)} %copy-done.1) | copy-start | bytes 3145732
  115.3 7.9 %collective-permute-start.3 = (bf16[90,1,128]{2,0,1:T(8,128)(2,1)}, bf16[90,1,128]{2,0,1:T(8,128)(2,1)S(1)}, u32[]{:S(2)}, u32[]{:S(2)}) collective-permute-start(bf16[90,1,128]{2,0,1:T(8,128)(2,1)} %get-tuple-element.10), channel_id=1, source_target_pairs={{2,0},{4,2},{6,4},{8,6},{10,8},{12,10},{14,12},{16,14},{18,16},{20... | collective-permute-start | bytes 69128 | tf_op jit(solution)/shard_map/ppermute | solution.py:20
  116.6 6.6 %collective-permute-start.2 = (bf16[90,1,128]{2,0,1:T(8,128)(2,1)S(1)}, bf16[90,1,128]{2,0,1:T(8,128)(2,1)S(1)}, u32[]{:S(2)}, u32[]{:S(2)}) collective-permute-start(bf16[90,1,128]{2,0,1:T(8,128)(2,1)S(1)} %get-tuple-element.11), channel_id=1, source_target_pairs={{0,2},{2,4},{4,6},{6,8},{8,10},{10,12},{12,14},{14,16},{16,18},{18... | collective-permute-start | bytes 69128 | tf_op jit(solution)/shard_map/ppermute | solution.py:17
  121.8 1.7 copy-start.6
Sparse Core Ops, SparseCore 0:
  25.2 80.3 all-gather.2
  123.3 473.6 all-reduce.3
where the time goes:
time: 607 us
  waiting for transfers between devices  550 us (91%)
  matrix products  15.6 us (3%)
  between operations  15.1 us (2%)
  starting transfers between devices  11.2 us (2%)
  other arithmetic  10.6 us (2%)
    psum x1, waiting for transfers between devices, local(): total = lax.psum(local_kernel, ('member', 'band', 'rep'))  467 us
    all_gather x1, waiting for transfers between devices, local(): everyone = lax.all_gather(predicted[None], 'member', axis=0, tiled=True)  80.5 us
  transfers between devices with their start and end apart: 6, of which 3 were waited for; matrix products, arithmetic and copies ran while one was open for 2% of the time, Pallas kernels for 0%

commit v1 on v0

v1 whole, which is shorter than its diff:
```python
import functools
import math

import jax
import jax.numpy as jnp
from jax import lax
from jax.experimental import pallas as pl
from jax.experimental.pallas import tpu as pltpu
from jax.sharding import PartitionSpec as P

smoothing = 0.1
alpha_level = 0.95
padded_chans = 96
half_chans = padded_chans // 2
taps_chans = 3 * padded_chans
lanes = 128


def slope(values):
    return values * lax.rsqrt(values * values + smoothing * smoothing)


def shifted(block, step):
    lane = lax.broadcasted_iota(jnp.int32, block.shape, 1)
    width = block.shape[1]
    if step == 1:
        return jnp.where(lane == 0, 0.0, pltpu.roll(block, 1, 1))
    return jnp.where(lane == width - 1, 0.0, pltpu.roll(block, width - 1, 1))


def forward_kernel(x_ref, low_ref, high_ref, weight_ref, offset_ref, out_ref):
    rows = x_ref.shape[0]
    stack = [low_ref[...]] + [x_ref[row] for row in range(rows)] + [high_ref[...]]
    wide = jnp.concatenate(stack, axis=1)
    size = rows * lanes
    total = None
    for tap in range(3):
        part = jnp.dot(
            weight_ref[tap * taps_chans : (tap + 1) * taps_chans, :],
            wide[:, tap * lanes : tap * lanes + size],
            preferred_element_type=jnp.float32,
        )
        total = part if total is None else total + part
    offset = offset_ref[...]
    for row in range(rows):
        cell = total[:, row * lanes : (row + 1) * lanes]
        value = (
            cell[padded_chans : 2 * padded_chans]
            + shifted(cell[:padded_chans], 1)
            + shifted(cell[2 * padded_chans :], -1)
            + offset
        )
        out_ref[2 * row] = value[:half_chans]
        out_ref[2 * row + 1] = value[half_chans:]


def pair_kernel(coef, area_ref, values_ref, truth_ref, out_ref):
    members = values_ref.shape[0]
    weight = area_ref[0, 0]

    for step in range(half_chans // 16):
        deltas = [[] for _ in range(members)]
        for part in range(2):
            start = step * 16 + part * 8
            rows = slice(start, start + 8)
            values = [values_ref[member, rows, :] for member in range(members)]
            truth = truth_ref[rows, :]
            sums = [None] * members
            for one in range(members):
                for two in range(one + 1, members):
                    term = slope(values[one] - values[two])
                    sums[one] = term if sums[one] is None else sums[one] + term
                    sums[two] = -term if sums[two] is None else sums[two] - term
            for member in range(members):
                own = slope(values[member] - truth)
                deltas[member].append(weight * (own - coef * sums[member]))
        for member in range(members):
            both = jnp.concatenate(deltas[member], axis=0)
            out_ref[member, step * 16 : (step + 1) * 16, :] = both.astype(jnp.bfloat16)


def spread(block):
    exact = block.astype(jnp.float32)
    return [
        shifted(exact, -1).astype(jnp.bfloat16),
        block,
        shifted(exact, 1).astype(jnp.bfloat16),
    ]


def weight_grad_kernel(side_ref, x_ref, low_ref, high_ref, delta_ref, own_ref, other_ref, spread_ref, total_ref):
    rows = x_ref.shape[0]
    pieces = []
    for row in range(rows):
        block = jnp.concatenate([delta_ref[2 * row], delta_ref[2 * row + 1]], axis=0)
        pieces.append(jnp.concatenate(spread(block), axis=0))
    wide_delta = jnp.concatenate(pieces, axis=1)
    spread_ref[...] = wide_delta
    stack = [low_ref[...]] + [x_ref[row] for row in range(rows)] + [high_ref[...]]
    wide = jnp.concatenate(stack, axis=1)
    size = rows * lanes
    for tap in range(3):
        total_ref[tap * taps_chans : (tap + 1) * taps_chans, :] = lax.dot_general(
            wide_delta,
            wide[:, tap * lanes : tap * lanes + size],
            (((1,), (1,)), ((), ())),
            preferred_element_type=jnp.float32,
        )
    used = 3 * taps_chans
    total_ref[used:, :] = jnp.zeros((total_ref.shape[0] - used, total_ref.shape[1]), jnp.float32)
    side = side_ref[0, 0]
    half = total_ref.shape[1] // 2
    group = own_ref.shape[1]
    for target, start in ((own_ref, side * half), (other_ref, (1 - side) * half)):
        for part in range(2):
            column = pl.multiple_of(start + part * lanes, lanes)
            for block in range(own_ref.shape[0] // 2):
                target[2 * block + part] = total_ref[
                    block * group : (block + 1) * group, pl.ds(column, lanes)
                ].astype(jnp.bfloat16)


def feature_grad_kernel(weight_ref, spread_ref, low_ref, high_ref, out_ref):
    rows = out_ref.shape[0]
    size = rows * lanes
    ends = []
    for ref in (low_ref, high_ref):
        block = jnp.concatenate([ref[0], ref[1]], axis=0)
        ends.append(jnp.concatenate(spread(block), axis=0))
    wide = jnp.concatenate([ends[0], spread_ref[...], ends[1]], axis=1)
    deep = jnp.concatenate(
        [wide[:, (2 - tap) * lanes : (2 - tap) * lanes + size] for tap in range(3)], axis=0
    )
    result = lax.dot_general(
        weight_ref[...], deep, (((0,), (0,)), ((), ())), preferred_element_type=jnp.float32
    )
    for row in range(rows):
        out_ref[row] = result[:, row * lanes : (row + 1) * lanes].astype(jnp.bfloat16)


def finish_kernel(side_ref, own_ref, other_ref, out_ref):
    side = side_ref[0, 0]
    chans = out_ref.shape[1]
    half = out_ref.shape[2] // 2
    group = own_ref.shape[1]
    for source, start in ((own_ref, side * half), (other_ref, (1 - side) * half)):
        for part in range(2):
            column = pl.multiple_of(start + part * lanes, lanes)
            joined = jnp.concatenate(
                [source[2 * block + part] for block in range(source.shape[0] // 2)], axis=0
            ).astype(jnp.float32)
            for tap in range(out_ref.shape[0]):
                out_ref[tap, :, pl.ds(column, lanes)] = joined[
                    tap * padded_chans : tap * padded_chans + chans
                ]


vmem = pl.BlockSpec(memory_space=pltpu.VMEM)
smem = pl.BlockSpec(memory_space=pltpu.SMEM)


def call(kernel, out_shape, in_specs, scratch=(), limit=32):
    many = isinstance(out_shape, (list, tuple))
    return pl.pallas_call(
        kernel,
        out_shape=out_shape,
        in_specs=in_specs,
        out_specs=[vmem] * len(out_shape) if many else vmem,
        scratch_shapes=list(scratch),
        compiler_params=pltpu.CompilerParams(vmem_limit_bytes=limit * 1024 * 1024),
    )


def neighbours(low_edge, high_edge):
    count = lax.axis_size("band")
    forward = [(i, i + 1) for i in range(count - 1)]
    backward = [(target, source) for source, target in forward]
    return lax.ppermute(high_edge, "band", forward), lax.ppermute(low_edge, "band", backward)


def exchange(block, axis):
    return lax.all_to_all(block, axis, 0, 0, tiled=True)


def shared(block, axis):
    count = lax.axis_size(axis)
    return exchange(jnp.broadcast_to(block[None], (count,) + block.shape), axis)


def local(features, kernel, noise_seed, noise_table, truth, area_weight):
    feature_map = features[0, 0]
    hidden, rows, cols = feature_map.shape
    chans = kernel.shape[3]
    members = lax.axis_size("member")
    place = lax.axis_index("member")
    side = lax.axis_index("rep")
    bf16, f32 = jnp.bfloat16, jnp.float32

    x_low, x_high = neighbours(feature_map[:, 0, :], feature_map[:, rows - 1, :])
    x_rows = jnp.transpose(feature_map, (1, 0, 2))
    weights = jnp.pad(
        jnp.transpose(kernel, (0, 1, 3, 2)), ((0, 0), (0, 0), (0, padded_chans - chans), (0, 0))
    ).reshape(9 * padded_chans, hidden)
    offset = jnp.pad(
        lax.dynamic_slice(noise_table, (noise_seed[0, 0], 0), (1, chans))[0],
        (0, padded_chans - chans),
    )
    offset = jnp.broadcast_to(offset[:, None], (padded_chans, lanes))
    own_truth = jnp.pad(truth[0], ((0, padded_chans - chans), (0, 0), (0, 0)))
    own_truth = lax.dynamic_slice(
        own_truth, ((place % 2) * half_chans, place // 2, 0), (half_chans, 1, cols)
    )[:, 0, :].astype(f32)
    own_area = lax.dynamic_slice(area_weight, (place // 2,), (1,)).reshape(1, 1)
    side = jnp.full((1, 1), side, jnp.int32)

    predicted = call(
        forward_kernel,
        jax.ShapeDtypeStruct((members, half_chans, cols), f32),
        [vmem] * 5,
    )(x_rows, x_low, x_high, weights, offset)

    eps_value = (1.0 - alpha_level) / members
    coef = (1.0 - eps_value) / (members - 1)
    deltas = call(
        functools.partial(pair_kernel, coef),
        jax.ShapeDtypeStruct((members, half_chans, cols), bf16),
        [smem, vmem, vmem],
    )(own_area, exchange(predicted, "member"), own_truth)
    delta = exchange(deltas, "member")

    d_low, d_high = neighbours(delta[:2], delta[members - 2 :])
    group = 112
    piece = jax.ShapeDtypeStruct((16, group, lanes), bf16)
    own, other, wide_delta = call(
        weight_grad_kernel,
        [piece, piece, jax.ShapeDtypeStruct((taps_chans, rows * cols), bf16)],
        [smem] + [vmem] * 4,
        [pltpu.VMEM((8 * group, hidden), f32)],
    )(side, x_rows, x_low, x_high, delta)

    swap = [(0, 1), (1, 0)]
    other = lax.ppermute(other, "rep", swap)
    grad_rows = call(
        feature_grad_kernel,
        jax.ShapeDtypeStruct((rows, hidden, cols), bf16),
        [vmem] * 4,
    )(weights, wide_delta, d_low, d_high)
    feature_grad = jnp.transpose(grad_rows, (1, 0, 2))[None, None]

    part = (own.astype(f32) + other.astype(f32)).astype(bf16)
    part = jnp.sum(exchange(part, "member").astype(f32), axis=0).astype(bf16)
    scale = 1.0 / math.sqrt(lax.axis_size("rep") * members * lax.axis_size("band") * rows * cols)
    part = (jnp.sum(shared(part, "band").astype(f32), axis=0) * scale).astype(bf16)
    part = shared(part, "member")
    other = lax.ppermute(part, "rep", swap)
    kernel_grad = call(
        finish_kernel,
        jax.ShapeDtypeStruct((9, chans, hidden), f32),
        [smem, vmem, vmem],
    )(side, part, other)
    kernel_grad = jnp.transpose(kernel_grad.reshape(3, 3, chans, hidden), (0, 1, 3, 2))
    return (feature_grad, kernel_grad)


def solution(mesh):
    return jax.shard_map(
        local,
        mesh=mesh,
        in_specs=(
            P("rep", "member", None, "band", None),
            P(),
            P("rep", "member"),
            P(),
            P("rep", None, "band", None),
            P("band"),
        ),
        out_specs=(P("rep", "member", None, "band", None), P()),
        check_vma=False,
    )
```

time: 607 us -> 134 us (0.22)
  waiting for transfers between devices: 550 us -> 23.3 us
  blocking collectives: 0 us -> 59.6 us
  starting transfers between devices: 11.2 us -> 36.8 us
  matrix products: 15.6 us -> 0 us
  between operations: 15.1 us -> 1.56 us
  other arithmetic: 10.6 us -> 0.31 us
  Pallas kernels: 0 us -> 8.15 us
    psum x1 -> x0, waiting for transfers between devices: 467 us -> none  [local(): total = lax.psum(local_kernel, ('member', 'band', 'rep'))]
    all_gather x1 -> x0, waiting for transfers between devices: 80.5 us -> none  [local(): everyone = lax.all_gather(predicted[None], 'member', axis=0, tiled=True)]
    all_to_all x0 -> x3, blocking collectives: none -> 59.6 us  [exchange(): return lax.all_to_all(block, axis, 0, 0, tiled=True)]
    dot_general x28 -> x0, matrix products: 15.6 us -> none  [the longest x9 6.7 us: local(): jnp.einsum('hc,crl->hrl', kernel[tap_row, tap_col], delta_pad[:, 2 - tap_...]
    ppermute x4 -> x6, starting transfers between devices: 11.1 us -> 26.1 us  [the longest x1 9.35 us: local(): other = lax.ppermute(part, 'rep', swap)]
    all_to_all x0 -> x2, waiting for transfers between devices: none -> 14.8 us  [exchange(): return lax.all_to_all(block, axis, 0, 0, tiled=True)]
    all_to_all x0 -> x2, starting transfers between devices: none -> 10.7 us  [exchange(): return lax.all_to_all(block, axis, 0, 0, tiled=True)]
    pallas_call x0 -> x5, Pallas kernels: none -> 8.15 us  [the longest x1 2.12 us: local(): call(functools.partial(pair_kernel, coef), jax.ShapeDtypeStruct((members,...]
  transfers between devices with their start and end apart: 6 -> 8, of which waited for: 3 -> 5; matrix products, arithmetic and copies ran while one was open for 2% -> 2% of each run, Pallas kernels for 0% -> 1%
where the time goes in v1:
time: 134 us
  blocking collectives  59.6 us (44%)
  starting transfers between devices  36.8 us (27%)
  waiting for transfers between devices  23.3 us (17%)
  Pallas kernels  8.15 us (6%)
  local copies, waits for them, and re-layouts  4.05 us (3%)
  between operations  1.56 us (1%)
    all_to_all x3, blocking collectives, exchange(): return lax.all_to_all(block, axis, 0, 0, tiled=True)  59.6 us
    all_to_all x2, waiting for transfers between devices, exchange(): return lax.all_to_all(block, axis, 0, 0, tiled=True)  14.8 us
    all_to_all x2, starting transfers between devices, exchange(): return lax.all_to_all(block, axis, 0, 0, tiled=True)  10.7 us
    ppermute x1, starting transfers between devices, local(): other = lax.ppermute(part, 'rep', swap)  9.35 us
    ppermute x2, starting transfers between devices, neighbours(): lax.ppermute(high_edge, 'band', forward)  8.1 us
    ppermute x2, waiting for transfers between devices, neighbours(): lax.ppermute(low_edge, 'band', backward)  7.03 us
    ppermute x1, starting transfers between devices, local(): other = lax.ppermute(other, 'rep', swap)  6.05 us
    unnamed x11, local copies, waits for them, and re-layouts  3.14 us
  transfers between devices with their start and end apart: 8, of which 5 were waited for; matrix products, arithmetic and copies ran while one was open for 2% of the time, Pallas kernels for 1%

profile of v1, /device:TPU:1, one launch (start us, length us, event | category | flops | bytes accessed | tf_op | source)
XLA Modules:
  0.0 133.7 jit_solution(8677083171496694415)
XLA Ops:
  0.7 1.4 %copy.17 = bf16[1,1,512,8,128]{4,2,3,1,0:T(8,128)(2,1)S(1)} copy(bf16[1,1,512,8,128]{4,3,2,1,0:T(8,128)(2,1)} %param.6) | data formatting | bytes 2097152 | tf_op args[0]
  2.1 4.4 %collective-permute-start = (bf16[512,128]{1,0:T(8,128)(2,1)S(1)}, bf16[512,128]{1,0:T(8,128)(2,1)S(1)}, u32[]{:S(2)}, u32[]{:S(2)}) collective-permute-start(bf16[512,128]{1,0:T(8,128)(2,1)S(1)} %get-tuple-element.13), channel_id=1, source_target_pairs={{0,2},{2,4},{4,6},{6,8},{8,10},{10,12},{12,14},{14,16},{16,18},{18... | collective-permute-start | bytes 393224 | tf_op jit(solution)/shard_map/ppermute | solution.py:178
  6.5 1.3 collective-permute-start.1
  8.6 3.8 %collective-permute-done.1.high_ref = bf16[512,128]{1,0:T(8,128)(2,1)S(1)} collective-permute-done((bf16[512,128]{1,0:T(8,128)(2,1)S(1)}, bf16[512,128]{1,0:T(8,128)(2,1)S(1)}, u32[]{:S(2)}, u32[]{:S(2)}) %collective-permute-start.1) | collective-permute-done | bytes 131104 | tf_op jit(solution)/shard_map/ppermute | solution.py:178
  12.5 1.9 %shard_map.77 = f32[16,48,128]{2,1,0:T(8,128)} custom-call(bf16[8,512,128]{2,1,0:T(8,128)(2,1)S(1)} %bitcast.33, bf16[512,128]{1,0:T(8,128)(2,1)S(1)} %collective-permute-done.low_ref, bf16[512,128]{1,0:T(8,128)(2,1)S(1)} %collective-permute-done.1.high_ref, bf16[864,512]{1,0:T(8,128)(2,1)S(1)} %bitcast.35, f32[96,128]{1,0:T(8,128)S(1)} %broadcast_in_dim.11.offset_ref), custom_call_target="tpu_custom_call" | custom-call | tf_op jit(solution)/shard_map/pallas_call | solution.py:216
  14.4 7.2 %all-to-all-start = ((f32[16,48,128]{2,1,0:T(8,128)}), f32[16,48,128]{2,1,0:T(8,128)S(1)}, u32[]{:S(2)}, u32[]{:S(2)}) async-start(f32[16,48,128]{2,1,0:T(8,128)} %shard_map.77), calls=%async_computation | async-start | bytes 786432 | tf_op jit(solution)/shard_map/all_to_all | solution.py:182
  21.7 0.6 dynamic_slice.9
  22.3 7.7 %all-to-all-done.values_ref = f32[16,48,128]{2,1,0:T(8,128)S(1)} async-done(((f32[16,48,128]{2,1,0:T(8,128)}), f32[16,48,128]{2,1,0:T(8,128)S(1)}, u32[]{:S(2)}, u32[]{:S(2)}) %all-to-all-start) | async-done | bytes 393248 | tf_op jit(solution)/shard_map/all_to_all | solution.py:182
  30.0 2.1 %shard_map.78 = bf16[16,48,128]{2,1,0:T(8,128)(2,1)} custom-call(f32[1,1]{1,0:T(1,128)} %bitcast.7.area_ref, f32[16,48,128]{2,1,0:T(8,128)S(1)} %all-to-all-done.values_ref, f32[48,128]{1,0:T(8,128)S(1)} %bitcast_convert_fusion.truth_ref), custom_call_target="tpu_custom_call" | custom-call | tf_op jit(solution)/shard_map/pallas_call | solution.py:224
  32.1 3.5 %all-to-all-start.1 = ((bf16[16,48,128]{2,1,0:T(8,128)(2,1)}), bf16[16,48,128]{2,1,0:T(8,128)(2,1)S(1)}, u32[]{:S(2)}, u32[]{:S(2)}) async-start(bf16[16,48,128]{2,1,0:T(8,128)(2,1)} %shard_map.78), calls=%async_computation.1 | async-start | bytes 393216 | tf_op jit(solution)/shard_map/all_to_all | solution.py:182
  35.6 7.2 %all-to-all-done.1.delta_ref = bf16[16,48,128]{2,1,0:T(8,128)(2,1)S(1)} async-done(((bf16[16,48,128]{2,1,0:T(8,128)(2,1)}), bf16[16,48,128]{2,1,0:T(8,128)(2,1)S(1)}, u32[]{:S(2)}, u32[]{:S(2)}) %all-to-all-start.1) | async-done | bytes 196640 | tf_op jit(solution)/shard_map/all_to_all | solution.py:182
  42.8 1.4 %shard_map.79 = (bf16[16,112,128]{2,1,0:T(8,128)(2,1)S(1)}, bf16[16,112,128]{2,1,0:T(8,128)(2,1)S(1)}, bf16[288,1024]{1,0:T(8,128)(2,1)S(1)}) custom-call(s32[1,1]{1,0:T(1,128)} %bitcast.2.side_ref, bf16[8,512,128]{2,1,0:T(8,128)(2,1)S(1)} %bitcast.34, bf16[512,128]{1,0:T(8,128)(2,1)S(1)} %collective-permute-done.low_ref, ...), custom_call_target="tpu_custom_call" | custom-call | tf_op jit(solution)/shard_map/pallas_call | solution.py:234
  44.1 6.0 %collective-permute-start.4 = (bf16[16,112,128]{2,1,0:T(8,128)(2,1)S(1)}, bf16[16,112,128]{2,1,0:T(8,128)(2,1)S(1)}, u32[]{:S(2)}, u32[]{:S(2)}) collective-permute-start(bf16[16,112,128]{2,1,0:T(8,128)(2,1)S(1)} %get-tuple-element.7), channel_id=1, source_target_pairs={{0,1},{1,0},{2,3},{3,2},{4,5},{5,4},{6,7},{7,6},{8,9},{9,8},{10,11... | collective-permute-start | bytes 1376264 | tf_op jit(solution)/shard_map/ppermute | solution.py:242
  50.2 1.4 %collective-permute-done.4 = bf16[16,112,128]{2,1,0:T(8,128)(2,1)S(1)} collective-permute-done((bf16[16,112,128]{2,1,0:T(8,128)(2,1)S(1)}, bf16[16,112,128]{2,1,0:T(8,128)(2,1)S(1)}, u32[]{:S(2)}, u32[]{:S(2)}) %collective-permute-start.4) | collective-permute-done | bytes 458784 | tf_op jit(solution)/shard_map/ppermute | solution.py:242
  51.8 12.6 %all_to_all.25 = bf16[16,112,128]{2,1,0:T(8,128)(2,1)S(1)} all-to-all(bf16[16,112,128]{2,1,0:T(8,128)(2,1)S(1)} %add_convert_fusion), channel_id=1, replica_groups=mesh['member'=16,'band'=16,'rep'=2] {'member'}, dimensions={0} | all-to-all | bytes 917504 | tf_op jit(solution)/shard_map/all_to_all | solution.py:182
  64.5 33.9 %all_to_all.26 = bf16[16,112,128]{2,1,0:T(8,128)(2,1)S(1)} all-to-all(bf16[16,112,128]{2,1,0:T(8,128)(2,1)S(1)} %broadcast_in_dim.13), channel_id=1, replica_groups=mesh['member'=16,'band'=16,'rep'=2] {'band'}, dimensions={0} | all-to-all | bytes 917504 | tf_op jit(solution)/shard_map/all_to_all | solution.py:182
  98.6 13.1 %all_to_all.27.own_ref = bf16[16,112,128]{2,1,0:T(8,128)(2,1)S(1)} all-to-all(bf16[16,112,128]{2,1,0:T(8,128)(2,1)S(1)} %broadcast_in_dim.28), channel_id=1, replica_groups=mesh['member'=16,'band'=16,'rep'=2] {'member'}, dimensions={0} | all-to-all | bytes 917504 | tf_op jit(solution)/shard_map/all_to_all | solution.py:182
  111.7 9.3 %collective-permute-start.5 = (bf16[16,112,128]{2,1,0:T(8,128)(2,1)S(1)}, bf16[16,112,128]{2,1,0:T(8,128)(2,1)S(1)}, u32[]{:S(2)}, u32[]{:S(2)}) collective-permute-start(bf16[16,112,128]{2,1,0:T(8,128)(2,1)S(1)} %all_to_all.27.own_ref), channel_id=1, source_target_pairs={{0,1},{1,0},{2,3},{3,2},{4,5},{5,4},{6,7},{7,6},{8,9},{9,8},{10,11... | collective-permute-start | bytes 1376264 | tf_op jit(solution)/shard_map/ppermute | solution.py:255
  121.1 3.7 %collective-permute-start.2 = (bf16[2,48,128]{2,1,0:T(8,128)(2,1)S(1)}, bf16[2,48,128]{2,1,0:T(8,128)(2,1)S(1)}, u32[]{:S(2)}, u32[]{:S(2)}) collective-permute-start(bf16[2,48,128]{2,1,0:T(8,128)(2,1)S(1)} %get-tuple-element.17), channel_id=1, source_target_pairs={{0,2},{2,4},{4,6},{6,8},{8,10},{10,12},{12,14},{14,16},{16,18},{18... | collective-permute-start | bytes 73736 | tf_op jit(solution)/shard_map/ppermute | solution.py:178
  124.8 1.3 collective-permute-start.3
  126.1 3.3 %collective-permute-done.3.high_ref = bf16[2,48,128]{2,1,0:T(8,128)(2,1)S(1)} collective-permute-done((bf16[2,48,128]{2,1,0:T(8,128)(2,1)S(1)}, bf16[2,48,128]{2,1,0:T(8,128)(2,1)S(1)}, u32[]{:S(2)}, u32[]{:S(2)}) %collective-permute-start.3) | collective-permute-done | bytes 24608 | tf_op jit(solution)/shard_map/ppermute | solution.py:178
  129.4 1.3 shard_map.80
  130.6 1.6 %copy.13 = bf16[1,1,512,8,128]{4,3,2,1,0:T(8,128)(2,1)} copy(bf16[1,1,512,8,128]{4,2,3,1,0:T(8,128)(2,1)S(1)} %bitcast.37) | data formatting | bytes 2097152
  132.3 1.4 %shard_map.81 = f32[9,90,512]{2,1,0:T(8,128)} custom-call(s32[1,1]{1,0:T(1,128)} %bitcast.2.side_ref, bf16[16,112,128]{2,1,0:T(8,128)(2,1)S(1)} %all_to_all.27.own_ref, bf16[16,112,128]{2,1,0:T(8,128)(2,1)S(1)} %collective-permute-done.5.other_ref), custom_call_target="tpu_custom_call" | custom-call | tf_op jit(solution)/shard_map/pallas_call | solution.py:256
  (25 shorter events, 0.7 us)
Async XLA Ops:
  0.6 8.0 %copy-start = (f32[32,90]{1,0:T(8,128)S(1)}, f32[32,90]{1,0:T(8,128)}, u32[]{:S(2)}) copy-start(f32[32,90]{1,0:T(8,128)} %param.9) | copy-start | bytes 34564
  0.6 7.8 %copy-start.1 = (bf16[3,3,512,90]{2,3,1,0:T(8,128)(2,1)S(1)}, bf16[3,3,512,90]{2,3,1,0:T(8,128)(2,1)}, u32[]{:S(2)}) copy-start(bf16[3,3,512,90]{2,3,1,0:T(8,128)(2,1)} %param.7) | copy-start | bytes 2488324
  2.1 6.5 %collective-permute-start = (bf16[512,128]{1,0:T(8,128)(2,1)S(1)}, bf16[512,128]{1,0:T(8,128)(2,1)S(1)}, u32[]{:S(2)}, u32[]{:S(2)}) collective-permute-start(bf16[512,128]{1,0:T(8,128)(2,1)S(1)} %get-tuple-element.13), channel_id=1, source_target_pairs={{0,2},{2,4},{4,6},{6,8},{8,10},{10,12},{12,14},{14,16},{16,18},{18... | collective-permute-start | bytes 393224 | tf_op jit(solution)/shard_map/ppermute | solution.py:178
  6.5 5.9 %collective-permute-start.1 = (bf16[512,128]{1,0:T(8,128)(2,1)S(1)}, bf16[512,128]{1,0:T(8,128)(2,1)S(1)}, u32[]{:S(2)}, u32[]{:S(2)}) collective-permute-start(bf16[512,128]{1,0:T(8,128)(2,1)S(1)} %get-tuple-element.12), channel_id=1, source_target_pairs={{2,0},{4,2},{6,4},{8,6},{10,8},{12,10},{14,12},{16,14},{18,16},{20... | collective-permute-start | bytes 393224 | tf_op jit(solution)/shard_map/ppermute | solution.py:178
  8.6 13.1 %copy-start.2 = (bf16[1,90,8,128]{3,2,1,0:T(8,128)(2,1)S(1)}, bf16[1,90,8,128]{3,2,1,0:T(8,128)(2,1)}, u32[]{:S(2)}) copy-start(bf16[1,90,8,128]{3,2,1,0:T(8,128)(2,1)} %param.10) | copy-start | bytes 552964
  12.5 9.2 %copy-start.3 = (f32[8]{0:T(128)S(1)}, f32[8]{0:T(128)}, u32[]{:S(2)}) copy-start(f32[8]{0:T(128)} %param.11) | copy-start | bytes 100
  14.4 15.5 %all-to-all-start = ((f32[16,48,128]{2,1,0:T(8,128)}), f32[16,48,128]{2,1,0:T(8,128)S(1)}, u32[]{:S(2)}, u32[]{:S(2)}) async-start(f32[16,48,128]{2,1,0:T(8,128)} %shard_map.77), calls=%async_computation | async-start | bytes 786432 | tf_op jit(solution)/shard_map/all_to_all | solution.py:182
  32.1 10.7 %all-to-all-start.1 = ((bf16[16,48,128]{2,1,0:T(8,128)(2,1)}), bf16[16,48,128]{2,1,0:T(8,128)(2,1)S(1)}, u32[]{:S(2)}, u32[]{:S(2)}) async-start(bf16[16,48,128]{2,1,0:T(8,128)(2,1)} %shard_map.78), calls=%async_computation.1 | async-start | bytes 393216 | tf_op jit(solution)/shard_map/all_to_all | solution.py:182
  44.1 7.5 %collective-permute-start.4 = (bf16[16,112,128]{2,1,0:T(8,128)(2,1)S(1)}, bf16[16,112,128]{2,1,0:T(8,128)(2,1)S(1)}, u32[]{:S(2)}, u32[]{:S(2)}) collective-permute-start(bf16[16,112,128]{2,1,0:T(8,128)(2,1)S(1)} %get-tuple-element.7), channel_id=1, source_target_pairs={{0,1},{1,0},{2,3},{3,2},{4,5},{5,4},{6,7},{7,6},{8,9},{9,8},{10,11... | collective-permute-start | bytes 1376264 | tf_op jit(solution)/shard_map/ppermute | solution.py:242
  111.7 20.6 %collective-permute-start.5 = (bf16[16,112,128]{2,1,0:T(8,128)(2,1)S(1)}, bf16[16,112,128]{2,1,0:T(8,128)(2,1)S(1)}, u32[]{:S(2)}, u32[]{:S(2)}) collective-permute-start(bf16[16,112,128]{2,1,0:T(8,128)(2,1)S(1)} %all_to_all.27.own_ref), channel_id=1, source_target_pairs={{0,1},{1,0},{2,3},{3,2},{4,5},{5,4},{6,7},{7,6},{8,9},{9,8},{10,11... | collective-permute-start | bytes 1376264 | tf_op jit(solution)/shard_map/ppermute | solution.py:255
  121.1 5.0 %collective-permute-start.2 = (bf16[2,48,128]{2,1,0:T(8,128)(2,1)S(1)}, bf16[2,48,128]{2,1,0:T(8,128)(2,1)S(1)}, u32[]{:S(2)}, u32[]{:S(2)}) collective-permute-start(bf16[2,48,128]{2,1,0:T(8,128)(2,1)S(1)} %get-tuple-element.17), channel_id=1, source_target_pairs={{0,2},{2,4},{4,6},{6,8},{8,10},{10,12},{12,14},{14,16},{16,18},{18... | collective-permute-start | bytes 73736 | tf_op jit(solution)/shard_map/ppermute | solution.py:178
  124.8 4.6 %collective-permute-start.3 = (bf16[2,48,128]{2,1,0:T(8,128)(2,1)S(1)}, bf16[2,48,128]{2,1,0:T(8,128)(2,1)S(1)}, u32[]{:S(2)}, u32[]{:S(2)}) collective-permute-start(bf16[2,48,128]{2,1,0:T(8,128)(2,1)S(1)} %get-tuple-element.16), channel_id=1, source_target_pairs={{2,0},{4,2},{6,4},{8,6},{10,8},{12,10},{14,12},{16,14},{18,16},{20... | collective-permute-start | bytes 73736 | tf_op jit(solution)/shard_map/ppermute | solution.py:178

commit v2 on v1

--- a/solution.py
+++ b/solution.py
@@ -138,7 +138,23 @@
         out_ref[row] = result[:, row * lanes : (row + 1) * lanes].astype(jnp.bfloat16)
 
 
-def finish_kernel(side_ref, own_ref, other_ref, out_ref):
+def join_kernel(own_ref, other_ref, out_ref):
+    for block in range(own_ref.shape[0]):
+        both = own_ref[block].astype(jnp.float32) + other_ref[block].astype(jnp.float32)
+        out_ref[block] = both.astype(jnp.bfloat16)
+
+
+def sum_kernel(scale, parts_ref, *refs):
+    out_ref = refs[-1]
+    total = parts_ref[0].astype(jnp.float32)
+    for part in range(1, parts_ref.shape[0]):
+        total = total + parts_ref[part].astype(jnp.float32)
+    value = (total * scale).astype(jnp.bfloat16)
+    for copy in range(out_ref.shape[0]):
+        out_ref[copy] = value
+
+
+def finish_kernel(side_ref, own_ref, other_ref, after_ref, out_ref):
     side = side_ref[0, 0]
     chans = out_ref.shape[1]
     half = out_ref.shape[2] // 2
@@ -157,9 +173,10 @@
 
 vmem = pl.BlockSpec(memory_space=pltpu.VMEM)
 smem = pl.BlockSpec(memory_space=pltpu.SMEM)
-
-
-def call(kernel, out_shape, in_specs, scratch=(), limit=32):
+anywhere = pl.BlockSpec(memory_space=pl.ANY)
+
+
+def call(kernel, out_shape, in_specs, scratch=(), limit=32, cost=(0, 0)):
     many = isinstance(out_shape, (list, tuple))
     return pl.pallas_call(
         kernel,
@@ -167,6 +184,7 @@
         in_specs=in_specs,
         out_specs=[vmem] * len(out_shape) if many else vmem,
         scratch_shapes=list(scratch),
+        cost_estimate=pl.CostEstimate(flops=cost[0], bytes_accessed=cost[1], transcendentals=0),
         compiler_params=pltpu.CompilerParams(vmem_limit_bytes=limit * 1024 * 1024),
     )
 
@@ -178,13 +196,17 @@
     return lax.ppermute(high_edge, "band", forward), lax.ppermute(low_edge, "band", backward)
 
 
-def exchange(block, axis):
-    return lax.all_to_all(block, axis, 0, 0, tiled=True)
-
-
-def shared(block, axis):
-    count = lax.axis_size(axis)
-    return exchange(jnp.broadcast_to(block[None], (count,) + block.shape), axis)
+def exchange(block, axis, groups=None):
+    return lax.all_to_all(block, axis, 0, 0, axis_index_groups=groups, tiled=True)
+
+
+def summed(parts, copies, scale=1.0, after=()):
+    return call(
+        functools.partial(sum_kernel, scale),
+        jax.ShapeDtypeStruct((copies,) + parts.shape[1:], jnp.bfloat16),
+        [vmem] + [anywhere] * len(after),
+        cost=(parts.size, 2 * parts.size),
+    )(parts, *after)
 
 
 def local(features, kernel, noise_seed, noise_table, truth, area_weight):
@@ -217,6 +239,7 @@
         forward_kernel,
         jax.ShapeDtypeStruct((members, half_chans, cols), f32),
         [vmem] * 5,
+        cost=(2 * hidden * 9 * chans * rows * cols, 4 * hidden * rows * cols),
     )(x_rows, x_low, x_high, weights, offset)
 
     eps_value = (1.0 - alpha_level) / members
@@ -225,6 +248,7 @@
         functools.partial(pair_kernel, coef),
         jax.ShapeDtypeStruct((members, half_chans, cols), bf16),
         [smem, vmem, vmem],
+        cost=(members * members * 8 * half_chans * cols, 6 * members * half_chans * cols),
     )(own_area, exchange(predicted, "member"), own_truth)
     delta = exchange(deltas, "member")
 
@@ -236,6 +260,7 @@
         [piece, piece, jax.ShapeDtypeStruct((taps_chans, rows * cols), bf16)],
         [smem] + [vmem] * 4,
         [pltpu.VMEM((8 * group, hidden), f32)],
+        cost=(2 * hidden * 9 * chans * rows * cols, 4 * hidden * rows * cols),
     )(side, x_rows, x_low, x_high, delta)
 
     swap = [(0, 1), (1, 0)]
@@ -244,20 +269,32 @@
         feature_grad_kernel,
         jax.ShapeDtypeStruct((rows, hidden, cols), bf16),
         [vmem] * 4,
+        cost=(2 * hidden * 9 * chans * rows * cols, 4 * hidden * rows * cols),
     )(weights, wide_delta, d_low, d_high)
     feature_grad = jnp.transpose(grad_rows, (1, 0, 2))[None, None]
 
-    part = (own.astype(f32) + other.astype(f32)).astype(bf16)
-    part = jnp.sum(exchange(part, "member").astype(f32), axis=0).astype(bf16)
-    scale = 1.0 / math.sqrt(lax.axis_size("rep") * members * lax.axis_size("band") * rows * cols)
-    part = (jnp.sum(shared(part, "band").astype(f32), axis=0) * scale).astype(bf16)
-    part = shared(part, "member")
+    part = call(
+        join_kernel,
+        jax.ShapeDtypeStruct((members, group, lanes), bf16),
+        [vmem, vmem],
+        cost=(own.size, 6 * own.size),
+    )(own, other)
+    bands = lax.axis_size("band")
+    near = 4
+    far = bands // near
+    nearby = [[far_step * near + step for step in range(near)] for far_step in range(far)]
+    distant = [[far_step * near + step for far_step in range(far)] for step in range(near)]
+    part = summed(exchange(part, "member"), far)
+    part = summed(exchange(part, "band", distant), near, after=(d_low, d_high))
+    scale = 1.0 / math.sqrt(lax.axis_size("rep") * members * bands * rows * cols)
+    part = summed(exchange(part, "band", nearby), members, scale)
+    part = exchange(part, "member")
     other = lax.ppermute(part, "rep", swap)
     kernel_grad = call(
         finish_kernel,
         jax.ShapeDtypeStruct((9, chans, hidden), f32),
-        [smem, vmem, vmem],
-    )(side, part, other)
+        [smem, vmem, vmem, anywhere],
+    )(side, part, other, feature_grad)
     kernel_grad = jnp.transpose(kernel_grad.reshape(3, 3, chans, hidden), (0, 1, 3, 2))
     return (feature_grad, kernel_grad)
 

time: 134 us -> 123 us (0.918)
  blocking collectives: 59.6 us -> 33.2 us
  starting transfers between devices: 36.8 us -> 47.5 us
  waiting for transfers between devices: 23.3 us -> 28.4 us
    all_to_all x3, blocking collectives: 59.6 us -> 33.2 us  [exchange(): lax.all_to_all(block, axis, 0, 0, axis_index_groups=groups, tiled=True)]
    all_to_all x2 -> x3, starting transfers between devices: 10.7 us -> 24.4 us  [exchange(): lax.all_to_all(block, axis, 0, 0, axis_index_groups=groups, tiled=True)]
    all_to_all x2 -> x3, waiting for transfers between devices: 14.8 us -> 19.9 us  [exchange(): lax.all_to_all(block, axis, 0, 0, axis_index_groups=groups, tiled=True)]
    ppermute x1, starting transfers between devices: 9.35 us -> 7.41 us  [local(): other = lax.ppermute(part, 'rep', swap)]
    unnamed x11 -> x12, local copies, waits for them, and re-layouts: 3.14 us -> 1.5 us
  transfers between devices with their start and end apart: 8 -> 9, of which waited for: 5 -> 6; matrix products, arithmetic and copies ran while one was open for 2% -> 1% of each run, Pallas kernels for 1% -> 1%
where the time goes in v2:
time: 123 us
  starting transfers between devices  47.5 us (39%)
  blocking collectives  33.2 us (27%)
  waiting for transfers between devices  28.4 us (23%)
  Pallas kernels  9.12 us (7%)
  local copies, waits for them, and re-layouts  2.96 us (2%)
  between operations  1.56 us (1%)
    all_to_all x3, blocking collectives, exchange(): lax.all_to_all(block, axis, 0, 0, axis_index_groups=groups, tiled=True)  33.2 us
    all_to_all x3, starting transfers between devices, exchange(): lax.all_to_all(block, axis, 0, 0, axis_index_groups=groups, tiled=True)  24.4 us
    all_to_all x3, waiting for transfers between devices, exchange(): lax.all_to_all(block, axis, 0, 0, axis_index_groups=groups, tiled=True)  19.9 us
    ppermute x1, starting transfers between devices, local(): other = lax.ppermute(part, 'rep', swap)  7.41 us
    ppermute x2, waiting for transfers between devices, neighbours(): lax.ppermute(low_edge, 'band', backward)  7.08 us
    ppermute x2, starting transfers between devices, neighbours(): lax.ppermute(high_edge, 'band', forward)  7.02 us
    ppermute x1, starting transfers between devices, local(): other = lax.ppermute(other, 'rep', swap)  6.04 us
    ppermute x2, starting transfers between devices, neighbours(): lax.ppermute(low_edge, 'band', backward)  2.58 us
  transfers between devices with their start and end apart: 9, of which 6 were waited for; matrix products, arithmetic and copies ran while one was open for 1% of the time, Pallas kernels for 1%

profile of v2, /device:TPU:1, one launch (start us, length us, event | category | flops | bytes accessed | tf_op | source)
XLA Modules:
  0.0 122.8 jit_solution(3548618587555501766)
XLA Ops:
  0.7 1.4 %copy.16 = bf16[1,1,512,8,128]{4,2,3,1,0:T(8,128)(2,1)S(1)} copy(bf16[1,1,512,8,128]{4,3,2,1,0:T(8,128)(2,1)} %param.6) | data formatting | bytes 2097152 | tf_op args[0]
  2.1 4.4 %collective-permute-start = (bf16[512,128]{1,0:T(8,128)(2,1)S(1)}, bf16[512,128]{1,0:T(8,128)(2,1)S(1)}, u32[]{:S(2)}, u32[]{:S(2)}) collective-permute-start(bf16[512,128]{1,0:T(8,128)(2,1)S(1)} %get-tuple-element.9), channel_id=1, source_target_pairs={{0,2},{2,4},{4,6},{6,8},{8,10},{10,12},{12,14},{14,16},{16,18},{18... | collective-permute-start | bytes 393224 | tf_op jit(solution)/shard_map/ppermute | solution.py:196
  6.5 1.3 %collective-permute-start.1 = (bf16[512,128]{1,0:T(8,128)(2,1)S(1)}, bf16[512,128]{1,0:T(8,128)(2,1)S(1)}, u32[]{:S(2)}, u32[]{:S(2)}) collective-permute-start(bf16[512,128]{1,0:T(8,128)(2,1)S(1)} %get-tuple-element.8), channel_id=1, source_target_pairs={{2,0},{4,2},{6,4},{8,6},{10,8},{12,10},{14,12},{16,14},{18,16},{20... | collective-permute-start | bytes 393224 | tf_op jit(solution)/shard_map/ppermute | solution.py:196
  8.6 3.8 %collective-permute-done.1.high_ref = bf16[512,128]{1,0:T(8,128)(2,1)S(1)} collective-permute-done((bf16[512,128]{1,0:T(8,128)(2,1)S(1)}, bf16[512,128]{1,0:T(8,128)(2,1)S(1)}, u32[]{:S(2)}, u32[]{:S(2)}) %collective-permute-start.1) | collective-permute-done | bytes 131104 | tf_op jit(solution)/shard_map/ppermute | solution.py:196
  12.5 1.9 %shard_map.77 = f32[16,48,128]{2,1,0:T(8,128)} custom-call(bf16[8,512,128]{2,1,0:T(8,128)(2,1)S(1)} %bitcast.37, bf16[512,128]{1,0:T(8,128)(2,1)S(1)} %collective-permute-done.low_ref, bf16[512,128]{1,0:T(8,128)(2,1)S(1)} %collective-permute-done.1.high_ref, bf16[864,512]{1,0:T(8,128)(2,1)S(1)} %bitcast.39, f32[96,128]{1,0:T(8,128)S(1)} %broadcast_in_dim.13.offset_ref), custom_call_target="tpu_custom_call" | custom-call | flops 849346560 | bytes 2097152 | tf_op jit(solution)/shard_map/pallas_call | solution.py:238
  14.4 7.2 %all-to-all-start = ((f32[16,48,128]{2,1,0:T(8,128)}), f32[16,48,128]{2,1,0:T(8,128)S(1)}, u32[]{:S(2)}, u32[]{:S(2)}) async-start(f32[16,48,128]{2,1,0:T(8,128)} %shard_map.77), calls=%async_computation | async-start | bytes 786432 | tf_op jit(solution)/shard_map/all_to_all | solution.py:200
  22.3 7.7 %all-to-all-done.values_ref = f32[16,48,128]{2,1,0:T(8,128)S(1)} async-done(((f32[16,48,128]{2,1,0:T(8,128)}), f32[16,48,128]{2,1,0:T(8,128)S(1)}, u32[]{:S(2)}, u32[]{:S(2)}) %all-to-all-start) | async-done | bytes 393248 | tf_op jit(solution)/shard_map/all_to_all | solution.py:200
  30.0 2.1 %shard_map.78 = bf16[16,48,128]{2,1,0:T(8,128)(2,1)} custom-call(f32[1,1]{1,0:T(1,128)} %bitcast.7.area_ref, f32[16,48,128]{2,1,0:T(8,128)S(1)} %all-to-all-done.values_ref, f32[48,128]{1,0:T(8,128)S(1)} %bitcast_convert_fusion.truth_ref), custom_call_target="tpu_custom_call" | custom-call | flops 12582912 | bytes 589824 | tf_op jit(solution)/shard_map/pallas_call | solution.py:247
  32.1 3.5 %all-to-all-start.1 = ((bf16[16,48,128]{2,1,0:T(8,128)(2,1)}), bf16[16,48,128]{2,1,0:T(8,128)(2,1)S(1)}, u32[]{:S(2)}, u32[]{:S(2)}) async-start(bf16[16,48,128]{2,1,0:T(8,128)(2,1)} %shard_map.78), calls=%async_computation.1 | async-start | bytes 393216 | tf_op jit(solution)/shard_map/all_to_all | solution.py:200
  35.6 7.2 %all-to-all-done.1.delta_ref = bf16[16,48,128]{2,1,0:T(8,128)(2,1)S(1)} async-done(((bf16[16,48,128]{2,1,0:T(8,128)(2,1)}), bf16[16,48,128]{2,1,0:T(8,128)(2,1)S(1)}, u32[]{:S(2)}, u32[]{:S(2)}) %all-to-all-start.1) | async-done | bytes 196640 | tf_op jit(solution)/shard_map/all_to_all | solution.py:200
  42.8 1.4 %shard_map.79 = (bf16[16,112,128]{2,1,0:T(8,128)(2,1)S(1)}, bf16[16,112,128]{2,1,0:T(8,128)(2,1)S(1)}, bf16[288,1024]{1,0:T(8,128)(2,1)S(1)}) custom-call(s32[1,1]{1,0:T(1,128)} %bitcast.2.side_ref, bf16[8,512,128]{2,1,0:T(8,128)(2,1)S(1)} %bitcast.38, bf16[512,128]{1,0:T(8,128)(2,1)S(1)} %collective-permute-done.low_ref, ...), custom_call_target="tpu_custom_call" | custom-call | flops 849346560 | bytes 2097152 | tf_op jit(solution)/shard_map/pallas_call | solution.py:258
  44.2 6.0 %collective-permute-start.4 = (bf16[16,112,128]{2,1,0:T(8,128)(2,1)S(1)}, bf16[16,112,128]{2,1,0:T(8,128)(2,1)S(1)}, u32[]{:S(2)}, u32[]{:S(2)}) collective-permute-start(bf16[16,112,128]{2,1,0:T(8,128)(2,1)S(1)} %get-tuple-element.7), channel_id=1, source_target_pairs={{0,1},{1,0},{2,3},{3,2},{4,5},{5,4},{6,7},{7,6},{8,9},{9,8},{10,11... | collective-permute-start | bytes 1376264 | tf_op jit(solution)/shard_map/ppermute | solution.py:267
  50.2 1.4 %collective-permute-done.4.other_ref = bf16[16,112,128]{2,1,0:T(8,128)(2,1)S(1)} collective-permute-done((bf16[16,112,128]{2,1,0:T(8,128)(2,1)S(1)}, bf16[16,112,128]{2,1,0:T(8,128)(2,1)S(1)}, u32[]{:S(2)}, u32[]{:S(2)}) %collective-permute-start.4) | collective-permute-done | bytes 458784 | tf_op jit(solution)/shard_map/ppermute | solution.py:267
  51.7 12.6 %all_to_all.30.parts_ref = bf16[16,112,128]{2,1,0:T(8,128)(2,1)S(1)} all-to-all(bf16[16,112,128]{2,1,0:T(8,128)(2,1)S(1)} %shard_map.81), channel_id=1, replica_groups=mesh['member'=16,'band'=16,'rep'=2] {'member'}, dimensions={0} | all-to-all | bytes 917504 | tf_op jit(solution)/shard_map/all_to_all | solution.py:200
  65.1 13.7 %all-to-all-start.3 = ((bf16[4,112,128]{2,1,0:T(8,128)(2,1)}), bf16[4,112,128]{2,1,0:T(8,128)(2,1)S(1)}, u32[]{:S(2)}, u32[]{:S(2)}) async-start(bf16[4,112,128]{2,1,0:T(8,128)(2,1)} %shard_map.82), calls=%async_computation.3 | async-start | bytes 229376 | tf_op jit(solution)/shard_map/all_to_all | solution.py:200
  78.8 2.6 %collective-permute-start.2 = (bf16[2,48,128]{2,1,0:T(8,128)(2,1)S(1)}, bf16[2,48,128]{2,1,0:T(8,128)(2,1)S(1)}, u32[]{:S(2)}, u32[]{:S(2)}) collective-permute-start(bf16[2,48,128]{2,1,0:T(8,128)(2,1)S(1)} %get-tuple-element.13), channel_id=1, source_target_pairs={{0,2},{2,4},{4,6},{6,8},{8,10},{10,12},{12,14},{14,16},{16,18},{18... | collective-permute-start | bytes 73736 | tf_op jit(solution)/shard_map/ppermute | solution.py:196
  81.5 1.3 %collective-permute-start.3 = (bf16[2,48,128]{2,1,0:T(8,128)(2,1)S(1)}, bf16[2,48,128]{2,1,0:T(8,128)(2,1)S(1)}, u32[]{:S(2)}, u32[]{:S(2)}) collective-permute-start(bf16[2,48,128]{2,1,0:T(8,128)(2,1)S(1)} %get-tuple-element.12), channel_id=1, source_target_pairs={{2,0},{4,2},{6,4},{8,6},{10,8},{12,10},{14,12},{16,14},{18,16},{20... | collective-permute-start | bytes 73736 | tf_op jit(solution)/shard_map/ppermute | solution.py:196
  82.8 3.3 %collective-permute-done.3.high_ref.refs_1_ = bf16[2,48,128]{2,1,0:T(8,128)(2,1)S(1)} collective-permute-done((bf16[2,48,128]{2,1,0:T(8,128)(2,1)S(1)}, bf16[2,48,128]{2,1,0:T(8,128)(2,1)S(1)}, u32[]{:S(2)}, u32[]{:S(2)}) %collective-permute-start.3) | collective-permute-done | bytes 24608 | tf_op jit(solution)/shard_map/ppermute | solution.py:196
  86.1 5.1 %all-to-all-done.3.parts_ref = bf16[4,112,128]{2,1,0:T(8,128)(2,1)S(1)} async-done(((bf16[4,112,128]{2,1,0:T(8,128)(2,1)}), bf16[4,112,128]{2,1,0:T(8,128)(2,1)S(1)}, u32[]{:S(2)}, u32[]{:S(2)}) %all-to-all-start.3) | async-done | bytes 114720 | tf_op jit(solution)/shard_map/all_to_all | solution.py:200
  91.2 9.4 %all_to_all.31.parts_ref = bf16[4,112,128]{2,1,0:T(8,128)(2,1)S(1)} all-to-all(bf16[4,112,128]{2,1,0:T(8,128)(2,1)S(1)} %shard_map.83), channel_id=1, replica_groups={{0,2,4,6},{8,10,12,14},{16,18,20,22},{24,26,28,30},{1,3,5,7},{9,11,13,1..., dimensions={0} | all-to-all | bytes 229376 | tf_op jit(solution)/shard_map/all_to_all | solution.py:200
  100.6 11.2 %all_to_all.32.own_ref = bf16[16,112,128]{2,1,0:T(8,128)(2,1)S(1)} all-to-all(bf16[16,112,128]{2,1,0:T(8,128)(2,1)S(1)} %shard_map.84), channel_id=1, replica_groups=mesh['member'=16,'band'=16,'rep'=2] {'member'}, dimensions={0} | all-to-all | bytes 917504 | tf_op jit(solution)/shard_map/all_to_all | solution.py:200
  111.8 7.4 %collective-permute-start.5 = (bf16[16,112,128]{2,1,0:T(8,128)(2,1)S(1)}, bf16[16,112,128]{2,1,0:T(8,128)(2,1)S(1)}, u32[]{:S(2)}, u32[]{:S(2)}) collective-permute-start(bf16[16,112,128]{2,1,0:T(8,128)(2,1)S(1)} %all_to_all.32.own_ref), channel_id=1, source_target_pairs={{0,1},{1,0},{2,3},{3,2},{4,5},{5,4},{6,7},{7,6},{8,9},{9,8},{10,11... | collective-permute-start | bytes 1376264 | tf_op jit(solution)/shard_map/ppermute | solution.py:292
  119.3 1.3 %shard_map.80 = bf16[8,512,128]{2,1,0:T(8,128)(2,1)S(1)} custom-call(bf16[864,512]{1,0:T(8,128)(2,1)S(1)} %bitcast.40, bf16[288,1024]{1,0:T(8,128)(2,1)S(1)} %get-tuple-element.5.spread_ref, bf16[2,48,128]{2,1,0:T(8,128)(2,1)S(1)} %collective-permute-done.2.low_ref.refs_0_, bf16[2,48,128]{2,1,0:T(8,128)(2,1)S(1)} %collective-permute-done.3.high_ref.refs_1_), custom_call_target="tpu_custom_call" | custom-call | flops 849346560 | bytes 2097152 | tf_op jit(solution)/shard_map/pallas_call | solution.py:268
  121.3 1.5 %shard_map.85 = f32[9,90,512]{2,1,0:T(8,128)} custom-call(s32[1,1]{1,0:T(1,128)} %bitcast.2.side_ref, bf16[16,112,128]{2,1,0:T(8,128)(2,1)S(1)} %all_to_all.32.own_ref, bf16[16,112,128]{2,1,0:T(8,128)(2,1)S(1)} %collective-permute-done.5.other_ref, bf16[1,1,512,8,128]{4,3,2,1,0:T(8,128)(2,1)S(1)} %bitcast.34), custom_call_target="tpu_custom_call" | custom-call | tf_op jit(solution)/shard_map/pallas_call | solution.py:293
  (27 shorter events, 2.4 us)
Async XLA Ops:
  0.6 7.8 %copy-start = (f32[32,90]{1,0:T(8,128)S(1)}, f32[32,90]{1,0:T(8,128)}, u32[]{:S(2)}) copy-start(f32[32,90]{1,0:T(8,128)} %param.9) | copy-start | bytes 34564
  0.6 7.9 %copy-start.2 = (bf16[3,3,512,90]{2,3,1,0:T(8,128)(2,1)S(1)}, bf16[3,3,512,90]{2,3,1,0:T(8,128)(2,1)}, u32[]{:S(2)}) copy-start(bf16[3,3,512,90]{2,3,1,0:T(8,128)(2,1)} %param.7) | copy-start | bytes 2488324
  2.1 6.5 %collective-permute-start = (bf16[512,128]{1,0:T(8,128)(2,1)S(1)}, bf16[512,128]{1,0:T(8,128)(2,1)S(1)}, u32[]{:S(2)}, u32[]{:S(2)}) collective-permute-start(bf16[512,128]{1,0:T(8,128)(2,1)S(1)} %get-tuple-element.9), channel_id=1, source_target_pairs={{0,2},{2,4},{4,6},{6,8},{8,10},{10,12},{12,14},{14,16},{16,18},{18... | collective-permute-start | bytes 393224 | tf_op jit(solution)/shard_map/ppermute | solution.py:196
  6.5 5.9 %collective-permute-start.1 = (bf16[512,128]{1,0:T(8,128)(2,1)S(1)}, bf16[512,128]{1,0:T(8,128)(2,1)S(1)}, u32[]{:S(2)}, u32[]{:S(2)}) collective-permute-start(bf16[512,128]{1,0:T(8,128)(2,1)S(1)} %get-tuple-element.8), channel_id=1, source_target_pairs={{2,0},{4,2},{6,4},{8,6},{10,8},{12,10},{14,12},{16,14},{18,16},{20... | collective-permute-start | bytes 393224 | tf_op jit(solution)/shard_map/ppermute | solution.py:196
  12.5 9.2 %copy-start.3 = (bf16[1,90,8,128]{3,2,1,0:T(8,128)(2,1)S(1)}, bf16[1,90,8,128]{3,2,1,0:T(8,128)(2,1)}, u32[]{:S(2)}) copy-start(bf16[1,90,8,128]{3,2,1,0:T(8,128)(2,1)} %param.10) | copy-start | bytes 552964
  12.5 9.2 %copy-start.4 = (f32[8]{0:T(128)S(1)}, f32[8]{0:T(128)}, u32[]{:S(2)}) copy-start(f32[8]{0:T(128)} %param.11) | copy-start | bytes 100
  14.4 15.5 %all-to-all-start = ((f32[16,48,128]{2,1,0:T(8,128)}), f32[16,48,128]{2,1,0:T(8,128)S(1)}, u32[]{:S(2)}, u32[]{:S(2)}) async-start(f32[16,48,128]{2,1,0:T(8,128)} %shard_map.77), calls=%async_computation | async-start | bytes 786432 | tf_op jit(solution)/shard_map/all_to_all | solution.py:200
  32.1 10.7 %all-to-all-start.1 = ((bf16[16,48,128]{2,1,0:T(8,128)(2,1)}), bf16[16,48,128]{2,1,0:T(8,128)(2,1)S(1)}, u32[]{:S(2)}, u32[]{:S(2)}) async-start(bf16[16,48,128]{2,1,0:T(8,128)(2,1)} %shard_map.78), calls=%async_computation.1 | async-start | bytes 393216 | tf_op jit(solution)/shard_map/all_to_all | solution.py:200
  44.2 7.5 %collective-permute-start.4 = (bf16[16,112,128]{2,1,0:T(8,128)(2,1)S(1)}, bf16[16,112,128]{2,1,0:T(8,128)(2,1)S(1)}, u32[]{:S(2)}, u32[]{:S(2)}) collective-permute-start(bf16[16,112,128]{2,1,0:T(8,128)(2,1)S(1)} %get-tuple-element.7), channel_id=1, source_target_pairs={{0,1},{1,0},{2,3},{3,2},{4,5},{5,4},{6,7},{7,6},{8,9},{9,8},{10,11... | collective-permute-start | bytes 1376264 | tf_op jit(solution)/shard_map/ppermute | solution.py:267
  65.1 26.1 %all-to-all-start.3 = ((bf16[4,112,128]{2,1,0:T(8,128)(2,1)}), bf16[4,112,128]{2,1,0:T(8,128)(2,1)S(1)}, u32[]{:S(2)}, u32[]{:S(2)}) async-start(bf16[4,112,128]{2,1,0:T(8,128)(2,1)} %shard_map.82), calls=%async_computation.3 | async-start | bytes 229376 | tf_op jit(solution)/shard_map/all_to_all | solution.py:200
  78.8 4.0 %collective-permute-start.2 = (bf16[2,48,128]{2,1,0:T(8,128)(2,1)S(1)}, bf16[2,48,128]{2,1,0:T(8,128)(2,1)S(1)}, u32[]{:S(2)}, u32[]{:S(2)}) collective-permute-start(bf16[2,48,128]{2,1,0:T(8,128)(2,1)S(1)} %get-tuple-element.13), channel_id=1, source_target_pairs={{0,2},{2,4},{4,6},{6,8},{8,10},{10,12},{12,14},{14,16},{16,18},{18... | collective-permute-start | bytes 73736 | tf_op jit(solution)/shard_map/ppermute | solution.py:196
  81.5 4.6 %collective-permute-start.3 = (bf16[2,48,128]{2,1,0:T(8,128)(2,1)S(1)}, bf16[2,48,128]{2,1,0:T(8,128)(2,1)S(1)}, u32[]{:S(2)}, u32[]{:S(2)}) collective-permute-start(bf16[2,48,128]{2,1,0:T(8,128)(2,1)S(1)} %get-tuple-element.12), channel_id=1, source_target_pairs={{2,0},{4,2},{6,4},{8,6},{10,8},{12,10},{14,12},{16,14},{18,16},{20... | collective-permute-start | bytes 73736 | tf_op jit(solution)/shard_map/ppermute | solution.py:196
  111.8 9.4 %collective-permute-start.5 = (bf16[16,112,128]{2,1,0:T(8,128)(2,1)S(1)}, bf16[16,112,128]{2,1,0:T(8,128)(2,1)S(1)}, u32[]{:S(2)}, u32[]{:S(2)}) collective-permute-start(bf16[16,112,128]{2,1,0:T(8,128)(2,1)S(1)} %all_to_all.32.own_ref), channel_id=1, source_target_pairs={{0,1},{1,0},{2,3},{3,2},{4,5},{5,4},{6,7},{7,6},{8,9},{9,8},{10,11... | collective-permute-start | bytes 1376264 | tf_op jit(solution)/shard_map/ppermute | solution.py:292
  121.2 1.6 %copy-start.1 = (bf16[8,512,128]{2,0,1:T(8,128)(2,1)}, bf16[8,512,128]{2,0,1:T(8,128)(2,1)S(1)}, u32[]{:S(2)}) copy-start(bf16[8,512,128]{2,0,1:T(8,128)(2,1)S(1)} %copy.15) | copy-start | bytes 3145732

commit v3 on v2

v3 whole, which is shorter than its diff:
```python
import functools
import math

import jax
import jax.numpy as jnp
from jax import lax
from jax.experimental import pallas as pl
from jax.experimental.pallas import tpu as pltpu
from jax.sharding import PartitionSpec as P

smoothing = 0.1
alpha_level = 0.95
padded_chans = 96
half_chans = padded_chans // 2
taps_chans = 3 * padded_chans
lanes = 128
padded_rows = 896


def slope(values):
    return values * lax.rsqrt(values * values + smoothing * smoothing)


def shifted(block, step):
    lane = lax.broadcasted_iota(jnp.int32, block.shape, 1)
    width = block.shape[1]
    if step == 1:
        return jnp.where(lane == 0, 0.0, pltpu.roll(block, 1, 1))
    return jnp.where(lane == width - 1, 0.0, pltpu.roll(block, width - 1, 1))


def folded(sums):
    return (
        sums[padded_chans : 2 * padded_chans]
        + shifted(sums[:padded_chans], 1)
        + shifted(sums[2 * padded_chans :], -1)
    )


def inner_kernel(x_ref, weight_ref, offset_ref, truth_ref, out_ref):
    rows = x_ref.shape[0]
    wide = jnp.concatenate([x_ref[row] for row in range(rows)], axis=1)
    sums = [
        jnp.dot(
            weight_ref[tap * taps_chans : (tap + 1) * taps_chans, :],
            wide[:, max(tap - 1, 0) * lanes : (rows + min(tap - 1, 0)) * lanes],
            preferred_element_type=jnp.float32,
        )
        for tap in range(3)
    ]
    offset = offset_ref[...]
    for row in range(rows):
        cell = sums[1][:, row * lanes : (row + 1) * lanes]
        if row > 0:
            cell = cell + sums[0][:, (row - 1) * lanes : row * lanes]
        if row < rows - 1:
            cell = cell + sums[2][:, row * lanes : (row + 1) * lanes]
        value = folded(cell) + offset
        out_ref[2 * row] = value[:half_chans]
        out_ref[2 * row + 1] = value[half_chans:]


def edge_kernel(inner_ref, low_ref, high_ref, weight_ref, out_ref):
    chunks = inner_ref.shape[0]
    for chunk in range(2, chunks - 2):
        out_ref[chunk] = inner_ref[chunk]
    for tap, ref, first in ((0, low_ref, 0), (2, high_ref, chunks - 2)):
        value = folded(
            jnp.dot(
                weight_ref[tap * taps_chans : (tap + 1) * taps_chans, :],
                ref[...],
                preferred_element_type=jnp.float32,
            )
        )
        out_ref[first] = inner_ref[first] + value[:half_chans]
        out_ref[first + 1] = inner_ref[first + 1] + value[half_chans:]


def pair_kernel(coef, values_ref, truth_ref, area_ref, out_ref, delta_ref):
    members = values_ref.shape[0]
    lane = lax.broadcasted_iota(jnp.int32, area_ref.shape, 1)
    row = lax.axis_index("member") // 2
    weight = jnp.sum(jnp.where(lane == row, area_ref[...], 0.0), axis=1, keepdims=True)
    weight = jnp.broadcast_to(weight, (8, lanes))
    for start in range(0, half_chans, 8):
        rows = slice(start, start + 8)
        values = [values_ref[member, rows, :] for member in range(members)]
        truth = truth_ref[rows, :]
        sums = [None] * members
        for one in range(members):
            for two in range(one + 1, members):
                term = slope(values[one] - values[two])
                sums[one] = term if sums[one] is None else sums[one] + term
                sums[two] = -term if sums[two] is None else sums[two] - term
        for member in range(members):
            own = slope(values[member] - truth)
            delta_ref[member, rows, :] = weight * (own - coef * sums[member])
    for member in range(members):
        out_ref[member] = delta_ref[member].astype(jnp.bfloat16)


def spread(block):
    exact = block.astype(jnp.float32)
    return [
        shifted(exact, -1).astype(jnp.bfloat16),
        block,
        shifted(exact, 1).astype(jnp.bfloat16),
    ]


def taps_product(wide_delta, side, x_ref, low_ref, high_ref):
    rows, hidden = x_ref.shape[:2]
    half = hidden // 2
    mine = pl.ds(pl.multiple_of(side * half, half), half)
    stack = [low_ref[mine, :]] + [x_ref[row, mine, :] for row in range(rows)] + [high_ref[mine, :]]
    wide = jnp.concatenate(stack, axis=1)
    size = rows * lanes
    parts = [
        lax.dot_general(
            wide_delta,
            wide[:, tap * lanes : tap * lanes + size],
            (((1,), (1,)), ((), ())),
            preferred_element_type=jnp.float32,
        )
        for tap in range(3)
    ]
    parts.append(jnp.zeros((padded_rows - 3 * taps_chans, half), jnp.float32))
    return jnp.concatenate(parts, axis=0)


def sent_kernel(delta_ref, x_ref, low_ref, high_ref, out_ref, spread_ref):
    pieces = []
    for row in range(x_ref.shape[0]):
        block = jnp.concatenate([delta_ref[2 * row], delta_ref[2 * row + 1]], axis=0)
        pieces.append(jnp.concatenate(spread(block), axis=0))
    wide_delta = jnp.concatenate(pieces, axis=1)
    spread_ref[...] = wide_delta
    side = 1 - lax.axis_index("rep")
    total = taps_product(wide_delta, side, x_ref, low_ref, high_ref)
    group = out_ref.shape[1]
    for block in range(out_ref.shape[0]):
        out_ref[block] = total[
            block // 2 * group : (block // 2 + 1) * group,
            block % 2 * lanes : (block % 2 + 1) * lanes,
        ].astype(jnp.bfloat16)


def kept_kernel(spread_ref, x_ref, low_ref, high_ref, other_ref, out_ref):
    side = lax.axis_index("rep")
    total = taps_product(spread_ref[...], side, x_ref, low_ref, high_ref)
    group = out_ref.shape[1]
    for block in range(out_ref.shape[0]):
        own = total[
            block // 2 * group : (block // 2 + 1) * group,
            block % 2 * lanes : (block % 2 + 1) * lanes,
        ]
        out_ref[block] = (own + other_ref[block].astype(jnp.float32)).astype(jnp.bfloat16)


def feature_grad_kernel(weight_ref, spread_ref, low_ref, high_ref, out_ref):
    rows = out_ref.shape[0]
    size = rows * lanes
    ends = []
    for ref in (low_ref, high_ref):
        block = jnp.concatenate([ref[0], ref[1]], axis=0)
        ends.append(jnp.concatenate(spread(block), axis=0))
    wide = jnp.concatenate([ends[0], spread_ref[...], ends[1]], axis=1)
    deep = jnp.concatenate(
        [wide[:, (2 - tap) * lanes : (2 - tap) * lanes + size] for tap in range(3)], axis=0
    )
    result = lax.dot_general(
        weight_ref[...], deep, (((0,), (0,)), ((), ())), preferred_element_type=jnp.float32
    )
    for row in range(rows):
        out_ref[row] = result[:, row * lanes : (row + 1) * lanes].astype(jnp.bfloat16)


def sum_kernel(scale, parts_ref, *refs):
    out_ref = refs[-1]
    total = parts_ref[0].astype(jnp.float32)
    for part in range(1, parts_ref.shape[0]):
        total = total + parts_ref[part].astype(jnp.float32)
    value = (total * scale).astype(jnp.bfloat16)
    for copy in range(out_ref.shape[0]):
        out_ref[copy] = value


def finish_kernel(away, source_ref, *refs):
    out_ref, block_ref, sem = refs[-3:]
    chans, half = block_ref.shape[1:]
    for part in range(2):
        joined = jnp.concatenate(
            [source_ref[2 * block + part] for block in range(source_ref.shape[0] // 2)], axis=0
        ).astype(jnp.float32)
        for tap in range(block_ref.shape[0]):
            block_ref[tap, :, part * lanes : (part + 1) * lanes] = joined[
                tap * padded_chans : tap * padded_chans + chans
            ]
    side = lax.axis_index("rep")
    side = 1 - side if away else side
    mine = pl.ds(pl.multiple_of(side * half, half), half)
    copy = pltpu.make_async_copy(block_ref, out_ref.at[:, :, mine], sem)
    copy.start()
    copy.wait()


vmem = pl.BlockSpec(memory_space=pltpu.VMEM)
anywhere = pl.BlockSpec(memory_space=pl.ANY)


def call(kernel, out_shape, in_specs, scratch=(), limit=32, cost=(0, 0)):
    many = isinstance(out_shape, (list, tuple))
    return pl.pallas_call(
        kernel,
        out_shape=out_shape,
        in_specs=in_specs,
        out_specs=[vmem] * len(out_shape) if many else vmem,
        scratch_shapes=list(scratch),
        cost_estimate=pl.CostEstimate(flops=cost[0], bytes_accessed=cost[1], transcendentals=0),
        compiler_params=pltpu.CompilerParams(vmem_limit_bytes=limit * 1024 * 1024),
    )


def neighbours(low_edge, high_edge):
    count = lax.axis_size("band")
    forward = [(i, i + 1) for i in range(count - 1)]
    backward = [(target, source) for source, target in forward]
    return lax.ppermute(high_edge, "band", forward), lax.ppermute(low_edge, "band", backward)


def exchange(block, axis, groups=None):
    return lax.all_to_all(block, axis, 0, 0, axis_index_groups=groups, tiled=True)


def summed(parts, copies, scale=1.0, after=()):
    return call(
        functools.partial(sum_kernel, scale),
        jax.ShapeDtypeStruct((copies,) + parts.shape[1:], jnp.bfloat16),
        [vmem] + [anywhere] * len(after),
        cost=(parts.size, 2 * parts.size),
    )(parts, *after)


def placed(away, source, shape, *before):
    return pl.pallas_call(
        functools.partial(finish_kernel, away),
        out_shape=jax.ShapeDtypeStruct(shape, jnp.float32),
        in_specs=[vmem] + [anywhere] * len(before),
        out_specs=anywhere,
        scratch_shapes=[
            pltpu.VMEM(shape[:2] + (shape[2] // 2,), jnp.float32),
            pltpu.SemaphoreType.DMA,
        ],
        input_output_aliases={1: 0} if before else {},
        cost_estimate=pl.CostEstimate(
            flops=source.size, bytes_accessed=6 * source.size, transcendentals=0
        ),
        compiler_params=pltpu.CompilerParams(vmem_limit_bytes=32 * 1024 * 1024),
    )(source, *before)


def local(features, kernel, noise_seed, noise_table, truth, area_weight):
    feature_map = features[0, 0]
    hidden, rows, cols = feature_map.shape
    chans = kernel.shape[3]
    members = lax.axis_size("member")
    place = lax.axis_index("member")
    bf16, f32 = jnp.bfloat16, jnp.float32

    x_low, x_high = neighbours(feature_map[:, 0, :], feature_map[:, rows - 1, :])
    x_rows = jnp.transpose(feature_map, (1, 0, 2))
    weights = jnp.pad(
        jnp.transpose(kernel, (0, 1, 3, 2)), ((0, 0), (0, 0), (0, padded_chans - chans), (0, 0))
    ).reshape(9 * padded_chans, hidden)
    offset = jnp.pad(
        lax.dynamic_slice(noise_table, (noise_seed[0, 0], 0), (1, chans))[0],
        (0, padded_chans - chans),
    )
    offset = jnp.broadcast_to(offset[:, None], (padded_chans, lanes))
    own_truth = jnp.pad(truth[0], ((0, padded_chans - chans), (0, 0), (0, 0)))
    own_truth = lax.dynamic_slice(
        own_truth, ((place % 2) * half_chans, place // 2, 0), (half_chans, 1, cols)
    )[:, 0, :].astype(f32)
    inner = call(
        inner_kernel,
        jax.ShapeDtypeStruct((members, half_chans, cols), f32),
        [vmem] * 3 + [anywhere],
        cost=(2 * hidden * 9 * chans * rows * cols, 4 * hidden * rows * cols),
    )(x_rows, weights, offset, own_truth)
    predicted = call(
        edge_kernel,
        jax.ShapeDtypeStruct((members, half_chans, cols), f32),
        [vmem] * 4,
        cost=(4 * hidden * 3 * chans * cols, 4 * hidden * cols),
    )(inner, x_low, x_high, weights)

    eps_value = (1.0 - alpha_level) / members
    coef = (1.0 - eps_value) / (members - 1)
    deltas = call(
        functools.partial(pair_kernel, coef),
        jax.ShapeDtypeStruct((members, half_chans, cols), bf16),
        [vmem] * 3,
        [pltpu.VMEM((members, half_chans, cols), f32)],
        cost=(members * members * 8 * half_chans * cols, 6 * members * half_chans * cols),
    )(exchange(predicted, "member"), own_truth, area_weight[None])
    delta = exchange(deltas, "member")

    d_low, d_high = neighbours(delta[:2], delta[members - 2 :])
    group = padded_rows // 8
    piece = jax.ShapeDtypeStruct((members, group, lanes), bf16)
    flops = hidden * 9 * chans * rows * cols
    sent, wide_delta = call(
        sent_kernel,
        [piece, jax.ShapeDtypeStruct((taps_chans, rows * cols), bf16)],
        [vmem] * 4,
        cost=(flops, 2 * hidden * rows * cols),
    )(delta, x_rows, x_low, x_high)
    swap = [(0, 1), (1, 0)]
    part = call(
        kept_kernel,
        piece,
        [vmem] * 5,
        cost=(flops, 2 * hidden * rows * cols),
    )(wide_delta, x_rows, x_low, x_high, lax.ppermute(sent, "rep", swap))
    grad_rows = call(
        feature_grad_kernel,
        jax.ShapeDtypeStruct((rows, hidden, cols), bf16),
        [vmem] * 4,
        cost=(2 * hidden * 9 * chans * rows * cols, 4 * hidden * rows * cols),
    )(weights, wide_delta, d_low, d_high)
    feature_grad = jnp.transpose(grad_rows, (1, 0, 2))[None, None]

    bands = lax.axis_size("band")
    near = 4
    far = bands // near
    nearby = [[far_step * near + step for step in range(near)] for far_step in range(far)]
    distant = [[far_step * near + step for far_step in range(far)] for step in range(near)]
    part = summed(exchange(part, "member"), far)
    part = summed(exchange(part, "band", distant), near, after=(d_low, d_high))
    scale = 1.0 / math.sqrt(lax.axis_size("rep") * members * bands * rows * cols)
    part = summed(exchange(part, "band", nearby), members, scale, after=(feature_grad,))
    part = exchange(part, "member")
    other = lax.ppermute(part, "rep", swap)
    kernel_grad = placed(False, part, (9, chans, hidden))
    kernel_grad = placed(True, other, (9, chans, hidden), kernel_grad)
    kernel_grad = jnp.transpose(kernel_grad.reshape(3, 3, chans, hidden), (0, 1, 3, 2))
    return (feature_grad, kernel_grad)


def solution(mesh):
    return jax.shard_map(
        local,
        mesh=mesh,
        in_specs=(
            P("rep", "member", None, "band", None),
            P(),
            P("rep", "member"),
            P(),
            P("rep", None, "band", None),
            P("band"),
        ),
        out_specs=(P("rep", "member", None, "band", None), P()),
        check_vma=False,
    )
```

time: 123 us -> 120 us (0.976)
  waiting for transfers between devices: 28.4 us -> 11.2 us
  blocking collectives: 33.2 us -> 50.4 us
  starting transfers between devices: 47.5 us -> 45 us
    all_to_all x3 -> x4, blocking collectives: 33.2 us -> 50.4 us  [exchange(): lax.all_to_all(block, axis, 0, 0, axis_index_groups=groups, tiled=True)]
    all_to_all x3 -> x2, waiting for transfers between devices: 19.9 us -> 8.43 us  [exchange(): lax.all_to_all(block, axis, 0, 0, axis_index_groups=groups, tiled=True)]
    ppermute x2, waiting for transfers between devices: 7.08 us -> 0.08 us  [neighbours(): lax.ppermute(low_edge, 'band', backward)]
    all_to_all x3 -> x2, starting transfers between devices: 24.4 us -> 18.9 us  [exchange(): lax.all_to_all(block, axis, 0, 0, axis_index_groups=groups, tiled=True)]
    ppermute x2, starting transfers between devices: 7.02 us -> 8.99 us  [neighbours(): lax.ppermute(high_edge, 'band', forward)]
    pallas_call x1, Pallas kernels: 2.12 us -> 0.78 us  [local(): call(functools.partial(pair_kernel, coef), jax.ShapeDtypeStruct((members,...]
    pallas_call x4 -> x6, Pallas kernels: 4.95 us -> 4.86 us  [the longest x2 1.96 us: placed(): pl.pallas_call(functools.partial(finish_kernel, away), out_shape=jax.Shap...]
  transfers between devices with their start and end apart: 9 -> 8, of which waited for: 6 -> 6; matrix products, arithmetic and copies ran while one was open for 1% -> 1% of each run, Pallas kernels for 1% -> 3%
where the time goes in v3:
time: 120 us; the launch traced here: 119 us
  blocking collectives  50.4 us (42%)
  starting transfers between devices  45 us (38%)
  waiting for transfers between devices  11.2 us (9%)
  Pallas kernels  8.35 us (7%)
  local copies, waits for them, and re-layouts  2.37 us (2%)
  between operations  1.59 us (1%)
    all_to_all x4, blocking collectives, exchange(): lax.all_to_all(block, axis, 0, 0, axis_index_groups=groups, tiled=True)  50.4 us
    all_to_all x2, starting transfers between devices, exchange(): lax.all_to_all(block, axis, 0, 0, axis_index_groups=groups, tiled=True)  18.9 us
    ppermute x2, starting transfers between devices, neighbours(): lax.ppermute(high_edge, 'band', forward)  8.99 us
    all_to_all x2, waiting for transfers between devices, exchange(): lax.all_to_all(block, axis, 0, 0, axis_index_groups=groups, tiled=True)  8.43 us
    ppermute x1, starting transfers between devices, local(): other = lax.ppermute(part, 'rep', swap)  7.34 us
    ppermute x1, starting transfers between devices, local(): lax.ppermute(sent, 'rep', swap)  7.15 us
    ppermute x2, starting transfers between devices, neighbours(): lax.ppermute(low_edge, 'band', backward)  2.57 us
  transfers between devices with their start and end apart: 8, of which 6 were waited for; matrix products, arithmetic and copies ran while one was open for 1% of the time, Pallas kernels for 3%

profile of v3, /device:TPU:1, one launch (start us, length us, event | category | flops | bytes accessed | tf_op | source)
XLA Modules:
  0.0 118.9 jit_solution(10237992453301199738)
XLA Ops:
  0.7 1.5 %copy.17 = bf16[1,1,512,8,128]{4,2,3,1,0:T(8,128)(2,1)S(1)} copy(bf16[1,1,512,8,128]{4,3,2,1,0:T(8,128)(2,1)} %param.6) | data formatting | bytes 2097152 | tf_op args[0]
  2.1 1.3 %collective-permute-start.1 = (bf16[512,128]{1,0:T(8,128)(2,1)S(1)}, bf16[512,128]{1,0:T(8,128)(2,1)S(1)}, u32[]{:S(2)}, u32[]{:S(2)}) collective-permute-start(bf16[512,128]{1,0:T(8,128)(2,1)S(1)} %get-tuple-element.6), channel_id=1, source_target_pairs={{2,0},{4,2},{6,4},{8,6},{10,8},{12,10},{14,12},{16,14},{18,16},{20... | collective-permute-start | bytes 393224 | tf_op jit(solution)/shard_map/ppermute | solution.py:228
  3.4 5.0 %collective-permute-start = (bf16[512,128]{1,0:T(8,128)(2,1)S(1)}, bf16[512,128]{1,0:T(8,128)(2,1)S(1)}, u32[]{:S(2)}, u32[]{:S(2)}) collective-permute-start(bf16[512,128]{1,0:T(8,128)(2,1)S(1)} %get-tuple-element.7), channel_id=1, source_target_pairs={{0,2},{2,4},{4,6},{6,8},{8,10},{10,12},{12,14},{14,16},{16,18},{18... | collective-permute-start | bytes 393224 | tf_op jit(solution)/shard_map/ppermute | solution.py:228
  9.4 1.2 shard_map.77.inner_ref
  11.0 14.8 %all_to_all.30.values_ref = f32[16,48,128]{2,1,0:T(8,128)S(1)} all-to-all(f32[16,48,128]{2,1,0:T(8,128)S(1)} %shard_map.78), channel_id=1, replica_groups=mesh['member'=16,'band'=16,'rep'=2] {'member'}, dimensions={0} | all-to-all | bytes 786432 | tf_op jit(solution)/shard_map/all_to_all | solution.py:232
  25.9 0.8 shard_map.79
  26.6 9.9 %all_to_all.31.delta_ref = bf16[16,48,128]{2,1,0:T(8,128)(2,1)S(1)} all-to-all(bf16[16,48,128]{2,1,0:T(8,128)(2,1)S(1)} %shard_map.79), channel_id=1, replica_groups=mesh['member'=16,'band'=16,'rep'=2] {'member'}, dimensions={0} | all-to-all | bytes 393216 | tf_op jit(solution)/shard_map/all_to_all | solution.py:232
  37.3 7.1 %collective-permute-start.4 = (bf16[16,112,128]{2,1,0:T(8,128)(2,1)S(1)}, bf16[16,112,128]{2,1,0:T(8,128)(2,1)S(1)}, u32[]{:S(2)}, u32[]{:S(2)}) collective-permute-start(bf16[16,112,128]{2,1,0:T(8,128)(2,1)S(1)} %get-tuple-element.5), channel_id=1, source_target_pairs={{0,1},{1,0},{2,3},{3,2},{4,5},{5,4},{6,7},{7,6},{8,9},{9,8},{10,11... | collective-permute-start | bytes 1376264 | tf_op jit(solution)/shard_map/ppermute | solution.py:324
  44.4 1.4 %collective-permute-done.4.other_ref = bf16[16,112,128]{2,1,0:T(8,128)(2,1)S(1)} collective-permute-done((bf16[16,112,128]{2,1,0:T(8,128)(2,1)S(1)}, bf16[16,112,128]{2,1,0:T(8,128)(2,1)S(1)}, u32[]{:S(2)}, u32[]{:S(2)}) %collective-permute-start.4) | collective-permute-done | bytes 458784 | tf_op jit(solution)/shard_map/ppermute | solution.py:324
  46.5 12.6 %all_to_all.32.parts_ref = bf16[16,112,128]{2,1,0:T(8,128)(2,1)S(1)} all-to-all(bf16[16,112,128]{2,1,0:T(8,128)(2,1)S(1)} %shard_map.82), channel_id=1, replica_groups=mesh['member'=16,'band'=16,'rep'=2] {'member'}, dimensions={0} | all-to-all | bytes 917504 | tf_op jit(solution)/shard_map/all_to_all | solution.py:232
  59.1 0.7 shard_map.83
  59.8 15.6 %all-to-all-start.3 = ((bf16[4,112,128]{2,1,0:T(8,128)(2,1)}), bf16[4,112,128]{2,1,0:T(8,128)(2,1)S(1)}, u32[]{:S(2)}, u32[]{:S(2)}) async-start(bf16[4,112,128]{2,1,0:T(8,128)(2,1)} %shard_map.83), calls=%async_computation.3 | async-start | bytes 229376 | tf_op jit(solution)/shard_map/all_to_all | solution.py:232
  75.4 1.3 %collective-permute-start.3 = (bf16[2,48,128]{2,1,0:T(8,128)(2,1)S(1)}, bf16[2,48,128]{2,1,0:T(8,128)(2,1)S(1)}, u32[]{:S(2)}, u32[]{:S(2)}) collective-permute-start(bf16[2,48,128]{2,1,0:T(8,128)(2,1)S(1)} %get-tuple-element.10), channel_id=1, source_target_pairs={{2,0},{4,2},{6,4},{8,6},{10,8},{12,10},{14,12},{16,14},{18,16},{20... | collective-permute-start | bytes 73736 | tf_op jit(solution)/shard_map/ppermute | solution.py:228
  76.7 4.0 %collective-permute-start.2 = (bf16[2,48,128]{2,1,0:T(8,128)(2,1)S(1)}, bf16[2,48,128]{2,1,0:T(8,128)(2,1)S(1)}, u32[]{:S(2)}, u32[]{:S(2)}) collective-permute-start(bf16[2,48,128]{2,1,0:T(8,128)(2,1)S(1)} %get-tuple-element.11), channel_id=1, source_target_pairs={{0,2},{2,4},{4,6},{6,8},{8,10},{10,12},{12,14},{14,16},{16,18},{18... | collective-permute-start | bytes 73736 | tf_op jit(solution)/shard_map/ppermute | solution.py:228
  80.8 0.9 collective-permute-done.2.low_ref.refs_0_
  81.6 5.7 %all-to-all-done.3.parts_ref = bf16[4,112,128]{2,1,0:T(8,128)(2,1)S(1)} async-done(((bf16[4,112,128]{2,1,0:T(8,128)(2,1)}), bf16[4,112,128]{2,1,0:T(8,128)(2,1)S(1)}, u32[]{:S(2)}, u32[]{:S(2)}) %all-to-all-start.3) | async-done | bytes 114720 | tf_op jit(solution)/shard_map/all_to_all | solution.py:232
  88.0 3.3 %all-to-all-start.4 = ((bf16[4,112,128]{2,1,0:T(8,128)(2,1)}), bf16[4,112,128]{2,1,0:T(8,128)(2,1)S(1)}, u32[]{:S(2)}, u32[]{:S(2)}) async-start(bf16[4,112,128]{2,1,0:T(8,128)(2,1)} %shard_map.84), calls=%async_computation.4 | async-start | bytes 229376 | tf_op jit(solution)/shard_map/all_to_all | solution.py:232
  91.4 1.3 %shard_map.81 = bf16[8,512,128]{2,1,0:T(8,128)(2,1)S(1)} custom-call(bf16[864,512]{1,0:T(8,128)(2,1)S(1)} %bitcast.41, bf16[288,1024]{1,0:T(8,128)(2,1)S(1)} %get-tuple-element.4.spread_ref, bf16[2,48,128]{2,1,0:T(8,128)(2,1)S(1)} %collective-permute-done.2.low_ref.refs_0_, bf16[2,48,128]{2,1,0:T(8,128)(2,1)S(1)} %collective-permute-done.3.high_ref.refs_1_), custom_call_target="tpu_custom_call" | custom-call | flops 849346560 | bytes 2097152 | tf_op jit(solution)/shard_map/pallas_call | solution.py:325
  92.7 0.7 copy.16
  93.4 2.7 %all-to-all-done.4.parts_ref = bf16[4,112,128]{2,1,0:T(8,128)(2,1)S(1)} async-done(((bf16[4,112,128]{2,1,0:T(8,128)(2,1)}), bf16[4,112,128]{2,1,0:T(8,128)(2,1)S(1)}, u32[]{:S(2)}, u32[]{:S(2)}) %all-to-all-start.4) | async-done | bytes 114720 | tf_op jit(solution)/shard_map/all_to_all | solution.py:232
  96.1 13.0 %all_to_all.33.source_ref = bf16[16,112,128]{2,1,0:T(8,128)(2,1)S(1)} all-to-all(bf16[16,112,128]{2,1,0:T(8,128)(2,1)S(1)} %shard_map.85), channel_id=1, replica_groups=mesh['member'=16,'band'=16,'rep'=2] {'member'}, dimensions={0} | all-to-all | bytes 917504 | tf_op jit(solution)/shard_map/all_to_all | solution.py:232
  109.1 7.3 %collective-permute-start.5 = (bf16[16,112,128]{2,1,0:T(8,128)(2,1)S(1)}, bf16[16,112,128]{2,1,0:T(8,128)(2,1)S(1)}, u32[]{:S(2)}, u32[]{:S(2)}) collective-permute-start(bf16[16,112,128]{2,1,0:T(8,128)(2,1)S(1)} %all_to_all.33.source_ref), channel_id=1, source_target_pairs={{0,1},{1,0},{2,3},{3,2},{4,5},{5,4},{6,7},{7,6},{8,9},{9,8},{10,11... | collective-permute-start | bytes 1376264 | tf_op jit(solution)/shard_map/ppermute | solution.py:343
  116.5 1.0 shard_map.86.refs_0_
  117.9 1.0 shard_map.87
  (27 shorter events, 3.2 us)
Async XLA Ops:
  0.6 8.6 %copy-start = (f32[32,90]{1,0:T(8,128)S(1)}, f32[32,90]{1,0:T(8,128)}, u32[]{:S(2)}) copy-start(f32[32,90]{1,0:T(8,128)} %param.9) | copy-start | bytes 34564
  0.6 8.5 %copy-start.4 = (bf16[1,90,8,128]{3,2,1,0:T(8,128)(2,1)S(1)}, bf16[1,90,8,128]{3,2,1,0:T(8,128)(2,1)}, u32[]{:S(2)}) copy-start(bf16[1,90,8,128]{3,2,1,0:T(8,128)(2,1)} %param.10) | copy-start | bytes 552964
  0.7 8.6 %copy-start.3 = (bf16[3,3,512,90]{2,3,1,0:T(8,128)(2,1)S(1)}, bf16[3,3,512,90]{2,3,1,0:T(8,128)(2,1)}, u32[]{:S(2)}) copy-start(bf16[3,3,512,90]{2,3,1,0:T(8,128)(2,1)} %param.7) | copy-start | bytes 2488324
  2.1 8.5 %collective-permute-start.1 = (bf16[512,128]{1,0:T(8,128)(2,1)S(1)}, bf16[512,128]{1,0:T(8,128)(2,1)S(1)}, u32[]{:S(2)}, u32[]{:S(2)}) collective-permute-start(bf16[512,128]{1,0:T(8,128)(2,1)S(1)} %get-tuple-element.6), channel_id=1, source_target_pairs={{2,0},{4,2},{6,4},{8,6},{10,8},{12,10},{14,12},{16,14},{18,16},{20... | collective-permute-start | bytes 393224 | tf_op jit(solution)/shard_map/ppermute | solution.py:228
  3.4 7.2 %collective-permute-start = (bf16[512,128]{1,0:T(8,128)(2,1)S(1)}, bf16[512,128]{1,0:T(8,128)(2,1)S(1)}, u32[]{:S(2)}, u32[]{:S(2)}) collective-permute-start(bf16[512,128]{1,0:T(8,128)(2,1)S(1)} %get-tuple-element.7), channel_id=1, source_target_pairs={{0,2},{2,4},{4,6},{6,8},{8,10},{10,12},{12,14},{14,16},{16,18},{18... | collective-permute-start | bytes 393224 | tf_op jit(solution)/shard_map/ppermute | solution.py:228
  10.6 15.2 %copy-start.2 = (f32[8]{0:T(128)S(1)}, f32[8]{0:T(128)}, u32[]{:S(2)}) copy-start(f32[8]{0:T(128)} %param.11) | copy-start | bytes 100
  37.3 8.6 %collective-permute-start.4 = (bf16[16,112,128]{2,1,0:T(8,128)(2,1)S(1)}, bf16[16,112,128]{2,1,0:T(8,128)(2,1)S(1)}, u32[]{:S(2)}, u32[]{:S(2)}) collective-permute-start(bf16[16,112,128]{2,1,0:T(8,128)(2,1)S(1)} %get-tuple-element.5), channel_id=1, source_target_pairs={{0,1},{1,0},{2,3},{3,2},{4,5},{5,4},{6,7},{7,6},{8,9},{9,8},{10,11... | collective-permute-start | bytes 1376264 | tf_op jit(solution)/shard_map/ppermute | solution.py:324
  59.8 27.5 %all-to-all-start.3 = ((bf16[4,112,128]{2,1,0:T(8,128)(2,1)}), bf16[4,112,128]{2,1,0:T(8,128)(2,1)S(1)}, u32[]{:S(2)}, u32[]{:S(2)}) async-start(bf16[4,112,128]{2,1,0:T(8,128)(2,1)} %shard_map.83), calls=%async_computation.3 | async-start | bytes 229376 | tf_op jit(solution)/shard_map/all_to_all | solution.py:232
  75.4 5.4 %collective-permute-start.3 = (bf16[2,48,128]{2,1,0:T(8,128)(2,1)S(1)}, bf16[2,48,128]{2,1,0:T(8,128)(2,1)S(1)}, u32[]{:S(2)}, u32[]{:S(2)}) collective-permute-start(bf16[2,48,128]{2,1,0:T(8,128)(2,1)S(1)} %get-tuple-element.10), channel_id=1, source_target_pairs={{2,0},{4,2},{6,4},{8,6},{10,8},{12,10},{14,12},{16,14},{18,16},{20... | collective-permute-start | bytes 73736 | tf_op jit(solution)/shard_map/ppermute | solution.py:228
  76.7 4.9 %collective-permute-start.2 = (bf16[2,48,128]{2,1,0:T(8,128)(2,1)S(1)}, bf16[2,48,128]{2,1,0:T(8,128)(2,1)S(1)}, u32[]{:S(2)}, u32[]{:S(2)}) collective-permute-start(bf16[2,48,128]{2,1,0:T(8,128)(2,1)S(1)} %get-tuple-element.11), channel_id=1, source_target_pairs={{0,2},{2,4},{4,6},{6,8},{8,10},{10,12},{12,14},{14,16},{16,18},{18... | collective-permute-start | bytes 73736 | tf_op jit(solution)/shard_map/ppermute | solution.py:228
  88.0 8.0 %all-to-all-start.4 = ((bf16[4,112,128]{2,1,0:T(8,128)(2,1)}), bf16[4,112,128]{2,1,0:T(8,128)(2,1)S(1)}, u32[]{:S(2)}, u32[]{:S(2)}) async-start(bf16[4,112,128]{2,1,0:T(8,128)(2,1)} %shard_map.84), calls=%async_computation.4 | async-start | bytes 229376 | tf_op jit(solution)/shard_map/all_to_all | solution.py:232
  93.3 24.1 %copy-start.1 = (bf16[8,512,128]{2,0,1:T(8,128)(2,1)}, bf16[8,512,128]{2,0,1:T(8,128)(2,1)S(1)}, u32[]{:S(2)}) copy-start(bf16[8,512,128]{2,0,1:T(8,128)(2,1)S(1)} %copy.16) | copy-start | bytes 3145732
  109.1 8.8 %collective-permute-start.5 = (bf16[16,112,128]{2,1,0:T(8,128)(2,1)S(1)}, bf16[16,112,128]{2,1,0:T(8,128)(2,1)S(1)}, u32[]{:S(2)}, u32[]{:S(2)}) collective-permute-start(bf16[16,112,128]{2,1,0:T(8,128)(2,1)S(1)} %all_to_all.33.source_ref), channel_id=1, source_target_pairs={{0,1},{1,0},{2,3},{3,2},{4,5},{5,4},{6,7},{7,6},{8,9},{9,8},{10,11... | collective-permute-start | bytes 1376264 | tf_op jit(solution)/shard_map/ppermute | solution.py:343

commit v4 on v3

--- a/solution.py
+++ b/solution.py
@@ -335,8 +335,9 @@
     far = bands // near
     nearby = [[far_step * near + step for step in range(near)] for far_step in range(far)]
     distant = [[far_step * near + step for far_step in range(far)] for step in range(near)]
-    part = summed(exchange(part, "member"), far)
-    part = summed(exchange(part, "band", distant), near, after=(d_low, d_high))
+    part = summed(exchange(part, "member"), 1)
+    part = lax.all_gather(part[0], "band", axis=0, axis_index_groups=distant)
+    part = summed(part, near, after=(d_low, d_high))
     scale = 1.0 / math.sqrt(lax.axis_size("rep") * members * bands * rows * cols)
     part = summed(exchange(part, "band", nearby), members, scale, after=(feature_grad,))
     part = exchange(part, "member")

time: 120 us -> 117 us (0.975)
  starting transfers between devices: 45 us -> 34 us
  blocking collectives: 50.4 us -> 61 us
  waiting for transfers between devices: 11.2 us -> 8.79 us
    all_gather x0 -> x1, blocking collectives: none -> 24.8 us  [local(): part = lax.all_gather(part[0], 'band', axis=0, axis_index_groups=distant)]
    all_to_all x4 -> x3, blocking collectives: 50.4 us -> 36.2 us  [exchange(): lax.all_to_all(block, axis, 0, 0, axis_index_groups=groups, tiled=True)]
    all_to_all x2, starting transfers between devices: 18.9 us -> 6.88 us  [exchange(): lax.all_to_all(block, axis, 0, 0, axis_index_groups=groups, tiled=True)]
    all_to_all x2, waiting for transfers between devices: 8.43 us -> 6.93 us  [exchange(): lax.all_to_all(block, axis, 0, 0, axis_index_groups=groups, tiled=True)]
  transfers between devices with their start and end apart: 8 -> 8, of which waited for: 6 -> 4; matrix products, arithmetic and copies ran while one was open for 1% -> 1% of each run, Pallas kernels for 3% -> 3%
where the time goes in v4:
time: 117 us; the launch traced here: 116 us
  blocking collectives  61 us (52%)
  starting transfers between devices  34 us (29%)
  waiting for transfers between devices  8.79 us (8%)
  Pallas kernels  8.47 us (7%)
  local copies, waits for them, and re-layouts  2.37 us (2%)
  between operations  1.6 us (1%)
    all_to_all x3, blocking collectives, exchange(): lax.all_to_all(block, axis, 0, 0, axis_index_groups=groups, tiled=True)  36.2 us
    all_gather x1, blocking collectives, local(): part = lax.all_gather(part[0], 'band', axis=0, axis_index_groups=distant)  24.8 us
    ppermute x2, starting transfers between devices, neighbours(): lax.ppermute(high_edge, 'band', forward)  9.71 us
    ppermute x1, starting transfers between devices, local(): other = lax.ppermute(part, 'rep', swap)  7.67 us
    ppermute x1, starting transfers between devices, local(): lax.ppermute(sent, 'rep', swap)  7.15 us
    all_to_all x2, waiting for transfers between devices, exchange(): lax.all_to_all(block, axis, 0, 0, axis_index_groups=groups, tiled=True)  6.93 us
    all_to_all x2, starting transfers between devices, exchange(): lax.all_to_all(block, axis, 0, 0, axis_index_groups=groups, tiled=True)  6.88 us
    ppermute x2, starting transfers between devices, neighbours(): lax.ppermute(low_edge, 'band', backward)  2.58 us
  transfers between devices with their start and end apart: 8, of which 4 were waited for; matrix products, arithmetic and copies ran while one was open for 1% of the time, Pallas kernels for 3%

profile of v4, /device:TPU:1, one launch (start us, length us, event | category | flops | bytes accessed | tf_op | source)
XLA Modules:
  0.0 116.2 jit_solution(2487951475424474416)
XLA Ops:
  0.7 1.5 %copy.20 = bf16[1,1,512,8,128]{4,2,3,1,0:T(8,128)(2,1)S(1)} copy(bf16[1,1,512,8,128]{4,3,2,1,0:T(8,128)(2,1)} %param.6) | data formatting | bytes 2097152 | tf_op args[0]
  2.1 1.3 %collective-permute-start.1 = (bf16[512,128]{1,0:T(8,128)(2,1)S(1)}, bf16[512,128]{1,0:T(8,128)(2,1)S(1)}, u32[]{:S(2)}, u32[]{:S(2)}) collective-permute-start(bf16[512,128]{1,0:T(8,128)(2,1)S(1)} %get-tuple-element.6), channel_id=1, source_target_pairs={{2,0},{4,2},{6,4},{8,6},{10,8},{12,10},{14,12},{16,14},{18,16},{20... | collective-permute-start | bytes 393224 | tf_op jit(solution)/shard_map/ppermute | solution.py:228
  3.4 5.0 %collective-permute-start = (bf16[512,128]{1,0:T(8,128)(2,1)S(1)}, bf16[512,128]{1,0:T(8,128)(2,1)S(1)}, u32[]{:S(2)}, u32[]{:S(2)}) collective-permute-start(bf16[512,128]{1,0:T(8,128)(2,1)S(1)} %get-tuple-element.7), channel_id=1, source_target_pairs={{0,2},{2,4},{4,6},{6,8},{8,10},{10,12},{12,14},{14,16},{16,18},{18... | collective-permute-start | bytes 393224 | tf_op jit(solution)/shard_map/ppermute | solution.py:228
  9.4 1.2 %shard_map.77.inner_ref = f32[16,48,128]{2,1,0:T(8,128)S(1)} custom-call(bf16[8,512,128]{2,1,0:T(8,128)(2,1)S(1)} %bitcast.34, bf16[864,512]{1,0:T(8,128)(2,1)S(1)} %bitcast.39, f32[96,128]{1,0:T(8,128)S(1)} %broadcast_in_dim.12.offset_ref, f32[48,128]{1,0:T(8,128)S(1)} %bitcast_convert_fusion.truth_ref), custom_call_target="tpu_custom_call" | custom-call | flops 849346560 | bytes 2097152 | tf_op jit(solution)/shard_map/pallas_call | solution.py:284
  11.0 14.8 %all_to_all.25.values_ref = f32[16,48,128]{2,1,0:T(8,128)S(1)} all-to-all(f32[16,48,128]{2,1,0:T(8,128)S(1)} %shard_map.78), channel_id=1, replica_groups=mesh['member'=16,'band'=16,'rep'=2] {'member'}, dimensions={0} | all-to-all | bytes 786432 | tf_op jit(solution)/shard_map/all_to_all | solution.py:232
  25.9 0.8 shard_map.79
  26.6 9.9 %all_to_all.26.delta_ref = bf16[16,48,128]{2,1,0:T(8,128)(2,1)S(1)} all-to-all(bf16[16,48,128]{2,1,0:T(8,128)(2,1)S(1)} %shard_map.79), channel_id=1, replica_groups=mesh['member'=16,'band'=16,'rep'=2] {'member'}, dimensions={0} | all-to-all | bytes 393216 | tf_op jit(solution)/shard_map/all_to_all | solution.py:232
  36.6 0.7 shard_map.80
  37.3 7.1 %collective-permute-start.4 = (bf16[16,112,128]{2,1,0:T(8,128)(2,1)S(1)}, bf16[16,112,128]{2,1,0:T(8,128)(2,1)S(1)}, u32[]{:S(2)}, u32[]{:S(2)}) collective-permute-start(bf16[16,112,128]{2,1,0:T(8,128)(2,1)S(1)} %get-tuple-element.5), channel_id=1, source_target_pairs={{0,1},{1,0},{2,3},{3,2},{4,5},{5,4},{6,7},{7,6},{8,9},{9,8},{10,11... | collective-permute-start | bytes 1376264 | tf_op jit(solution)/shard_map/ppermute | solution.py:324
  44.4 1.4 %collective-permute-done.4.other_ref = bf16[16,112,128]{2,1,0:T(8,128)(2,1)S(1)} collective-permute-done((bf16[16,112,128]{2,1,0:T(8,128)(2,1)S(1)}, bf16[16,112,128]{2,1,0:T(8,128)(2,1)S(1)}, u32[]{:S(2)}, u32[]{:S(2)}) %collective-permute-start.4) | collective-permute-done | bytes 458784 | tf_op jit(solution)/shard_map/ppermute | solution.py:324
  45.8 1.4 %shard_map.82 = bf16[16,112,128]{2,1,0:T(8,128)(2,1)} custom-call(bf16[288,1024]{1,0:T(8,128)(2,1)S(1)} %get-tuple-element.4.spread_ref, bf16[8,512,128]{2,1,0:T(8,128)(2,1)S(1)} %bitcast.36, bf16[512,128]{1,0:T(8,128)(2,1)S(1)} %collective-permute-done.low_ref, bf16[512,128]{1,0:T(8,128)(2,1)S(1)} %collective-permute-done.1.high_ref, ...), custom_call_target="tpu_custom_call" | custom-call | flops 424673280 | bytes 1048576 | tf_op jit(solution)/shard_map/pallas_call | solution.py:319
  47.3 3.6 %all-to-all-start.2 = ((bf16[16,112,128]{2,1,0:T(8,128)(2,1)}), bf16[16,112,128]{2,1,0:T(8,128)(2,1)S(1)}, u32[]{:S(2)}, u32[]{:S(2)}) async-start(bf16[16,112,128]{2,1,0:T(8,128)(2,1)} %shard_map.82), calls=%async_computation.2 | async-start | bytes 917504 | tf_op jit(solution)/shard_map/all_to_all | solution.py:232
  50.8 1.3 %collective-permute-start.3 = (bf16[2,48,128]{2,1,0:T(8,128)(2,1)S(1)}, bf16[2,48,128]{2,1,0:T(8,128)(2,1)S(1)}, u32[]{:S(2)}, u32[]{:S(2)}) collective-permute-start(bf16[2,48,128]{2,1,0:T(8,128)(2,1)S(1)} %get-tuple-element.10), channel_id=1, source_target_pairs={{2,0},{4,2},{6,4},{8,6},{10,8},{12,10},{14,12},{16,14},{18,16},{20... | collective-permute-start | bytes 73736 | tf_op jit(solution)/shard_map/ppermute | solution.py:228
  52.1 4.7 %collective-permute-start.2 = (bf16[2,48,128]{2,1,0:T(8,128)(2,1)S(1)}, bf16[2,48,128]{2,1,0:T(8,128)(2,1)S(1)}, u32[]{:S(2)}, u32[]{:S(2)}) collective-permute-start(bf16[2,48,128]{2,1,0:T(8,128)(2,1)S(1)} %get-tuple-element.11), channel_id=1, source_target_pairs={{0,2},{2,4},{4,6},{6,8},{8,10},{10,12},{12,14},{14,16},{16,18},{18... | collective-permute-start | bytes 73736 | tf_op jit(solution)/shard_map/ppermute | solution.py:228
  56.9 4.2 %all-to-all-done.2.parts_ref = bf16[16,112,128]{2,1,0:T(8,128)(2,1)S(1)} async-done(((bf16[16,112,128]{2,1,0:T(8,128)(2,1)}), bf16[16,112,128]{2,1,0:T(8,128)(2,1)S(1)}, u32[]{:S(2)}, u32[]{:S(2)}) %all-to-all-start.2) | async-done | bytes 458784 | tf_op jit(solution)/shard_map/all_to_all | solution.py:232
  61.2 24.8 %all_gather.3.parts_ref = bf16[4,112,128]{2,1,0:T(8,128)(2,1)S(1)} all-gather(bf16[1,112,128]{2,1,0:T(8,128)(2,1)S(1)} %shard_map.83), channel_id=1, replica_groups={{0,8,16,24},{2,10,18,26},{4,12,20,28},{6,14,22,30},{1,9,17,25},{3,11,19..., dimensions={0}, use_global_device_ids=true | all-gather | bytes 143360 | tf_op jit(solution)/shard_map/all_gather | solution.py:339
  86.7 3.3 %all-to-all-start.3 = ((bf16[4,112,128]{2,1,0:T(8,128)(2,1)}), bf16[4,112,128]{2,1,0:T(8,128)(2,1)S(1)}, u32[]{:S(2)}, u32[]{:S(2)}) async-start(bf16[4,112,128]{2,1,0:T(8,128)(2,1)} %shard_map.84), calls=%async_computation.3 | async-start | bytes 229376 | tf_op jit(solution)/shard_map/all_to_all | solution.py:232
  90.0 1.3 %shard_map.81 = bf16[8,512,128]{2,1,0:T(8,128)(2,1)S(1)} custom-call(bf16[864,512]{1,0:T(8,128)(2,1)S(1)} %bitcast.41, bf16[288,1024]{1,0:T(8,128)(2,1)S(1)} %get-tuple-element.4.spread_ref, bf16[2,48,128]{2,1,0:T(8,128)(2,1)S(1)} %collective-permute-done.2.low_ref.refs_0_, bf16[2,48,128]{2,1,0:T(8,128)(2,1)S(1)} %collective-permute-done.3.high_ref.refs_1_), custom_call_target="tpu_custom_call" | custom-call | flops 849346560 | bytes 2097152 | tf_op jit(solution)/shard_map/pallas_call | solution.py:325
  91.3 0.7 copy.19
  92.0 2.7 %all-to-all-done.3.parts_ref = bf16[4,112,128]{2,1,0:T(8,128)(2,1)S(1)} async-done(((bf16[4,112,128]{2,1,0:T(8,128)(2,1)}), bf16[4,112,128]{2,1,0:T(8,128)(2,1)S(1)}, u32[]{:S(2)}, u32[]{:S(2)}) %all-to-all-start.3) | async-done | bytes 114720 | tf_op jit(solution)/shard_map/all_to_all | solution.py:232
  94.7 11.4 %all_to_all.27.source_ref = bf16[16,112,128]{2,1,0:T(8,128)(2,1)S(1)} all-to-all(bf16[16,112,128]{2,1,0:T(8,128)(2,1)S(1)} %shard_map.85), channel_id=1, replica_groups=mesh['member'=16,'band'=16,'rep'=2] {'member'}, dimensions={0} | all-to-all | bytes 917504 | tf_op jit(solution)/shard_map/all_to_all | solution.py:232
  106.2 7.7 %collective-permute-start.5 = (bf16[16,112,128]{2,1,0:T(8,128)(2,1)S(1)}, bf16[16,112,128]{2,1,0:T(8,128)(2,1)S(1)}, u32[]{:S(2)}, u32[]{:S(2)}) collective-permute-start(bf16[16,112,128]{2,1,0:T(8,128)(2,1)S(1)} %all_to_all.27.source_ref), channel_id=1, source_target_pairs={{0,1},{1,0},{2,3},{3,2},{4,5},{5,4},{6,7},{7,6},{8,9},{9,8},{10,11... | collective-permute-start | bytes 1376264 | tf_op jit(solution)/shard_map/ppermute | solution.py:344
  113.8 1.0 shard_map.86.refs_0_
  115.3 1.0 shard_map.87
  (27 shorter events, 1.9 us)
Async XLA Ops:
  0.6 8.6 %copy-start = (f32[32,90]{1,0:T(8,128)S(1)}, f32[32,90]{1,0:T(8,128)}, u32[]{:S(2)}) copy-start(f32[32,90]{1,0:T(8,128)} %param.9) | copy-start | bytes 34564
  0.6 8.5 %copy-start.4 = (bf16[1,90,8,128]{3,2,1,0:T(8,128)(2,1)S(1)}, bf16[1,90,8,128]{3,2,1,0:T(8,128)(2,1)}, u32[]{:S(2)}) copy-start(bf16[1,90,8,128]{3,2,1,0:T(8,128)(2,1)} %param.10) | copy-start | bytes 552964
  0.7 8.6 %copy-start.3 = (bf16[3,3,512,90]{2,3,1,0:T(8,128)(2,1)S(1)}, bf16[3,3,512,90]{2,3,1,0:T(8,128)(2,1)}, u32[]{:S(2)}) copy-start(bf16[3,3,512,90]{2,3,1,0:T(8,128)(2,1)} %param.7) | copy-start | bytes 2488324
  2.1 8.5 %collective-permute-start.1 = (bf16[512,128]{1,0:T(8,128)(2,1)S(1)}, bf16[512,128]{1,0:T(8,128)(2,1)S(1)}, u32[]{:S(2)}, u32[]{:S(2)}) collective-permute-start(bf16[512,128]{1,0:T(8,128)(2,1)S(1)} %get-tuple-element.6), channel_id=1, source_target_pairs={{2,0},{4,2},{6,4},{8,6},{10,8},{12,10},{14,12},{16,14},{18,16},{20... | collective-permute-start | bytes 393224 | tf_op jit(solution)/shard_map/ppermute | solution.py:228
  3.4 7.2 %collective-permute-start = (bf16[512,128]{1,0:T(8,128)(2,1)S(1)}, bf16[512,128]{1,0:T(8,128)(2,1)S(1)}, u32[]{:S(2)}, u32[]{:S(2)}) collective-permute-start(bf16[512,128]{1,0:T(8,128)(2,1)S(1)} %get-tuple-element.7), channel_id=1, source_target_pairs={{0,2},{2,4},{4,6},{6,8},{8,10},{10,12},{12,14},{14,16},{16,18},{18... | collective-permute-start | bytes 393224 | tf_op jit(solution)/shard_map/ppermute | solution.py:228
  10.6 15.2 %copy-start.2 = (f32[8]{0:T(128)S(1)}, f32[8]{0:T(128)}, u32[]{:S(2)}) copy-start(f32[8]{0:T(128)} %param.11) | copy-start | bytes 100
  37.3 8.6 %collective-permute-start.4 = (bf16[16,112,128]{2,1,0:T(8,128)(2,1)S(1)}, bf16[16,112,128]{2,1,0:T(8,128)(2,1)S(1)}, u32[]{:S(2)}, u32[]{:S(2)}) collective-permute-start(bf16[16,112,128]{2,1,0:T(8,128)(2,1)S(1)} %get-tuple-element.5), channel_id=1, source_target_pairs={{0,1},{1,0},{2,3},{3,2},{4,5},{5,4},{6,7},{7,6},{8,9},{9,8},{10,11... | collective-permute-start | bytes 1376264 | tf_op jit(solution)/shard_map/ppermute | solution.py:324
  47.3 13.8 %all-to-all-start.2 = ((bf16[16,112,128]{2,1,0:T(8,128)(2,1)}), bf16[16,112,128]{2,1,0:T(8,128)(2,1)S(1)}, u32[]{:S(2)}, u32[]{:S(2)}) async-start(bf16[16,112,128]{2,1,0:T(8,128)(2,1)} %shard_map.82), calls=%async_computation.2 | async-start | bytes 917504 | tf_op jit(solution)/shard_map/all_to_all | solution.py:232
  50.8 35.2 %collective-permute-start.3 = (bf16[2,48,128]{2,1,0:T(8,128)(2,1)S(1)}, bf16[2,48,128]{2,1,0:T(8,128)(2,1)S(1)}, u32[]{:S(2)}, u32[]{:S(2)}) collective-permute-start(bf16[2,48,128]{2,1,0:T(8,128)(2,1)S(1)} %get-tuple-element.10), channel_id=1, source_target_pairs={{2,0},{4,2},{6,4},{8,6},{10,8},{12,10},{14,12},{16,14},{18,16},{20... | collective-permute-start | bytes 73736 | tf_op jit(solution)/shard_map/ppermute | solution.py:228
  52.1 33.9 %collective-permute-start.2 = (bf16[2,48,128]{2,1,0:T(8,128)(2,1)S(1)}, bf16[2,48,128]{2,1,0:T(8,128)(2,1)S(1)}, u32[]{:S(2)}, u32[]{:S(2)}) collective-permute-start(bf16[2,48,128]{2,1,0:T(8,128)(2,1)S(1)} %get-tuple-element.11), channel_id=1, source_target_pairs={{0,2},{2,4},{4,6},{6,8},{8,10},{10,12},{12,14},{14,16},{16,18},{18... | collective-permute-start | bytes 73736 | tf_op jit(solution)/shard_map/ppermute | solution.py:228
  86.7 8.0 %all-to-all-start.3 = ((bf16[4,112,128]{2,1,0:T(8,128)(2,1)}), bf16[4,112,128]{2,1,0:T(8,128)(2,1)S(1)}, u32[]{:S(2)}, u32[]{:S(2)}) async-start(bf16[4,112,128]{2,1,0:T(8,128)(2,1)} %shard_map.84), calls=%async_computation.3 | async-start | bytes 229376 | tf_op jit(solution)/shard_map/all_to_all | solution.py:232
  92.0 22.9 %copy-start.1 = (bf16[8,512,128]{2,0,1:T(8,128)(2,1)}, bf16[8,512,128]{2,0,1:T(8,128)(2,1)S(1)}, u32[]{:S(2)}) copy-start(bf16[8,512,128]{2,0,1:T(8,128)(2,1)S(1)} %copy.19) | copy-start | bytes 3145732
  106.2 9.1 %collective-permute-start.5 = (bf16[16,112,128]{2,1,0:T(8,128)(2,1)S(1)}, bf16[16,112,128]{2,1,0:T(8,128)(2,1)S(1)}, u32[]{:S(2)}, u32[]{:S(2)}) collective-permute-start(bf16[16,112,128]{2,1,0:T(8,128)(2,1)S(1)} %all_to_all.27.source_ref), channel_id=1, source_target_pairs={{0,1},{1,0},{2,3},{3,2},{4,5},{5,4},{6,7},{7,6},{8,9},{9,8},{10,11... | collective-permute-start | bytes 1376264 | tf_op jit(solution)/shard_map/ppermute | solution.py:344

commit v5 on v4

--- a/solution.py
+++ b/solution.py
@@ -154,7 +154,7 @@
             block // 2 * group : (block // 2 + 1) * group,
             block % 2 * lanes : (block % 2 + 1) * lanes,
         ]
-        out_ref[block] = (own + other_ref[block].astype(jnp.float32)).astype(jnp.bfloat16)
+        out_ref[block] = (own + other_ref[1 - side, block].astype(jnp.float32)).astype(jnp.bfloat16)
 
 
 def feature_grad_kernel(weight_ref, spread_ref, low_ref, high_ref, out_ref):
@@ -321,7 +321,7 @@
         piece,
         [vmem] * 5,
         cost=(flops, 2 * hidden * rows * cols),
-    )(wide_delta, x_rows, x_low, x_high, lax.ppermute(sent, "rep", swap))
+    )(wide_delta, x_rows, x_low, x_high, lax.all_gather(sent, "rep", axis=0))
     grad_rows = call(
         feature_grad_kernel,
         jax.ShapeDtypeStruct((rows, hidden, cols), bf16),
@@ -335,9 +335,19 @@
     far = bands // near
     nearby = [[far_step * near + step for step in range(near)] for far_step in range(far)]
     distant = [[far_step * near + step for far_step in range(far)] for step in range(near)]
+    def pairs(distance):
+        return [
+            [base + step, base + step + distance]
+            for base in range(0, bands, 2 * distance)
+            for step in range(distance)
+        ]
+
+    def paired(part, distance):
+        return lax.all_gather(part[0], "band", axis=0, axis_index_groups=pairs(distance))
+
     part = summed(exchange(part, "member"), 1)
-    part = lax.all_gather(part[0], "band", axis=0, axis_index_groups=distant)
-    part = summed(part, near, after=(d_low, d_high))
+    part = summed(paired(part, 8), 1, after=(d_low, d_high))
+    part = summed(paired(part, 4), near)
     scale = 1.0 / math.sqrt(lax.axis_size("rep") * members * bands * rows * cols)
     part = summed(exchange(part, "band", nearby), members, scale, after=(feature_grad,))
     part = exchange(part, "member")

time: 117 us -> 115 us (0.983)
  starting transfers between devices: 34 us -> 26.6 us
  blocking collectives: 61 us -> 67.8 us
  waiting for transfers between devices: 8.79 us -> 7.35 us
    ppermute x1 -> x0, starting transfers between devices: 7.15 us -> none  [local(): lax.ppermute(sent, 'rep', swap)]
    all_gather x1 -> x3, blocking collectives: 24.8 us -> 31.6 us  [the longest x2 24.3 us: paired(): lax.all_gather(part[0], 'band', axis=0, axis_index_groups=pairs(distance))]
    ppermute x1 -> x0, waiting for transfers between devices: 1.42 us -> none  [local(): lax.ppermute(sent, 'rep', swap)]
  transfers between devices with their start and end apart: 8 -> 7, of which waited for: 4 -> 3; matrix products, arithmetic and copies ran while one was open for 1% -> 1% of each run, Pallas kernels for 3% -> 3%
where the time goes in v5:
time: 115 us; the launch traced here: 114 us
  blocking collectives  67.8 us (59%)
  starting transfers between devices  26.6 us (23%)
  Pallas kernels  8.47 us (7%)
  waiting for transfers between devices  7.35 us (6%)
  local copies, waits for them, and re-layouts  2.37 us (2%)
  between operations  1.59 us (1%)
    all_to_all x3, blocking collectives, exchange(): lax.all_to_all(block, axis, 0, 0, axis_index_groups=groups, tiled=True)  36.2 us
    all_gather x2, blocking collectives, paired(): lax.all_gather(part[0], 'band', axis=0, axis_index_groups=pairs(distance))  24.3 us
    ppermute x2, starting transfers between devices, neighbours(): lax.ppermute(high_edge, 'band', forward)  9.72 us
    ppermute x1, starting transfers between devices, local(): other = lax.ppermute(part, 'rep', swap)  7.46 us
    all_gather x1, blocking collectives, local(): lax.all_gather(sent, 'rep', axis=0)  7.33 us
    all_to_all x2, waiting for transfers between devices, exchange(): lax.all_to_all(block, axis, 0, 0, axis_index_groups=groups, tiled=True)  6.92 us
    all_to_all x2, starting transfers between devices, exchange(): lax.all_to_all(block, axis, 0, 0, axis_index_groups=groups, tiled=True)  6.88 us
    ppermute x2, starting transfers between devices, neighbours(): lax.ppermute(low_edge, 'band', backward)  2.58 us
  transfers between devices with their start and end apart: 7, of which 3 were waited for; matrix products, arithmetic and copies ran while one was open for 1% of the time, Pallas kernels for 3%

profile of v5, /device:TPU:1, one launch (start us, length us, event | category | flops | bytes accessed | tf_op | source)
XLA Modules:
  0.0 114.2 jit_solution(7087458618713703911)
XLA Ops:
  0.7 1.5 %copy.20 = bf16[1,1,512,8,128]{4,2,3,1,0:T(8,128)(2,1)S(1)} copy(bf16[1,1,512,8,128]{4,3,2,1,0:T(8,128)(2,1)} %param.6) | data formatting | bytes 2097152 | tf_op args[0]
  2.1 1.3 %collective-permute-start.1 = (bf16[512,128]{1,0:T(8,128)(2,1)S(1)}, bf16[512,128]{1,0:T(8,128)(2,1)S(1)}, u32[]{:S(2)}, u32[]{:S(2)}) collective-permute-start(bf16[512,128]{1,0:T(8,128)(2,1)S(1)} %get-tuple-element.6), channel_id=1, source_target_pairs={{2,0},{4,2},{6,4},{8,6},{10,8},{12,10},{14,12},{16,14},{18,16},{20... | collective-permute-start | bytes 393224 | tf_op jit(solution)/shard_map/ppermute | solution.py:228
  3.4 5.0 %collective-permute-start = (bf16[512,128]{1,0:T(8,128)(2,1)S(1)}, bf16[512,128]{1,0:T(8,128)(2,1)S(1)}, u32[]{:S(2)}, u32[]{:S(2)}) collective-permute-start(bf16[512,128]{1,0:T(8,128)(2,1)S(1)} %get-tuple-element.7), channel_id=1, source_target_pairs={{0,2},{2,4},{4,6},{6,8},{8,10},{10,12},{12,14},{14,16},{16,18},{18... | collective-permute-start | bytes 393224 | tf_op jit(solution)/shard_map/ppermute | solution.py:228
  9.4 1.2 %shard_map.77.inner_ref = f32[16,48,128]{2,1,0:T(8,128)S(1)} custom-call(bf16[8,512,128]{2,1,0:T(8,128)(2,1)S(1)} %bitcast.35, bf16[864,512]{1,0:T(8,128)(2,1)S(1)} %bitcast.41, f32[96,128]{1,0:T(8,128)S(1)} %broadcast_in_dim.12.offset_ref, f32[48,128]{1,0:T(8,128)S(1)} %bitcast_convert_fusion.truth_ref), custom_call_target="tpu_custom_call" | custom-call | flops 849346560 | bytes 2097152 | tf_op jit(solution)/shard_map/pallas_call | solution.py:284
  11.0 14.8 %all_to_all.25.values_ref = f32[16,48,128]{2,1,0:T(8,128)S(1)} all-to-all(f32[16,48,128]{2,1,0:T(8,128)S(1)} %shard_map.78), channel_id=1, replica_groups=mesh['member'=16,'band'=16,'rep'=2] {'member'}, dimensions={0} | all-to-all | bytes 786432 | tf_op jit(solution)/shard_map/all_to_all | solution.py:232
  25.9 0.8 shard_map.79
  26.6 9.9 %all_to_all.26.delta_ref = bf16[16,48,128]{2,1,0:T(8,128)(2,1)S(1)} all-to-all(bf16[16,48,128]{2,1,0:T(8,128)(2,1)S(1)} %shard_map.79), channel_id=1, replica_groups=mesh['member'=16,'band'=16,'rep'=2] {'member'}, dimensions={0} | all-to-all | bytes 393216 | tf_op jit(solution)/shard_map/all_to_all | solution.py:232
  36.6 0.7 shard_map.80
  37.3 7.3 %all-gather = bf16[32,112,128]{2,1,0:T(8,128)(2,1)S(1)} all-gather(bf16[16,112,128]{2,1,0:T(8,128)(2,1)S(1)} %get-tuple-element.5), channel_id=2, replica_groups=mesh['member'=16,'band'=16,'rep'=2] {'rep'}, dimensions={0}, use_global_device_ids=true | all-gather | bytes 1376256 | tf_op jit(solution)/shard_map/all_gather | solution.py:324
  44.6 1.4 %shard_map.82 = bf16[16,112,128]{2,1,0:T(8,128)(2,1)} custom-call(bf16[288,1024]{1,0:T(8,128)(2,1)S(1)} %get-tuple-element.4.spread_ref, bf16[8,512,128]{2,1,0:T(8,128)(2,1)S(1)} %bitcast.37, bf16[512,128]{1,0:T(8,128)(2,1)S(1)} %collective-permute-done.low_ref, bf16[512,128]{1,0:T(8,128)(2,1)S(1)} %collective-permute-done.1.high_ref, ...), custom_call_target="tpu_custom_call" | custom-call | flops 424673280 | bytes 1048576 | tf_op jit(solution)/shard_map/pallas_call | solution.py:319
  46.0 3.6 %all-to-all-start.2 = ((bf16[16,112,128]{2,1,0:T(8,128)(2,1)}), bf16[16,112,128]{2,1,0:T(8,128)(2,1)S(1)}, u32[]{:S(2)}, u32[]{:S(2)}) async-start(bf16[16,112,128]{2,1,0:T(8,128)(2,1)} %shard_map.82), calls=%async_computation.2 | async-start | bytes 917504 | tf_op jit(solution)/shard_map/all_to_all | solution.py:232
  49.6 1.3 %collective-permute-start.3 = (bf16[2,48,128]{2,1,0:T(8,128)(2,1)S(1)}, bf16[2,48,128]{2,1,0:T(8,128)(2,1)S(1)}, u32[]{:S(2)}, u32[]{:S(2)}) collective-permute-start(bf16[2,48,128]{2,1,0:T(8,128)(2,1)S(1)} %get-tuple-element.10), channel_id=1, source_target_pairs={{2,0},{4,2},{6,4},{8,6},{10,8},{12,10},{14,12},{16,14},{18,16},{20... | collective-permute-start | bytes 73736 | tf_op jit(solution)/shard_map/ppermute | solution.py:228
  50.9 4.7 %collective-permute-start.2 = (bf16[2,48,128]{2,1,0:T(8,128)(2,1)S(1)}, bf16[2,48,128]{2,1,0:T(8,128)(2,1)S(1)}, u32[]{:S(2)}, u32[]{:S(2)}) collective-permute-start(bf16[2,48,128]{2,1,0:T(8,128)(2,1)S(1)} %get-tuple-element.11), channel_id=1, source_target_pairs={{0,2},{2,4},{4,6},{6,8},{8,10},{10,12},{12,14},{14,16},{16,18},{18... | collective-permute-start | bytes 73736 | tf_op jit(solution)/shard_map/ppermute | solution.py:228
  55.6 4.2 %all-to-all-done.2.parts_ref = bf16[16,112,128]{2,1,0:T(8,128)(2,1)S(1)} async-done(((bf16[16,112,128]{2,1,0:T(8,128)(2,1)}), bf16[16,112,128]{2,1,0:T(8,128)(2,1)S(1)}, u32[]{:S(2)}, u32[]{:S(2)}) %all-to-all-start.2) | async-done | bytes 458784 | tf_op jit(solution)/shard_map/all_to_all | solution.py:232
  59.9 16.8 %all_gather.14.parts_ref = bf16[2,112,128]{2,1,0:T(8,128)(2,1)S(1)} all-gather(bf16[1,112,128]{2,1,0:T(8,128)(2,1)S(1)} %shard_map.83), channel_id=1, replica_groups={{0,16},{2,18},{4,20},{6,22},{8,24},{10,26},{12,28},{14,30},{1,17},{3,19..., dimensions={0}, use_global_device_ids=true | all-gather | bytes 86016 | tf_op jit(solution)/shard_map/all_gather | solution.py:346
  76.7 7.5 %all_gather.15.parts_ref = bf16[2,112,128]{2,1,0:T(8,128)(2,1)S(1)} all-gather(bf16[1,112,128]{2,1,0:T(8,128)(2,1)S(1)} %shard_map.84), channel_id=1, replica_groups={{0,8},{2,10},{4,12},{6,14},{16,24},{18,26},{20,28},{22,30},{1,9},{3,11}..., dimensions={0}, use_global_device_ids=true | all-gather | bytes 86016 | tf_op jit(solution)/shard_map/all_gather | solution.py:346
  84.8 3.3 %all-to-all-start.3 = ((bf16[4,112,128]{2,1,0:T(8,128)(2,1)}), bf16[4,112,128]{2,1,0:T(8,128)(2,1)S(1)}, u32[]{:S(2)}, u32[]{:S(2)}) async-start(bf16[4,112,128]{2,1,0:T(8,128)(2,1)} %shard_map.85), calls=%async_computation.3 | async-start | bytes 229376 | tf_op jit(solution)/shard_map/all_to_all | solution.py:232
  88.2 1.3 %shard_map.81 = bf16[8,512,128]{2,1,0:T(8,128)(2,1)S(1)} custom-call(bf16[864,512]{1,0:T(8,128)(2,1)S(1)} %bitcast.43, bf16[288,1024]{1,0:T(8,128)(2,1)S(1)} %get-tuple-element.4.spread_ref, bf16[2,48,128]{2,1,0:T(8,128)(2,1)S(1)} %collective-permute-done.2.low_ref.refs_0_, bf16[2,48,128]{2,1,0:T(8,128)(2,1)S(1)} %collective-permute-done.3.high_ref.refs_1_), custom_call_target="tpu_custom_call" | custom-call | flops 849346560 | bytes 2097152 | tf_op jit(solution)/shard_map/pallas_call | solution.py:325
  89.5 0.7 copy.19
  90.2 2.7 %all-to-all-done.3.parts_ref = bf16[4,112,128]{2,1,0:T(8,128)(2,1)S(1)} async-done(((bf16[4,112,128]{2,1,0:T(8,128)(2,1)}), bf16[4,112,128]{2,1,0:T(8,128)(2,1)S(1)}, u32[]{:S(2)}, u32[]{:S(2)}) %all-to-all-start.3) | async-done | bytes 114720 | tf_op jit(solution)/shard_map/all_to_all | solution.py:232
  92.9 11.5 %all_to_all.27.source_ref = bf16[16,112,128]{2,1,0:T(8,128)(2,1)S(1)} all-to-all(bf16[16,112,128]{2,1,0:T(8,128)(2,1)S(1)} %shard_map.86), channel_id=1, replica_groups=mesh['member'=16,'band'=16,'rep'=2] {'member'}, dimensions={0} | all-to-all | bytes 917504 | tf_op jit(solution)/shard_map/all_to_all | solution.py:232
  104.4 7.5 %collective-permute-start.4 = (bf16[16,112,128]{2,1,0:T(8,128)(2,1)S(1)}, bf16[16,112,128]{2,1,0:T(8,128)(2,1)S(1)}, u32[]{:S(2)}, u32[]{:S(2)}) collective-permute-start(bf16[16,112,128]{2,1,0:T(8,128)(2,1)S(1)} %all_to_all.27.source_ref), channel_id=1, source_target_pairs={{0,1},{1,0},{2,3},{3,2},{4,5},{5,4},{6,7},{7,6},{8,9},{9,8},{10,11... | collective-permute-start | bytes 1376264 | tf_op jit(solution)/shard_map/ppermute | solution.py:354
  111.8 1.0 shard_map.87.refs_0_
  113.3 1.0 shard_map.88
  (28 shorter events, 1.9 us)
Async XLA Ops:
  0.6 8.6 %copy-start = (f32[32,90]{1,0:T(8,128)S(1)}, f32[32,90]{1,0:T(8,128)}, u32[]{:S(2)}) copy-start(f32[32,90]{1,0:T(8,128)} %param.9) | copy-start | bytes 34564
  0.6 8.5 %copy-start.4 = (bf16[1,90,8,128]{3,2,1,0:T(8,128)(2,1)S(1)}, bf16[1,90,8,128]{3,2,1,0:T(8,128)(2,1)}, u32[]{:S(2)}) copy-start(bf16[1,90,8,128]{3,2,1,0:T(8,128)(2,1)} %param.10) | copy-start | bytes 552964
  0.7 8.6 %copy-start.3 = (bf16[3,3,512,90]{2,3,1,0:T(8,128)(2,1)S(1)}, bf16[3,3,512,90]{2,3,1,0:T(8,128)(2,1)}, u32[]{:S(2)}) copy-start(bf16[3,3,512,90]{2,3,1,0:T(8,128)(2,1)} %param.7) | copy-start | bytes 2488324
  2.1 8.5 %collective-permute-start.1 = (bf16[512,128]{1,0:T(8,128)(2,1)S(1)}, bf16[512,128]{1,0:T(8,128)(2,1)S(1)}, u32[]{:S(2)}, u32[]{:S(2)}) collective-permute-start(bf16[512,128]{1,0:T(8,128)(2,1)S(1)} %get-tuple-element.6), channel_id=1, source_target_pairs={{2,0},{4,2},{6,4},{8,6},{10,8},{12,10},{14,12},{16,14},{18,16},{20... | collective-permute-start | bytes 393224 | tf_op jit(solution)/shard_map/ppermute | solution.py:228
  3.4 7.2 %collective-permute-start = (bf16[512,128]{1,0:T(8,128)(2,1)S(1)}, bf16[512,128]{1,0:T(8,128)(2,1)S(1)}, u32[]{:S(2)}, u32[]{:S(2)}) collective-permute-start(bf16[512,128]{1,0:T(8,128)(2,1)S(1)} %get-tuple-element.7), channel_id=1, source_target_pairs={{0,2},{2,4},{4,6},{6,8},{8,10},{10,12},{12,14},{14,16},{16,18},{18... | collective-permute-start | bytes 393224 | tf_op jit(solution)/shard_map/ppermute | solution.py:228
  10.6 15.2 %copy-start.2 = (f32[8]{0:T(128)S(1)}, f32[8]{0:T(128)}, u32[]{:S(2)}) copy-start(f32[8]{0:T(128)} %param.11) | copy-start | bytes 100
  46.0 13.8 %all-to-all-start.2 = ((bf16[16,112,128]{2,1,0:T(8,128)(2,1)}), bf16[16,112,128]{2,1,0:T(8,128)(2,1)S(1)}, u32[]{:S(2)}, u32[]{:S(2)}) async-start(bf16[16,112,128]{2,1,0:T(8,128)(2,1)} %shard_map.82), calls=%async_computation.2 | async-start | bytes 917504 | tf_op jit(solution)/shard_map/all_to_all | solution.py:232
  49.6 27.1 %collective-permute-start.3 = (bf16[2,48,128]{2,1,0:T(8,128)(2,1)S(1)}, bf16[2,48,128]{2,1,0:T(8,128)(2,1)S(1)}, u32[]{:S(2)}, u32[]{:S(2)}) collective-permute-start(bf16[2,48,128]{2,1,0:T(8,128)(2,1)S(1)} %get-tuple-element.10), channel_id=1, source_target_pairs={{2,0},{4,2},{6,4},{8,6},{10,8},{12,10},{14,12},{16,14},{18,16},{20... | collective-permute-start | bytes 73736 | tf_op jit(solution)/shard_map/ppermute | solution.py:228
  50.9 25.8 %collective-permute-start.2 = (bf16[2,48,128]{2,1,0:T(8,128)(2,1)S(1)}, bf16[2,48,128]{2,1,0:T(8,128)(2,1)S(1)}, u32[]{:S(2)}, u32[]{:S(2)}) collective-permute-start(bf16[2,48,128]{2,1,0:T(8,128)(2,1)S(1)} %get-tuple-element.11), channel_id=1, source_target_pairs={{0,2},{2,4},{4,6},{6,8},{8,10},{10,12},{12,14},{14,16},{16,18},{18... | collective-permute-start | bytes 73736 | tf_op jit(solution)/shard_map/ppermute | solution.py:228
  84.8 8.0 %all-to-all-start.3 = ((bf16[4,112,128]{2,1,0:T(8,128)(2,1)}), bf16[4,112,128]{2,1,0:T(8,128)(2,1)S(1)}, u32[]{:S(2)}, u32[]{:S(2)}) async-start(bf16[4,112,128]{2,1,0:T(8,128)(2,1)} %shard_map.85), calls=%async_computation.3 | async-start | bytes 229376 | tf_op jit(solution)/shard_map/all_to_all | solution.py:232
  90.1 22.7 %copy-start.1 = (bf16[8,512,128]{2,0,1:T(8,128)(2,1)}, bf16[8,512,128]{2,0,1:T(8,128)(2,1)S(1)}, u32[]{:S(2)}) copy-start(bf16[8,512,128]{2,0,1:T(8,128)(2,1)S(1)} %copy.19) | copy-start | bytes 3145732
  104.4 8.9 %collective-permute-start.4 = (bf16[16,112,128]{2,1,0:T(8,128)(2,1)S(1)}, bf16[16,112,128]{2,1,0:T(8,128)(2,1)S(1)}, u32[]{:S(2)}, u32[]{:S(2)}) collective-permute-start(bf16[16,112,128]{2,1,0:T(8,128)(2,1)S(1)} %all_to_all.27.source_ref), channel_id=1, source_target_pairs={{0,1},{1,0},{2,3},{3,2},{4,5},{5,4},{6,7},{7,6},{8,9},{9,8},{10,11... | collective-permute-start | bytes 1376264 | tf_op jit(solution)/shard_map/ppermute | solution.py:354

commit v6 on v5

--- a/solution.py
+++ b/solution.py
@@ -60,7 +60,7 @@
         out_ref[2 * row + 1] = value[half_chans:]
 
 
-def edge_kernel(inner_ref, low_ref, high_ref, weight_ref, out_ref):
+def edge_kernel(inner_ref, high_ref, low_ref, weight_ref, out_ref):
     chunks = inner_ref.shape[0]
     for chunk in range(2, chunks - 2):
         out_ref[chunk] = inner_ref[chunk]
@@ -128,7 +128,7 @@
     return jnp.concatenate(parts, axis=0)
 
 
-def sent_kernel(delta_ref, x_ref, low_ref, high_ref, out_ref, spread_ref):
+def sent_kernel(delta_ref, x_ref, high_ref, low_ref, out_ref, spread_ref):
     pieces = []
     for row in range(x_ref.shape[0]):
         block = jnp.concatenate([delta_ref[2 * row], delta_ref[2 * row + 1]], axis=0)
@@ -145,7 +145,7 @@
         ].astype(jnp.bfloat16)
 
 
-def kept_kernel(spread_ref, x_ref, low_ref, high_ref, other_ref, out_ref):
+def kept_kernel(spread_ref, x_ref, high_ref, low_ref, other_ref, out_ref):
     side = lax.axis_index("rep")
     total = taps_product(spread_ref[...], side, x_ref, low_ref, high_ref)
     group = out_ref.shape[1]
@@ -157,7 +157,7 @@
         out_ref[block] = (own + other_ref[1 - side, block].astype(jnp.float32)).astype(jnp.bfloat16)
 
 
-def feature_grad_kernel(weight_ref, spread_ref, low_ref, high_ref, out_ref):
+def feature_grad_kernel(weight_ref, spread_ref, high_ref, low_ref, out_ref):
     rows = out_ref.shape[0]
     size = rows * lanes
     ends = []
@@ -185,23 +185,30 @@
         out_ref[copy] = value
 
 
-def finish_kernel(away, source_ref, *refs):
-    out_ref, block_ref, sem = refs[-3:]
-    chans, half = block_ref.shape[1:]
-    for part in range(2):
-        joined = jnp.concatenate(
-            [source_ref[2 * block + part] for block in range(source_ref.shape[0] // 2)], axis=0
-        ).astype(jnp.float32)
-        for tap in range(block_ref.shape[0]):
-            block_ref[tap, :, part * lanes : (part + 1) * lanes] = joined[
-                tap * padded_chans : tap * padded_chans + chans
-            ]
-    side = lax.axis_index("rep")
-    side = 1 - side if away else side
-    mine = pl.ds(pl.multiple_of(side * half, half), half)
-    copy = pltpu.make_async_copy(block_ref, out_ref.at[:, :, mine], sem)
-    copy.start()
-    copy.wait()
+def finish_kernel(source_ref, out_ref, block_ref, sems):
+    sides, chunks = source_ref.shape[:2]
+    taps, chans = block_ref.shape[1:3]
+    half = block_ref.shape[3]
+    copies = []
+    for side in range(sides):
+        for part in range(2):
+            joined = jnp.concatenate(
+                [source_ref[side, 2 * block + part] for block in range(chunks // 2)], axis=0
+            ).astype(jnp.float32)
+            for tap in range(taps):
+                block_ref[side, tap, :, part * lanes : (part + 1) * lanes] = joined[
+                    tap * padded_chans : tap * padded_chans + chans
+                ]
+        copies.append(
+            pltpu.make_async_copy(
+                block_ref.at[side],
+                out_ref.at[:, :, pl.ds(side * half, half)],
+                sems.at[side],
+            )
+        )
+        copies[-1].start()
+    for copy in copies:
+        copy.wait()
 
 
 vmem = pl.BlockSpec(memory_space=pltpu.VMEM)
@@ -241,22 +248,22 @@
     )(parts, *after)
 
 
-def placed(away, source, shape, *before):
+def placed(source, shape):
+    sides = source.shape[0]
     return pl.pallas_call(
-        functools.partial(finish_kernel, away),
+        finish_kernel,
         out_shape=jax.ShapeDtypeStruct(shape, jnp.float32),
-        in_specs=[vmem] + [anywhere] * len(before),
+        in_specs=[vmem],
         out_specs=anywhere,
         scratch_shapes=[
-            pltpu.VMEM(shape[:2] + (shape[2] // 2,), jnp.float32),
-            pltpu.SemaphoreType.DMA,
+            pltpu.VMEM((sides,) + shape[:2] + (shape[2] // sides,), jnp.float32),
+            pltpu.SemaphoreType.DMA((sides,)),
         ],
-        input_output_aliases={1: 0} if before else {},
         cost_estimate=pl.CostEstimate(
             flops=source.size, bytes_accessed=6 * source.size, transcendentals=0
         ),
         compiler_params=pltpu.CompilerParams(vmem_limit_bytes=32 * 1024 * 1024),
-    )(source, *before)
+    )(source)
 
 
 def local(features, kernel, noise_seed, noise_table, truth, area_weight):
@@ -292,7 +299,7 @@
         jax.ShapeDtypeStruct((members, half_chans, cols), f32),
         [vmem] * 4,
         cost=(4 * hidden * 3 * chans * cols, 4 * hidden * cols),
-    )(inner, x_low, x_high, weights)
+    )(inner, x_high, x_low, weights)
 
     eps_value = (1.0 - alpha_level) / members
     coef = (1.0 - eps_value) / (members - 1)
@@ -314,20 +321,19 @@
         [piece, jax.ShapeDtypeStruct((taps_chans, rows * cols), bf16)],
         [vmem] * 4,
         cost=(flops, 2 * hidden * rows * cols),
-    )(delta, x_rows, x_low, x_high)
-    swap = [(0, 1), (1, 0)]
+    )(delta, x_rows, x_high, x_low)
     part = call(
         kept_kernel,
         piece,
         [vmem] * 5,
         cost=(flops, 2 * hidden * rows * cols),
-    )(wide_delta, x_rows, x_low, x_high, lax.all_gather(sent, "rep", axis=0))
+    )(wide_delta, x_rows, x_high, x_low, lax.all_gather(sent, "rep", axis=0))
     grad_rows = call(
         feature_grad_kernel,
         jax.ShapeDtypeStruct((rows, hidden, cols), bf16),
         [vmem] * 4,
         cost=(2 * hidden * 9 * chans * rows * cols, 4 * hidden * rows * cols),
-    )(weights, wide_delta, d_low, d_high)
+    )(weights, wide_delta, d_high, d_low)
     feature_grad = jnp.transpose(grad_rows, (1, 0, 2))[None, None]
 
     bands = lax.axis_size("band")
@@ -346,14 +352,12 @@
         return lax.all_gather(part[0], "band", axis=0, axis_index_groups=pairs(distance))
 
     part = summed(exchange(part, "member"), 1)
-    part = summed(paired(part, 8), 1, after=(d_low, d_high))
+    part = summed(paired(part, 8), 1, after=(d_high, d_low))
     part = summed(paired(part, 4), near)
     scale = 1.0 / math.sqrt(lax.axis_size("rep") * members * bands * rows * cols)
     part = summed(exchange(part, "band", nearby), members, scale, after=(feature_grad,))
     part = exchange(part, "member")
-    other = lax.ppermute(part, "rep", swap)
-    kernel_grad = placed(False, part, (9, chans, hidden))
-    kernel_grad = placed(True, other, (9, chans, hidden), kernel_grad)
+    kernel_grad = placed(lax.all_gather(part, "rep", axis=0), (9, chans, hidden))
     kernel_grad = jnp.transpose(kernel_grad.reshape(3, 3, chans, hidden), (0, 1, 3, 2))
     return (feature_grad, kernel_grad)
 

time: 115 us -> 114 us (level)
  blocking collectives: 67.8 us -> 75.4 us
  starting transfers between devices: 26.6 us -> 19.2 us
    all_gather x0 -> x1, blocking collectives: none -> 7.64 us  [local(): lax.all_gather(part, 'rep', axis=0)]
    ppermute x1 -> x0, starting transfers between devices: 7.46 us -> none  [local(): other = lax.ppermute(part, 'rep', swap)]
  transfers between devices with their start and end apart: 7 -> 6, of which waited for: 3 -> 2; matrix products, arithmetic and copies ran while one was open for 1% -> 1% of each run, Pallas kernels for 3% -> 2%
where the time goes in v6:
time: 114 us; the launch traced here: 113 us
  blocking collectives  75.4 us (66%)
  starting transfers between devices  19.2 us (17%)
  Pallas kernels  7.81 us (7%)
  waiting for transfers between devices  6.95 us (6%)
  local copies, waits for them, and re-layouts  2.39 us (2%)
  between operations  1.57 us (1%)
    all_to_all x3, blocking collectives, exchange(): lax.all_to_all(block, axis, 0, 0, axis_index_groups=groups, tiled=True)  36.2 us
    all_gather x2, blocking collectives, paired(): lax.all_gather(part[0], 'band', axis=0, axis_index_groups=pairs(distance))  24.2 us
    ppermute x2, starting transfers between devices, neighbours(): lax.ppermute(high_edge, 'band', forward)  9.69 us
    all_gather x1, blocking collectives, local(): lax.all_gather(part, 'rep', axis=0)  7.64 us
    all_gather x1, blocking collectives, local(): lax.all_gather(sent, 'rep', axis=0)  7.32 us
    all_to_all x2, waiting for transfers between devices, exchange(): lax.all_to_all(block, axis, 0, 0, axis_index_groups=groups, tiled=True)  6.94 us
    all_to_all x2, starting transfers between devices, exchange(): lax.all_to_all(block, axis, 0, 0, axis_index_groups=groups, tiled=True)  6.88 us
    ppermute x2, starting transfers between devices, neighbours(): lax.ppermute(low_edge, 'band', backward)  2.58 us
  transfers between devices with their start and end apart: 6, of which 2 were waited for; matrix products, arithmetic and copies ran while one was open for 1% of the time, Pallas kernels for 2%

profile of v6, /device:TPU:1, one launch (start us, length us, event | category | flops | bytes accessed | tf_op | source)
XLA Modules:
  0.0 113.3 jit_solution(14338293864426396387)
XLA Ops:
  0.7 1.5 %copy.19 = bf16[1,1,512,8,128]{4,2,3,1,0:T(8,128)(2,1)S(1)} copy(bf16[1,1,512,8,128]{4,3,2,1,0:T(8,128)(2,1)} %param.6) | data formatting | bytes 2097152 | tf_op args[0]
  2.1 1.3 %collective-permute-start = (bf16[512,128]{1,0:T(8,128)(2,1)S(1)}, bf16[512,128]{1,0:T(8,128)(2,1)S(1)}, u32[]{:S(2)}, u32[]{:S(2)}) collective-permute-start(bf16[512,128]{1,0:T(8,128)(2,1)S(1)} %get-tuple-element.7), channel_id=1, source_target_pairs={{2,0},{4,2},{6,4},{8,6},{10,8},{12,10},{14,12},{16,14},{18,16},{20... | collective-permute-start | bytes 393224 | tf_op jit(solution)/shard_map/ppermute | solution.py:235
  3.4 5.0 %collective-permute-start.1 = (bf16[512,128]{1,0:T(8,128)(2,1)S(1)}, bf16[512,128]{1,0:T(8,128)(2,1)S(1)}, u32[]{:S(2)}, u32[]{:S(2)}) collective-permute-start(bf16[512,128]{1,0:T(8,128)(2,1)S(1)} %get-tuple-element.6), channel_id=1, source_target_pairs={{0,2},{2,4},{4,6},{6,8},{8,10},{10,12},{12,14},{14,16},{16,18},{18... | collective-permute-start | bytes 393224 | tf_op jit(solution)/shard_map/ppermute | solution.py:235
  9.4 1.2 %shard_map.77.inner_ref = f32[16,48,128]{2,1,0:T(8,128)S(1)} custom-call(bf16[8,512,128]{2,1,0:T(8,128)(2,1)S(1)} %bitcast.36, bf16[864,512]{1,0:T(8,128)(2,1)S(1)} %bitcast.43, f32[96,128]{1,0:T(8,128)S(1)} %broadcast_in_dim.12.offset_ref, f32[48,128]{1,0:T(8,128)S(1)} %bitcast_convert_fusion.truth_ref), custom_call_target="tpu_custom_call" | custom-call | flops 849346560 | bytes 2097152 | tf_op jit(solution)/shard_map/pallas_call | solution.py:291
  11.1 14.8 %all_to_all.25.values_ref = f32[16,48,128]{2,1,0:T(8,128)S(1)} all-to-all(f32[16,48,128]{2,1,0:T(8,128)S(1)} %shard_map.78), channel_id=1, replica_groups=mesh['member'=16,'band'=16,'rep'=2] {'member'}, dimensions={0} | all-to-all | bytes 786432 | tf_op jit(solution)/shard_map/all_to_all | solution.py:239
  25.9 0.8 shard_map.79
  26.7 9.9 %all_to_all.26.delta_ref = bf16[16,48,128]{2,1,0:T(8,128)(2,1)S(1)} all-to-all(bf16[16,48,128]{2,1,0:T(8,128)(2,1)S(1)} %shard_map.79), channel_id=1, replica_groups=mesh['member'=16,'band'=16,'rep'=2] {'member'}, dimensions={0} | all-to-all | bytes 393216 | tf_op jit(solution)/shard_map/all_to_all | solution.py:239
  36.6 0.7 shard_map.80
  37.3 7.3 %all-gather = bf16[32,112,128]{2,1,0:T(8,128)(2,1)S(1)} all-gather(bf16[16,112,128]{2,1,0:T(8,128)(2,1)S(1)} %get-tuple-element.5), channel_id=2, replica_groups=mesh['member'=16,'band'=16,'rep'=2] {'rep'}, dimensions={0}, use_global_device_ids=true | all-gather | bytes 1376256 | tf_op jit(solution)/shard_map/all_gather | solution.py:330
  44.6 1.4 %shard_map.82 = bf16[16,112,128]{2,1,0:T(8,128)(2,1)} custom-call(bf16[288,1024]{1,0:T(8,128)(2,1)S(1)} %get-tuple-element.4.spread_ref, bf16[8,512,128]{2,1,0:T(8,128)(2,1)S(1)} %bitcast.38, bf16[512,128]{1,0:T(8,128)(2,1)S(1)} %collective-permute-done.high_ref, bf16[512,128]{1,0:T(8,128)(2,1)S(1)} %collective-permute-done.1.low_ref, ...), custom_call_target="tpu_custom_call" | custom-call | flops 424673280 | bytes 1048576 | tf_op jit(solution)/shard_map/pallas_call | solution.py:325
  46.0 3.6 %all-to-all-start.2 = ((bf16[16,112,128]{2,1,0:T(8,128)(2,1)}), bf16[16,112,128]{2,1,0:T(8,128)(2,1)S(1)}, u32[]{:S(2)}, u32[]{:S(2)}) async-start(bf16[16,112,128]{2,1,0:T(8,128)(2,1)} %shard_map.82), calls=%async_computation.2 | async-start | bytes 917504 | tf_op jit(solution)/shard_map/all_to_all | solution.py:239
  49.6 1.3 %collective-permute-start.2 = (bf16[2,48,128]{2,1,0:T(8,128)(2,1)S(1)}, bf16[2,48,128]{2,1,0:T(8,128)(2,1)S(1)}, u32[]{:S(2)}, u32[]{:S(2)}) collective-permute-start(bf16[2,48,128]{2,1,0:T(8,128)(2,1)S(1)} %get-tuple-element.11), channel_id=1, source_target_pairs={{2,0},{4,2},{6,4},{8,6},{10,8},{12,10},{14,12},{16,14},{18,16},{20... | collective-permute-start | bytes 73736 | tf_op jit(solution)/shard_map/ppermute | solution.py:235
  50.9 4.7 %collective-permute-start.3 = (bf16[2,48,128]{2,1,0:T(8,128)(2,1)S(1)}, bf16[2,48,128]{2,1,0:T(8,128)(2,1)S(1)}, u32[]{:S(2)}, u32[]{:S(2)}) collective-permute-start(bf16[2,48,128]{2,1,0:T(8,128)(2,1)S(1)} %get-tuple-element.10), channel_id=1, source_target_pairs={{0,2},{2,4},{4,6},{6,8},{8,10},{10,12},{12,14},{14,16},{16,18},{18... | collective-permute-start | bytes 73736 | tf_op jit(solution)/shard_map/ppermute | solution.py:235
  55.6 4.2 %all-to-all-done.2.parts_ref = bf16[16,112,128]{2,1,0:T(8,128)(2,1)S(1)} async-done(((bf16[16,112,128]{2,1,0:T(8,128)(2,1)}), bf16[16,112,128]{2,1,0:T(8,128)(2,1)S(1)}, u32[]{:S(2)}, u32[]{:S(2)}) %all-to-all-start.2) | async-done | bytes 458784 | tf_op jit(solution)/shard_map/all_to_all | solution.py:239
  59.9 16.7 %all_gather.20.parts_ref = bf16[2,112,128]{2,1,0:T(8,128)(2,1)S(1)} all-gather(bf16[1,112,128]{2,1,0:T(8,128)(2,1)S(1)} %shard_map.83), channel_id=1, replica_groups={{0,16},{2,18},{4,20},{6,22},{8,24},{10,26},{12,28},{14,30},{1,17},{3,19..., dimensions={0}, use_global_device_ids=true | all-gather | bytes 86016 | tf_op jit(solution)/shard_map/all_gather | solution.py:352
  76.7 7.5 %all_gather.21.parts_ref = bf16[2,112,128]{2,1,0:T(8,128)(2,1)S(1)} all-gather(bf16[1,112,128]{2,1,0:T(8,128)(2,1)S(1)} %shard_map.84), channel_id=1, replica_groups={{0,8},{2,10},{4,12},{6,14},{16,24},{18,26},{20,28},{22,30},{1,9},{3,11}..., dimensions={0}, use_global_device_ids=true | all-gather | bytes 86016 | tf_op jit(solution)/shard_map/all_gather | solution.py:352
  84.2 0.7 shard_map.85
  84.8 3.3 %all-to-all-start.3 = ((bf16[4,112,128]{2,1,0:T(8,128)(2,1)}), bf16[4,112,128]{2,1,0:T(8,128)(2,1)S(1)}, u32[]{:S(2)}, u32[]{:S(2)}) async-start(bf16[4,112,128]{2,1,0:T(8,128)(2,1)} %shard_map.85), calls=%async_computation.3 | async-start | bytes 229376 | tf_op jit(solution)/shard_map/all_to_all | solution.py:239
  88.2 1.3 %shard_map.81 = bf16[8,512,128]{2,1,0:T(8,128)(2,1)S(1)} custom-call(bf16[864,512]{1,0:T(8,128)(2,1)S(1)} %bitcast.45, bf16[288,1024]{1,0:T(8,128)(2,1)S(1)} %get-tuple-element.4.spread_ref, bf16[2,48,128]{2,1,0:T(8,128)(2,1)S(1)} %collective-permute-done.2.high_ref.refs_0_, bf16[2,48,128]{2,1,0:T(8,128)(2,1)S(1)} %collective-permute-done.3.low_ref.refs_1_), custom_call_target="tpu_custom_call" | custom-call | flops 849346560 | bytes 2097152 | tf_op jit(solution)/shard_map/pallas_call | solution.py:331
  89.5 0.7 copy.18
  90.2 2.7 %all-to-all-done.3.parts_ref = bf16[4,112,128]{2,1,0:T(8,128)(2,1)S(1)} async-done(((bf16[4,112,128]{2,1,0:T(8,128)(2,1)}), bf16[4,112,128]{2,1,0:T(8,128)(2,1)S(1)}, u32[]{:S(2)}, u32[]{:S(2)}) %all-to-all-start.3) | async-done | bytes 114720 | tf_op jit(solution)/shard_map/all_to_all | solution.py:239
  92.9 11.5 %all_to_all.27 = bf16[16,112,128]{2,1,0:T(8,128)(2,1)S(1)} all-to-all(bf16[16,112,128]{2,1,0:T(8,128)(2,1)S(1)} %shard_map.86), channel_id=1, replica_groups=mesh['member'=16,'band'=16,'rep'=2] {'member'}, dimensions={0} | all-to-all | bytes 917504 | tf_op jit(solution)/shard_map/all_to_all | solution.py:239
  104.4 7.6 %all-gather.1 = bf16[32,112,128]{2,1,0:T(8,128)(2,1)S(1)} all-gather(bf16[16,112,128]{2,1,0:T(8,128)(2,1)S(1)} %all_to_all.27), channel_id=3, replica_groups=mesh['member'=16,'band'=16,'rep'=2] {'rep'}, dimensions={0}, use_global_device_ids=true | all-gather | bytes 1376256 | tf_op jit(solution)/shard_map/all_gather | solution.py:360
  112.0 1.3 %shard_map.87 = f32[9,90,512]{2,1,0:T(8,128)} custom-call(bf16[2,16,112,128]{3,2,1,0:T(8,128)(2,1)S(1)} %bitcast.42), custom_call_target="tpu_custom_call" | custom-call | flops 458752 | bytes 2752512 | tf_op jit(solution)/shard_map/pallas_call | solution.py:253
  (26 shorter events, 0.8 us)
Async XLA Ops:
  0.6 8.6 %copy-start = (f32[32,90]{1,0:T(8,128)S(1)}, f32[32,90]{1,0:T(8,128)}, u32[]{:S(2)}) copy-start(f32[32,90]{1,0:T(8,128)} %param.9) | copy-start | bytes 34564
  0.6 7.8 %copy-start.4 = (bf16[1,90,8,128]{3,2,1,0:T(8,128)(2,1)S(1)}, bf16[1,90,8,128]{3,2,1,0:T(8,128)(2,1)}, u32[]{:S(2)}) copy-start(bf16[1,90,8,128]{3,2,1,0:T(8,128)(2,1)} %param.10) | copy-start | bytes 552964
  0.7 8.6 %copy-start.3 = (bf16[3,3,512,90]{2,3,1,0:T(8,128)(2,1)S(1)}, bf16[3,3,512,90]{2,3,1,0:T(8,128)(2,1)}, u32[]{:S(2)}) copy-start(bf16[3,3,512,90]{2,3,1,0:T(8,128)(2,1)} %param.7) | copy-start | bytes 2488324
  2.1 8.5 %collective-permute-start = (bf16[512,128]{1,0:T(8,128)(2,1)S(1)}, bf16[512,128]{1,0:T(8,128)(2,1)S(1)}, u32[]{:S(2)}, u32[]{:S(2)}) collective-permute-start(bf16[512,128]{1,0:T(8,128)(2,1)S(1)} %get-tuple-element.7), channel_id=1, source_target_pairs={{2,0},{4,2},{6,4},{8,6},{10,8},{12,10},{14,12},{16,14},{18,16},{20... | collective-permute-start | bytes 393224 | tf_op jit(solution)/shard_map/ppermute | solution.py:235
  3.4 7.2 %collective-permute-start.1 = (bf16[512,128]{1,0:T(8,128)(2,1)S(1)}, bf16[512,128]{1,0:T(8,128)(2,1)S(1)}, u32[]{:S(2)}, u32[]{:S(2)}) collective-permute-start(bf16[512,128]{1,0:T(8,128)(2,1)S(1)} %get-tuple-element.6), channel_id=1, source_target_pairs={{0,2},{2,4},{4,6},{6,8},{8,10},{10,12},{12,14},{14,16},{16,18},{18... | collective-permute-start | bytes 393224 | tf_op jit(solution)/shard_map/ppermute | solution.py:235
  10.6 15.2 %copy-start.2 = (f32[8]{0:T(128)S(1)}, f32[8]{0:T(128)}, u32[]{:S(2)}) copy-start(f32[8]{0:T(128)} %param.11) | copy-start | bytes 100
  46.0 13.8 %all-to-all-start.2 = ((bf16[16,112,128]{2,1,0:T(8,128)(2,1)}), bf16[16,112,128]{2,1,0:T(8,128)(2,1)S(1)}, u32[]{:S(2)}, u32[]{:S(2)}) async-start(bf16[16,112,128]{2,1,0:T(8,128)(2,1)} %shard_map.82), calls=%async_computation.2 | async-start | bytes 917504 | tf_op jit(solution)/shard_map/all_to_all | solution.py:239
  49.6 27.0 %collective-permute-start.2 = (bf16[2,48,128]{2,1,0:T(8,128)(2,1)S(1)}, bf16[2,48,128]{2,1,0:T(8,128)(2,1)S(1)}, u32[]{:S(2)}, u32[]{:S(2)}) collective-permute-start(bf16[2,48,128]{2,1,0:T(8,128)(2,1)S(1)} %get-tuple-element.11), channel_id=1, source_target_pairs={{2,0},{4,2},{6,4},{8,6},{10,8},{12,10},{14,12},{16,14},{18,16},{20... | collective-permute-start | bytes 73736 | tf_op jit(solution)/shard_map/ppermute | solution.py:235
  50.9 25.7 %collective-permute-start.3 = (bf16[2,48,128]{2,1,0:T(8,128)(2,1)S(1)}, bf16[2,48,128]{2,1,0:T(8,128)(2,1)S(1)}, u32[]{:S(2)}, u32[]{:S(2)}) collective-permute-start(bf16[2,48,128]{2,1,0:T(8,128)(2,1)S(1)} %get-tuple-element.10), channel_id=1, source_target_pairs={{0,2},{2,4},{4,6},{6,8},{8,10},{10,12},{12,14},{14,16},{16,18},{18... | collective-permute-start | bytes 73736 | tf_op jit(solution)/shard_map/ppermute | solution.py:235
  84.8 8.0 %all-to-all-start.3 = ((bf16[4,112,128]{2,1,0:T(8,128)(2,1)}), bf16[4,112,128]{2,1,0:T(8,128)(2,1)S(1)}, u32[]{:S(2)}, u32[]{:S(2)}) async-start(bf16[4,112,128]{2,1,0:T(8,128)(2,1)} %shard_map.85), calls=%async_computation.3 | async-start | bytes 229376 | tf_op jit(solution)/shard_map/all_to_all | solution.py:239
  90.1 21.9 %copy-start.1 = (bf16[8,512,128]{2,0,1:T(8,128)(2,1)}, bf16[8,512,128]{2,0,1:T(8,128)(2,1)S(1)}, u32[]{:S(2)}) copy-start(bf16[8,512,128]{2,0,1:T(8,128)(2,1)S(1)} %copy.18) | copy-start | bytes 3145732

commit v7 on v6

--- a/solution.py
+++ b/solution.py
@@ -352,8 +352,8 @@
         return lax.all_gather(part[0], "band", axis=0, axis_index_groups=pairs(distance))
 
     part = summed(exchange(part, "member"), 1)
-    part = summed(paired(part, 8), 1, after=(d_high, d_low))
-    part = summed(paired(part, 4), near)
+    part = summed(paired(part, 4), 1, after=(d_high, d_low))
+    part = summed(paired(part, 8), near)
     scale = 1.0 / math.sqrt(lax.axis_size("rep") * members * bands * rows * cols)
     part = summed(exchange(part, "band", nearby), members, scale, after=(feature_grad,))
     part = exchange(part, "member")

time: 114 us -> 114 us (level)
  no operation moved by 1% of the time
where the time goes in v7:
time: 114 us; the launch traced here: 113 us
  blocking collectives  75.6 us (66%)
  starting transfers between devices  19.2 us (17%)
  Pallas kernels  7.8 us (7%)
  waiting for transfers between devices  6.96 us (6%)
  local copies, waits for them, and re-layouts  2.39 us (2%)
  between operations  1.57 us (1%)
    all_to_all x3, blocking collectives, exchange(): lax.all_to_all(block, axis, 0, 0, axis_index_groups=groups, tiled=True)  36.8 us
    all_gather x2, blocking collectives, paired(): lax.all_gather(part[0], 'band', axis=0, axis_index_groups=pairs(distance))  24.4 us
    ppermute x2, starting transfers between devices, neighbours(): lax.ppermute(high_edge, 'band', forward)  9.69 us
    all_gather x1, blocking collectives, local(): lax.all_gather(sent, 'rep', axis=0)  7.32 us
    all_gather x1, blocking collectives, local(): lax.all_gather(part, 'rep', axis=0)  7.02 us
    all_to_all x2, waiting for transfers between devices, exchange(): lax.all_to_all(block, axis, 0, 0, axis_index_groups=groups, tiled=True)  6.95 us
    all_to_all x2, starting transfers between devices, exchange(): lax.all_to_all(block, axis, 0, 0, axis_index_groups=groups, tiled=True)  6.88 us
    ppermute x2, starting transfers between devices, neighbours(): lax.ppermute(low_edge, 'band', backward)  2.58 us
  transfers between devices with their start and end apart: 6, of which 2 were waited for; matrix products, arithmetic and copies ran while one was open for 1% of the time, Pallas kernels for 2%

profile of v7, /device:TPU:1, one launch (start us, length us, event | category | flops | bytes accessed | tf_op | source)
XLA Modules:
  0.0 113.5 jit_solution(2846774874460647277)
XLA Ops:
  0.7 1.5 %copy.19 = bf16[1,1,512,8,128]{4,2,3,1,0:T(8,128)(2,1)S(1)} copy(bf16[1,1,512,8,128]{4,3,2,1,0:T(8,128)(2,1)} %param.6) | data formatting | bytes 2097152 | tf_op args[0]
  2.1 1.3 %collective-permute-start = (bf16[512,128]{1,0:T(8,128)(2,1)S(1)}, bf16[512,128]{1,0:T(8,128)(2,1)S(1)}, u32[]{:S(2)}, u32[]{:S(2)}) collective-permute-start(bf16[512,128]{1,0:T(8,128)(2,1)S(1)} %get-tuple-element.7), channel_id=1, source_target_pairs={{2,0},{4,2},{6,4},{8,6},{10,8},{12,10},{14,12},{16,14},{18,16},{20... | collective-permute-start | bytes 393224 | tf_op jit(solution)/shard_map/ppermute | solution.py:235
  3.4 5.0 %collective-permute-start.1 = (bf16[512,128]{1,0:T(8,128)(2,1)S(1)}, bf16[512,128]{1,0:T(8,128)(2,1)S(1)}, u32[]{:S(2)}, u32[]{:S(2)}) collective-permute-start(bf16[512,128]{1,0:T(8,128)(2,1)S(1)} %get-tuple-element.6), channel_id=1, source_target_pairs={{0,2},{2,4},{4,6},{6,8},{8,10},{10,12},{12,14},{14,16},{16,18},{18... | collective-permute-start | bytes 393224 | tf_op jit(solution)/shard_map/ppermute | solution.py:235
  9.4 1.2 %shard_map.77.inner_ref = f32[16,48,128]{2,1,0:T(8,128)S(1)} custom-call(bf16[8,512,128]{2,1,0:T(8,128)(2,1)S(1)} %bitcast.36, bf16[864,512]{1,0:T(8,128)(2,1)S(1)} %bitcast.43, f32[96,128]{1,0:T(8,128)S(1)} %broadcast_in_dim.12.offset_ref, f32[48,128]{1,0:T(8,128)S(1)} %bitcast_convert_fusion.truth_ref), custom_call_target="tpu_custom_call" | custom-call | flops 849346560 | bytes 2097152 | tf_op jit(solution)/shard_map/pallas_call | solution.py:291
  11.1 14.8 %all_to_all.25.values_ref = f32[16,48,128]{2,1,0:T(8,128)S(1)} all-to-all(f32[16,48,128]{2,1,0:T(8,128)S(1)} %shard_map.78), channel_id=1, replica_groups=mesh['member'=16,'band'=16,'rep'=2] {'member'}, dimensions={0} | all-to-all | bytes 786432 | tf_op jit(solution)/shard_map/all_to_all | solution.py:239
  25.9 0.8 shard_map.79
  26.7 9.9 %all_to_all.26.delta_ref = bf16[16,48,128]{2,1,0:T(8,128)(2,1)S(1)} all-to-all(bf16[16,48,128]{2,1,0:T(8,128)(2,1)S(1)} %shard_map.79), channel_id=1, replica_groups=mesh['member'=16,'band'=16,'rep'=2] {'member'}, dimensions={0} | all-to-all | bytes 393216 | tf_op jit(solution)/shard_map/all_to_all | solution.py:239
  36.6 0.7 shard_map.80
  37.3 7.3 %all-gather = bf16[32,112,128]{2,1,0:T(8,128)(2,1)S(1)} all-gather(bf16[16,112,128]{2,1,0:T(8,128)(2,1)S(1)} %get-tuple-element.5), channel_id=2, replica_groups=mesh['member'=16,'band'=16,'rep'=2] {'rep'}, dimensions={0}, use_global_device_ids=true | all-gather | bytes 1376256 | tf_op jit(solution)/shard_map/all_gather | solution.py:330
  44.6 1.4 %shard_map.82 = bf16[16,112,128]{2,1,0:T(8,128)(2,1)} custom-call(bf16[288,1024]{1,0:T(8,128)(2,1)S(1)} %get-tuple-element.4.spread_ref, bf16[8,512,128]{2,1,0:T(8,128)(2,1)S(1)} %bitcast.38, bf16[512,128]{1,0:T(8,128)(2,1)S(1)} %collective-permute-done.high_ref, bf16[512,128]{1,0:T(8,128)(2,1)S(1)} %collective-permute-done.1.low_ref, ...), custom_call_target="tpu_custom_call" | custom-call | flops 424673280 | bytes 1048576 | tf_op jit(solution)/shard_map/pallas_call | solution.py:325
  46.0 3.6 %all-to-all-start.2 = ((bf16[16,112,128]{2,1,0:T(8,128)(2,1)}), bf16[16,112,128]{2,1,0:T(8,128)(2,1)S(1)}, u32[]{:S(2)}, u32[]{:S(2)}) async-start(bf16[16,112,128]{2,1,0:T(8,128)(2,1)} %shard_map.82), calls=%async_computation.2 | async-start | bytes 917504 | tf_op jit(solution)/shard_map/all_to_all | solution.py:239
  49.6 1.3 %collective-permute-start.2 = (bf16[2,48,128]{2,1,0:T(8,128)(2,1)S(1)}, bf16[2,48,128]{2,1,0:T(8,128)(2,1)S(1)}, u32[]{:S(2)}, u32[]{:S(2)}) collective-permute-start(bf16[2,48,128]{2,1,0:T(8,128)(2,1)S(1)} %get-tuple-element.11), channel_id=1, source_target_pairs={{2,0},{4,2},{6,4},{8,6},{10,8},{12,10},{14,12},{16,14},{18,16},{20... | collective-permute-start | bytes 73736 | tf_op jit(solution)/shard_map/ppermute | solution.py:235
  50.9 4.7 %collective-permute-start.3 = (bf16[2,48,128]{2,1,0:T(8,128)(2,1)S(1)}, bf16[2,48,128]{2,1,0:T(8,128)(2,1)S(1)}, u32[]{:S(2)}, u32[]{:S(2)}) collective-permute-start(bf16[2,48,128]{2,1,0:T(8,128)(2,1)S(1)} %get-tuple-element.10), channel_id=1, source_target_pairs={{0,2},{2,4},{4,6},{6,8},{8,10},{10,12},{12,14},{14,16},{16,18},{18... | collective-permute-start | bytes 73736 | tf_op jit(solution)/shard_map/ppermute | solution.py:235
  55.6 4.2 %all-to-all-done.2.parts_ref = bf16[16,112,128]{2,1,0:T(8,128)(2,1)S(1)} async-done(((bf16[16,112,128]{2,1,0:T(8,128)(2,1)}), bf16[16,112,128]{2,1,0:T(8,128)(2,1)S(1)}, u32[]{:S(2)}, u32[]{:S(2)}) %all-to-all-start.2) | async-done | bytes 458784 | tf_op jit(solution)/shard_map/all_to_all | solution.py:239
  59.9 9.9 %all_gather.20.parts_ref = bf16[2,112,128]{2,1,0:T(8,128)(2,1)S(1)} all-gather(bf16[1,112,128]{2,1,0:T(8,128)(2,1)S(1)} %shard_map.83), channel_id=1, replica_groups={{0,8},{2,10},{4,12},{6,14},{16,24},{18,26},{20,28},{22,30},{1,9},{3,11}..., dimensions={0}, use_global_device_ids=true | all-gather | bytes 86016 | tf_op jit(solution)/shard_map/all_gather | solution.py:352
  69.8 14.5 %all_gather.21.parts_ref = bf16[2,112,128]{2,1,0:T(8,128)(2,1)S(1)} all-gather(bf16[1,112,128]{2,1,0:T(8,128)(2,1)S(1)} %shard_map.84), channel_id=1, replica_groups={{0,16},{2,18},{4,20},{6,22},{8,24},{10,26},{12,28},{14,30},{1,17},{3,19..., dimensions={0}, use_global_device_ids=true | all-gather | bytes 86016 | tf_op jit(solution)/shard_map/all_gather | solution.py:352
  84.4 0.7 shard_map.85
  85.0 3.3 %all-to-all-start.3 = ((bf16[4,112,128]{2,1,0:T(8,128)(2,1)}), bf16[4,112,128]{2,1,0:T(8,128)(2,1)S(1)}, u32[]{:S(2)}, u32[]{:S(2)}) async-start(bf16[4,112,128]{2,1,0:T(8,128)(2,1)} %shard_map.85), calls=%async_computation.3 | async-start | bytes 229376 | tf_op jit(solution)/shard_map/all_to_all | solution.py:239
  88.3 1.3 %shard_map.81 = bf16[8,512,128]{2,1,0:T(8,128)(2,1)S(1)} custom-call(bf16[864,512]{1,0:T(8,128)(2,1)S(1)} %bitcast.45, bf16[288,1024]{1,0:T(8,128)(2,1)S(1)} %get-tuple-element.4.spread_ref, bf16[2,48,128]{2,1,0:T(8,128)(2,1)S(1)} %collective-permute-done.2.high_ref.refs_0_, bf16[2,48,128]{2,1,0:T(8,128)(2,1)S(1)} %collective-permute-done.3.low_ref.refs_1_), custom_call_target="tpu_custom_call" | custom-call | flops 849346560 | bytes 2097152 | tf_op jit(solution)/shard_map/pallas_call | solution.py:331
  89.6 0.7 copy.18
  90.3 2.7 %all-to-all-done.3.parts_ref = bf16[4,112,128]{2,1,0:T(8,128)(2,1)S(1)} async-done(((bf16[4,112,128]{2,1,0:T(8,128)(2,1)}), bf16[4,112,128]{2,1,0:T(8,128)(2,1)S(1)}, u32[]{:S(2)}, u32[]{:S(2)}) %all-to-all-start.3) | async-done | bytes 114720 | tf_op jit(solution)/shard_map/all_to_all | solution.py:239
  93.1 12.1 %all_to_all.27 = bf16[16,112,128]{2,1,0:T(8,128)(2,1)S(1)} all-to-all(bf16[16,112,128]{2,1,0:T(8,128)(2,1)S(1)} %shard_map.86), channel_id=1, replica_groups=mesh['member'=16,'band'=16,'rep'=2] {'member'}, dimensions={0} | all-to-all | bytes 917504 | tf_op jit(solution)/shard_map/all_to_all | solution.py:239
  105.2 7.0 %all-gather.1 = bf16[32,112,128]{2,1,0:T(8,128)(2,1)S(1)} all-gather(bf16[16,112,128]{2,1,0:T(8,128)(2,1)S(1)} %all_to_all.27), channel_id=3, replica_groups=mesh['member'=16,'band'=16,'rep'=2] {'rep'}, dimensions={0}, use_global_device_ids=true | all-gather | bytes 1376256 | tf_op jit(solution)/shard_map/all_gather | solution.py:360
  112.2 1.3 %shard_map.87 = f32[9,90,512]{2,1,0:T(8,128)} custom-call(bf16[2,16,112,128]{3,2,1,0:T(8,128)(2,1)S(1)} %bitcast.42), custom_call_target="tpu_custom_call" | custom-call | flops 458752 | bytes 2752512 | tf_op jit(solution)/shard_map/pallas_call | solution.py:253
  (26 shorter events, 0.8 us)
Async XLA Ops:
  0.6 8.6 %copy-start = (f32[32,90]{1,0:T(8,128)S(1)}, f32[32,90]{1,0:T(8,128)}, u32[]{:S(2)}) copy-start(f32[32,90]{1,0:T(8,128)} %param.9) | copy-start | bytes 34564
  0.6 7.8 %copy-start.4 = (bf16[1,90,8,128]{3,2,1,0:T(8,128)(2,1)S(1)}, bf16[1,90,8,128]{3,2,1,0:T(8,128)(2,1)}, u32[]{:S(2)}) copy-start(bf16[1,90,8,128]{3,2,1,0:T(8,128)(2,1)} %param.10) | copy-start | bytes 552964
  0.7 8.6 %copy-start.3 = (bf16[3,3,512,90]{2,3,1,0:T(8,128)(2,1)S(1)}, bf16[3,3,512,90]{2,3,1,0:T(8,128)(2,1)}, u32[]{:S(2)}) copy-start(bf16[3,3,512,90]{2,3,1,0:T(8,128)(2,1)} %param.7) | copy-start | bytes 2488324
  2.1 8.5 %collective-permute-start = (bf16[512,128]{1,0:T(8,128)(2,1)S(1)}, bf16[512,128]{1,0:T(8,128)(2,1)S(1)}, u32[]{:S(2)}, u32[]{:S(2)}) collective-permute-start(bf16[512,128]{1,0:T(8,128)(2,1)S(1)} %get-tuple-element.7), channel_id=1, source_target_pairs={{2,0},{4,2},{6,4},{8,6},{10,8},{12,10},{14,12},{16,14},{18,16},{20... | collective-permute-start | bytes 393224 | tf_op jit(solution)/shard_map/ppermute | solution.py:235
  3.4 7.2 %collective-permute-start.1 = (bf16[512,128]{1,0:T(8,128)(2,1)S(1)}, bf16[512,128]{1,0:T(8,128)(2,1)S(1)}, u32[]{:S(2)}, u32[]{:S(2)}) collective-permute-start(bf16[512,128]{1,0:T(8,128)(2,1)S(1)} %get-tuple-element.6), channel_id=1, source_target_pairs={{0,2},{2,4},{4,6},{6,8},{8,10},{10,12},{12,14},{14,16},{16,18},{18... | collective-permute-start | bytes 393224 | tf_op jit(solution)/shard_map/ppermute | solution.py:235
  10.6 15.2 %copy-start.2 = (f32[8]{0:T(128)S(1)}, f32[8]{0:T(128)}, u32[]{:S(2)}) copy-start(f32[8]{0:T(128)} %param.11) | copy-start | bytes 100
  46.0 13.8 %all-to-all-start.2 = ((bf16[16,112,128]{2,1,0:T(8,128)(2,1)}), bf16[16,112,128]{2,1,0:T(8,128)(2,1)S(1)}, u32[]{:S(2)}, u32[]{:S(2)}) async-start(bf16[16,112,128]{2,1,0:T(8,128)(2,1)} %shard_map.82), calls=%async_computation.2 | async-start | bytes 917504 | tf_op jit(solution)/shard_map/all_to_all | solution.py:239
  49.6 20.2 %collective-permute-start.2 = (bf16[2,48,128]{2,1,0:T(8,128)(2,1)S(1)}, bf16[2,48,128]{2,1,0:T(8,128)(2,1)S(1)}, u32[]{:S(2)}, u32[]{:S(2)}) collective-permute-start(bf16[2,48,128]{2,1,0:T(8,128)(2,1)S(1)} %get-tuple-element.11), channel_id=1, source_target_pairs={{2,0},{4,2},{6,4},{8,6},{10,8},{12,10},{14,12},{16,14},{18,16},{20... | collective-permute-start | bytes 73736 | tf_op jit(solution)/shard_map/ppermute | solution.py:235
  50.9 18.9 %collective-permute-start.3 = (bf16[2,48,128]{2,1,0:T(8,128)(2,1)S(1)}, bf16[2,48,128]{2,1,0:T(8,128)(2,1)S(1)}, u32[]{:S(2)}, u32[]{:S(2)}) collective-permute-start(bf16[2,48,128]{2,1,0:T(8,128)(2,1)S(1)} %get-tuple-element.10), channel_id=1, source_target_pairs={{0,2},{2,4},{4,6},{6,8},{8,10},{10,12},{12,14},{14,16},{16,18},{18... | collective-permute-start | bytes 73736 | tf_op jit(solution)/shard_map/ppermute | solution.py:235
  85.0 8.0 %all-to-all-start.3 = ((bf16[4,112,128]{2,1,0:T(8,128)(2,1)}), bf16[4,112,128]{2,1,0:T(8,128)(2,1)S(1)}, u32[]{:S(2)}, u32[]{:S(2)}) async-start(bf16[4,112,128]{2,1,0:T(8,128)(2,1)} %shard_map.85), calls=%async_computation.3 | async-start | bytes 229376 | tf_op jit(solution)/shard_map/all_to_all | solution.py:239
  90.3 21.9 %copy-start.1 = (bf16[8,512,128]{2,0,1:T(8,128)(2,1)}, bf16[8,512,128]{2,0,1:T(8,128)(2,1)S(1)}, u32[]{:S(2)}) copy-start(bf16[8,512,128]{2,0,1:T(8,128)(2,1)S(1)} %copy.18) | copy-start | bytes 3145732

commit v8 on v6

--- a/solution.py
+++ b/solution.py
@@ -215,7 +215,7 @@
 anywhere = pl.BlockSpec(memory_space=pl.ANY)
 
 
-def call(kernel, out_shape, in_specs, scratch=(), limit=32, cost=(0, 0)):
+def call(kernel, out_shape, in_specs, scratch=(), limit=14, cost=(0, 0)):
     many = isinstance(out_shape, (list, tuple))
     return pl.pallas_call(
         kernel,

time: 114 us -> 114 us (level)
  no operation moved by 1% of the time
where the time goes in v8:
time: 114 us; the launch traced here: 113 us
  blocking collectives  75.4 us (66%)
  starting transfers between devices  19.2 us (17%)
  Pallas kernels  7.81 us (7%)
  waiting for transfers between devices  6.95 us (6%)
  local copies, waits for them, and re-layouts  2.39 us (2%)
  between operations  1.57 us (1%)
    all_to_all x3, blocking collectives, exchange(): lax.all_to_all(block, axis, 0, 0, axis_index_groups=groups, tiled=True)  36.2 us
    all_gather x2, blocking collectives, paired(): lax.all_gather(part[0], 'band', axis=0, axis_index_groups=pairs(distance))  24.2 us
    ppermute x2, starting transfers between devices, neighbours(): lax.ppermute(high_edge, 'band', forward)  9.69 us
    all_gather x1, blocking collectives, local(): lax.all_gather(part, 'rep', axis=0)  7.64 us
    all_gather x1, blocking collectives, local(): lax.all_gather(sent, 'rep', axis=0)  7.32 us
    all_to_all x2, waiting for transfers between devices, exchange(): lax.all_to_all(block, axis, 0, 0, axis_index_groups=groups, tiled=True)  6.94 us
    all_to_all x2, starting transfers between devices, exchange(): lax.all_to_all(block, axis, 0, 0, axis_index_groups=groups, tiled=True)  6.88 us
    ppermute x2, starting transfers between devices, neighbours(): lax.ppermute(low_edge, 'band', backward)  2.58 us
  transfers between devices with their start and end apart: 6, of which 2 were waited for; matrix products, arithmetic and copies ran while one was open for 1% of the time, Pallas kernels for 2%

profile of v8, /device:TPU:1, one launch (start us, length us, event | category | flops | bytes accessed | tf_op | source)
XLA Modules:
  0.0 113.3 jit_solution(891797882255068484)
XLA Ops:
  0.7 1.5 %copy.19 = bf16[1,1,512,8,128]{4,2,3,1,0:T(8,128)(2,1)S(1)} copy(bf16[1,1,512,8,128]{4,3,2,1,0:T(8,128)(2,1)} %param.6) | data formatting | bytes 2097152 | tf_op args[0]
  2.1 1.3 %collective-permute-start = (bf16[512,128]{1,0:T(8,128)(2,1)S(1)}, bf16[512,128]{1,0:T(8,128)(2,1)S(1)}, u32[]{:S(2)}, u32[]{:S(2)}) collective-permute-start(bf16[512,128]{1,0:T(8,128)(2,1)S(1)} %get-tuple-element.7), channel_id=1, source_target_pairs={{2,0},{4,2},{6,4},{8,6},{10,8},{12,10},{14,12},{16,14},{18,16},{20... | collective-permute-start | bytes 393224 | tf_op jit(solution)/shard_map/ppermute | solution.py:235
  3.4 5.0 %collective-permute-start.1 = (bf16[512,128]{1,0:T(8,128)(2,1)S(1)}, bf16[512,128]{1,0:T(8,128)(2,1)S(1)}, u32[]{:S(2)}, u32[]{:S(2)}) collective-permute-start(bf16[512,128]{1,0:T(8,128)(2,1)S(1)} %get-tuple-element.6), channel_id=1, source_target_pairs={{0,2},{2,4},{4,6},{6,8},{8,10},{10,12},{12,14},{14,16},{16,18},{18... | collective-permute-start | bytes 393224 | tf_op jit(solution)/shard_map/ppermute | solution.py:235
  9.4 1.2 %shard_map.77.inner_ref = f32[16,48,128]{2,1,0:T(8,128)S(1)} custom-call(bf16[8,512,128]{2,1,0:T(8,128)(2,1)S(1)} %bitcast.36, bf16[864,512]{1,0:T(8,128)(2,1)S(1)} %bitcast.43, f32[96,128]{1,0:T(8,128)S(1)} %broadcast_in_dim.12.offset_ref, f32[48,128]{1,0:T(8,128)S(1)} %bitcast_convert_fusion.truth_ref), custom_call_target="tpu_custom_call" | custom-call | flops 849346560 | bytes 2097152 | tf_op jit(solution)/shard_map/pallas_call | solution.py:291
  11.1 14.8 %all_to_all.25.values_ref = f32[16,48,128]{2,1,0:T(8,128)S(1)} all-to-all(f32[16,48,128]{2,1,0:T(8,128)S(1)} %shard_map.78), channel_id=1, replica_groups=mesh['member'=16,'band'=16,'rep'=2] {'member'}, dimensions={0} | all-to-all | bytes 786432 | tf_op jit(solution)/shard_map/all_to_all | solution.py:239
  25.9 0.8 shard_map.79
  26.7 9.9 %all_to_all.26.delta_ref = bf16[16,48,128]{2,1,0:T(8,128)(2,1)S(1)} all-to-all(bf16[16,48,128]{2,1,0:T(8,128)(2,1)S(1)} %shard_map.79), channel_id=1, replica_groups=mesh['member'=16,'band'=16,'rep'=2] {'member'}, dimensions={0} | all-to-all | bytes 393216 | tf_op jit(solution)/shard_map/all_to_all | solution.py:239
  36.6 0.7 shard_map.80
  37.3 7.3 %all-gather = bf16[32,112,128]{2,1,0:T(8,128)(2,1)S(1)} all-gather(bf16[16,112,128]{2,1,0:T(8,128)(2,1)S(1)} %get-tuple-element.5), channel_id=2, replica_groups=mesh['member'=16,'band'=16,'rep'=2] {'rep'}, dimensions={0}, use_global_device_ids=true | all-gather | bytes 1376256 | tf_op jit(solution)/shard_map/all_gather | solution.py:330
  44.6 1.4 %shard_map.82 = bf16[16,112,128]{2,1,0:T(8,128)(2,1)} custom-call(bf16[288,1024]{1,0:T(8,128)(2,1)S(1)} %get-tuple-element.4.spread_ref, bf16[8,512,128]{2,1,0:T(8,128)(2,1)S(1)} %bitcast.38, bf16[512,128]{1,0:T(8,128)(2,1)S(1)} %collective-permute-done.high_ref, bf16[512,128]{1,0:T(8,128)(2,1)S(1)} %collective-permute-done.1.low_ref, ...), custom_call_target="tpu_custom_call" | custom-call | flops 424673280 | bytes 1048576 | tf_op jit(solution)/shard_map/pallas_call | solution.py:325
  46.0 3.6 %all-to-all-start.2 = ((bf16[16,112,128]{2,1,0:T(8,128)(2,1)}), bf16[16,112,128]{2,1,0:T(8,128)(2,1)S(1)}, u32[]{:S(2)}, u32[]{:S(2)}) async-start(bf16[16,112,128]{2,1,0:T(8,128)(2,1)} %shard_map.82), calls=%async_computation.2 | async-start | bytes 917504 | tf_op jit(solution)/shard_map/all_to_all | solution.py:239
  49.6 1.3 %collective-permute-start.2 = (bf16[2,48,128]{2,1,0:T(8,128)(2,1)S(1)}, bf16[2,48,128]{2,1,0:T(8,128)(2,1)S(1)}, u32[]{:S(2)}, u32[]{:S(2)}) collective-permute-start(bf16[2,48,128]{2,1,0:T(8,128)(2,1)S(1)} %get-tuple-element.11), channel_id=1, source_target_pairs={{2,0},{4,2},{6,4},{8,6},{10,8},{12,10},{14,12},{16,14},{18,16},{20... | collective-permute-start | bytes 73736 | tf_op jit(solution)/shard_map/ppermute | solution.py:235
  50.9 4.7 %collective-permute-start.3 = (bf16[2,48,128]{2,1,0:T(8,128)(2,1)S(1)}, bf16[2,48,128]{2,1,0:T(8,128)(2,1)S(1)}, u32[]{:S(2)}, u32[]{:S(2)}) collective-permute-start(bf16[2,48,128]{2,1,0:T(8,128)(2,1)S(1)} %get-tuple-element.10), channel_id=1, source_target_pairs={{0,2},{2,4},{4,6},{6,8},{8,10},{10,12},{12,14},{14,16},{16,18},{18... | collective-permute-start | bytes 73736 | tf_op jit(solution)/shard_map/ppermute | solution.py:235
  55.6 4.2 %all-to-all-done.2.parts_ref = bf16[16,112,128]{2,1,0:T(8,128)(2,1)S(1)} async-done(((bf16[16,112,128]{2,1,0:T(8,128)(2,1)}), bf16[16,112,128]{2,1,0:T(8,128)(2,1)S(1)}, u32[]{:S(2)}, u32[]{:S(2)}) %all-to-all-start.2) | async-done | bytes 458784 | tf_op jit(solution)/shard_map/all_to_all | solution.py:239
  59.9 16.7 %all_gather.20.parts_ref = bf16[2,112,128]{2,1,0:T(8,128)(2,1)S(1)} all-gather(bf16[1,112,128]{2,1,0:T(8,128)(2,1)S(1)} %shard_map.83), channel_id=1, replica_groups={{0,16},{2,18},{4,20},{6,22},{8,24},{10,26},{12,28},{14,30},{1,17},{3,19..., dimensions={0}, use_global_device_ids=true | all-gather | bytes 86016 | tf_op jit(solution)/shard_map/all_gather | solution.py:352
  76.7 7.5 %all_gather.21.parts_ref = bf16[2,112,128]{2,1,0:T(8,128)(2,1)S(1)} all-gather(bf16[1,112,128]{2,1,0:T(8,128)(2,1)S(1)} %shard_map.84), channel_id=1, replica_groups={{0,8},{2,10},{4,12},{6,14},{16,24},{18,26},{20,28},{22,30},{1,9},{3,11}..., dimensions={0}, use_global_device_ids=true | all-gather | bytes 86016 | tf_op jit(solution)/shard_map/all_gather | solution.py:352
  84.2 0.7 shard_map.85
  84.8 3.3 %all-to-all-start.3 = ((bf16[4,112,128]{2,1,0:T(8,128)(2,1)}), bf16[4,112,128]{2,1,0:T(8,128)(2,1)S(1)}, u32[]{:S(2)}, u32[]{:S(2)}) async-start(bf16[4,112,128]{2,1,0:T(8,128)(2,1)} %shard_map.85), calls=%async_computation.3 | async-start | bytes 229376 | tf_op jit(solution)/shard_map/all_to_all | solution.py:239
  88.2 1.3 %shard_map.81 = bf16[8,512,128]{2,1,0:T(8,128)(2,1)S(1)} custom-call(bf16[864,512]{1,0:T(8,128)(2,1)S(1)} %bitcast.45, bf16[288,1024]{1,0:T(8,128)(2,1)S(1)} %get-tuple-element.4.spread_ref, bf16[2,48,128]{2,1,0:T(8,128)(2,1)S(1)} %collective-permute-done.2.high_ref.refs_0_, bf16[2,48,128]{2,1,0:T(8,128)(2,1)S(1)} %collective-permute-done.3.low_ref.refs_1_), custom_call_target="tpu_custom_call" | custom-call | flops 849346560 | bytes 2097152 | tf_op jit(solution)/shard_map/pallas_call | solution.py:331
  89.5 0.7 copy.18
  90.2 2.7 %all-to-all-done.3.parts_ref = bf16[4,112,128]{2,1,0:T(8,128)(2,1)S(1)} async-done(((bf16[4,112,128]{2,1,0:T(8,128)(2,1)}), bf16[4,112,128]{2,1,0:T(8,128)(2,1)S(1)}, u32[]{:S(2)}, u32[]{:S(2)}) %all-to-all-start.3) | async-done | bytes 114720 | tf_op jit(solution)/shard_map/all_to_all | solution.py:239
  92.9 11.5 %all_to_all.27 = bf16[16,112,128]{2,1,0:T(8,128)(2,1)S(1)} all-to-all(bf16[16,112,128]{2,1,0:T(8,128)(2,1)S(1)} %shard_map.86), channel_id=1, replica_groups=mesh['member'=16,'band'=16,'rep'=2] {'member'}, dimensions={0} | all-to-all | bytes 917504 | tf_op jit(solution)/shard_map/all_to_all | solution.py:239
  104.4 7.6 %all-gather.1 = bf16[32,112,128]{2,1,0:T(8,128)(2,1)S(1)} all-gather(bf16[16,112,128]{2,1,0:T(8,128)(2,1)S(1)} %all_to_all.27), channel_id=3, replica_groups=mesh['member'=16,'band'=16,'rep'=2] {'rep'}, dimensions={0}, use_global_device_ids=true | all-gather | bytes 1376256 | tf_op jit(solution)/shard_map/all_gather | solution.py:360
  112.0 1.3 %shard_map.87 = f32[9,90,512]{2,1,0:T(8,128)} custom-call(bf16[2,16,112,128]{3,2,1,0:T(8,128)(2,1)S(1)} %bitcast.42), custom_call_target="tpu_custom_call" | custom-call | flops 458752 | bytes 2752512 | tf_op jit(solution)/shard_map/pallas_call | solution.py:253
  (26 shorter events, 0.8 us)
Async XLA Ops:
  0.6 8.6 %copy-start = (f32[32,90]{1,0:T(8,128)S(1)}, f32[32,90]{1,0:T(8,128)}, u32[]{:S(2)}) copy-start(f32[32,90]{1,0:T(8,128)} %param.9) | copy-start | bytes 34564
  0.6 7.8 %copy-start.4 = (bf16[1,90,8,128]{3,2,1,0:T(8,128)(2,1)S(1)}, bf16[1,90,8,128]{3,2,1,0:T(8,128)(2,1)}, u32[]{:S(2)}) copy-start(bf16[1,90,8,128]{3,2,1,0:T(8,128)(2,1)} %param.10) | copy-start | bytes 552964
  0.7 8.6 %copy-start.3 = (bf16[3,3,512,90]{2,3,1,0:T(8,128)(2,1)S(1)}, bf16[3,3,512,90]{2,3,1,0:T(8,128)(2,1)}, u32[]{:S(2)}) copy-start(bf16[3,3,512,90]{2,3,1,0:T(8,128)(2,1)} %param.7) | copy-start | bytes 2488324
  2.1 8.5 %collective-permute-start = (bf16[512,128]{1,0:T(8,128)(2,1)S(1)}, bf16[512,128]{1,0:T(8,128)(2,1)S(1)}, u32[]{:S(2)}, u32[]{:S(2)}) collective-permute-start(bf16[512,128]{1,0:T(8,128)(2,1)S(1)} %get-tuple-element.7), channel_id=1, source_target_pairs={{2,0},{4,2},{6,4},{8,6},{10,8},{12,10},{14,12},{16,14},{18,16},{20... | collective-permute-start | bytes 393224 | tf_op jit(solution)/shard_map/ppermute | solution.py:235
  3.4 7.2 %collective-permute-start.1 = (bf16[512,128]{1,0:T(8,128)(2,1)S(1)}, bf16[512,128]{1,0:T(8,128)(2,1)S(1)}, u32[]{:S(2)}, u32[]{:S(2)}) collective-permute-start(bf16[512,128]{1,0:T(8,128)(2,1)S(1)} %get-tuple-element.6), channel_id=1, source_target_pairs={{0,2},{2,4},{4,6},{6,8},{8,10},{10,12},{12,14},{14,16},{16,18},{18... | collective-permute-start | bytes 393224 | tf_op jit(solution)/shard_map/ppermute | solution.py:235
  10.6 15.2 %copy-start.2 = (f32[8]{0:T(128)S(1)}, f32[8]{0:T(128)}, u32[]{:S(2)}) copy-start(f32[8]{0:T(128)} %param.11) | copy-start | bytes 100
  46.0 13.8 %all-to-all-start.2 = ((bf16[16,112,128]{2,1,0:T(8,128)(2,1)}), bf16[16,112,128]{2,1,0:T(8,128)(2,1)S(1)}, u32[]{:S(2)}, u32[]{:S(2)}) async-start(bf16[16,112,128]{2,1,0:T(8,128)(2,1)} %shard_map.82), calls=%async_computation.2 | async-start | bytes 917504 | tf_op jit(solution)/shard_map/all_to_all | solution.py:239
  49.6 27.0 %collective-permute-start.2 = (bf16[2,48,128]{2,1,0:T(8,128)(2,1)S(1)}, bf16[2,48,128]{2,1,0:T(8,128)(2,1)S(1)}, u32[]{:S(2)}, u32[]{:S(2)}) collective-permute-start(bf16[2,48,128]{2,1,0:T(8,128)(2,1)S(1)} %get-tuple-element.11), channel_id=1, source_target_pairs={{2,0},{4,2},{6,4},{8,6},{10,8},{12,10},{14,12},{16,14},{18,16},{20... | collective-permute-start | bytes 73736 | tf_op jit(solution)/shard_map/ppermute | solution.py:235
  50.9 25.7 %collective-permute-start.3 = (bf16[2,48,128]{2,1,0:T(8,128)(2,1)S(1)}, bf16[2,48,128]{2,1,0:T(8,128)(2,1)S(1)}, u32[]{:S(2)}, u32[]{:S(2)}) collective-permute-start(bf16[2,48,128]{2,1,0:T(8,128)(2,1)S(1)} %get-tuple-element.10), channel_id=1, source_target_pairs={{0,2},{2,4},{4,6},{6,8},{8,10},{10,12},{12,14},{14,16},{16,18},{18... | collective-permute-start | bytes 73736 | tf_op jit(solution)/shard_map/ppermute | solution.py:235
  84.8 8.0 %all-to-all-start.3 = ((bf16[4,112,128]{2,1,0:T(8,128)(2,1)}), bf16[4,112,128]{2,1,0:T(8,128)(2,1)S(1)}, u32[]{:S(2)}, u32[]{:S(2)}) async-start(bf16[4,112,128]{2,1,0:T(8,128)(2,1)} %shard_map.85), calls=%async_computation.3 | async-start | bytes 229376 | tf_op jit(solution)/shard_map/all_to_all | solution.py:239
  90.1 21.9 %copy-start.1 = (bf16[8,512,128]{2,0,1:T(8,128)(2,1)}, bf16[8,512,128]{2,0,1:T(8,128)(2,1)S(1)}, u32[]{:S(2)}) copy-start(bf16[8,512,128]{2,0,1:T(8,128)(2,1)S(1)} %copy.18) | copy-start | bytes 3145732
